TPU v7x, 32 devices: a whole 2x2x4 slice. The times are simulated.
32 devices in a mesh: shard: 16 (over z, y, x), rep: 2 (over core).
Axes of the slice: x: 2, y: 2, z: 4, core: 2. Of those that a mesh axis runs over, the one named last changes fastest.
Arguments:
- queries: bfloat16 [128, 32, 128], P(('rep', 'shard')), parts along dimension 0, may hold values from -0.5 to 0.5
- centroids: bfloat16 [32768, 128], P('shard'), may hold values from -0.5 to 0.5
- codes: int32 [512, 128], P('shard'), may hold values from 0 to 2047
- residual_codes: int32 [512, 128, 128], P('shard'), may hold values from 0 to 3
- lengths: int32 [512], P('shard'), may hold values from 1 to 128
- bucket_weights: float32 [4], replicated, may hold values from -0.12 to 0.12
- candidates: int32 [128, 32], P(('rep', 'shard')), parts along dimension 0, may hold values from 0 to 511, as said below
Outputs:
- exact_scores: float32 [128, 32], P(('rep', 'shard')), parts along dimension 0
- approx_scores: float32 [128, 32], P(('rep', 'shard')), parts along dimension 0
There are 2 independent parts, one for each index of `rep`. A program takes and returns all parts, laid end to end along the dimension named above; an argument that names none is the same for every part. Nothing has to cross between parts.
Inputs may be any that keep to these rules, and one draw needn't show every extreme that they name: `candidates`: of the 128 candidate slots of one shard's queries, at most 16 name passages of any one index shard, and some index shard is named by exactly 16 of them.
All inputs are finite; a program needn't handle non-finite values.
Results may differ from a plain program's by a relative error of at most 0.0003.
Values may be sent and summed in bfloat16 or wider, within the bound.
No kernel may reach another device: no remote copies, remote signals or barrier semaphores. Data moves between devices by JAX's collectives and lax.ppermute only.
A program may use at most 128 MiB of HBM per device.

v0:
```python
import jax
import jax.numpy as jnp
from jax import lax
from jax.sharding import PartitionSpec as P


def decompress(centroid_rows, residual_codes, bucket_weights):
    levels = jnp.zeros(residual_codes.shape, jnp.float32)
    for bucket_index in range(4):
        levels = levels + jnp.where(
            residual_codes == bucket_index, bucket_weights[bucket_index], 0.0
        )
    values = centroid_rows.astype(jnp.float32) + levels
    return (values * lax.rsqrt(jnp.sum(values * values, axis=-1, keepdims=True) + 1e-06)).astype(
        jnp.bfloat16
    )


def max_sum(dots, live_tokens):
    masked = jnp.where(live_tokens[..., None, :], dots, -jnp.inf)
    return jnp.sum(jnp.max(masked, axis=-1), axis=-1)


def per_device(queries, centroids, codes, residual_codes, lengths, bucket_weights, candidates):
    shards = lax.axis_size("shard")
    q_local, top_k = candidates.shape
    passages_dev = codes.shape[0]
    token_slots = codes.shape[1]
    slot_count = q_local * top_k
    capacity = max(2, 2 * slot_count // shards)
    flat_cand = candidates.reshape(slot_count)
    target = flat_cand // passages_dev
    local_id = flat_cand % passages_dev
    onehot = (target[:, None] == jnp.arange(shards)[None, :]).astype(jnp.int32)
    position = jnp.sum((jnp.cumsum(onehot, axis=0) - 1) * onehot, axis=1)
    bucket = target * capacity + position
    query_of = jnp.arange(slot_count) // top_k
    send_ids = jnp.full((shards * capacity,), -1, jnp.int32).at[bucket].set(local_id)
    send_ids = send_ids.reshape(shards, capacity)
    send_rows = jnp.zeros((shards * capacity,) + queries.shape[1:], jnp.bfloat16)
    send_rows = (
        send_rows.at[bucket].set(queries[query_of]).reshape((shards, capacity) + queries.shape[1:])
    )
    passage_ids = lax.all_to_all(send_ids, "shard", split_axis=0, concat_axis=0, tiled=True)
    query_rows = lax.all_to_all(send_rows, "shard", split_axis=0, concat_axis=0, tiled=True)
    safe_ids = jnp.maximum(passage_ids, 0)
    cent_rows = centroids[codes[safe_ids]]
    passage_len = lengths[safe_ids]
    live_tokens = jnp.arange(token_slots) < passage_len[..., None]
    approx = max_sum(
        jnp.einsum("nctd,ncjd->nctj", query_rows, cent_rows, preferred_element_type=jnp.float32),
        live_tokens,
    )
    passage_rows = decompress(cent_rows, residual_codes[safe_ids], bucket_weights)
    approx_back, length_back = (
        lax.all_to_all(approx, "shard", split_axis=0, concat_axis=0, tiled=True),
        lax.all_to_all(
            passage_len.astype(jnp.float32), "shard", split_axis=0, concat_axis=0, tiled=True
        ),
    )
    rows_back = lax.all_to_all(passage_rows, "shard", split_axis=0, concat_axis=0, tiled=True)
    approx_scores = approx_back.reshape(-1)[bucket].reshape(q_local, top_k)
    chosen_len = length_back.reshape(-1)[bucket].reshape(q_local, top_k)
    chosen_rows = rows_back.reshape((shards * capacity,) + rows_back.shape[2:])[bucket]
    chosen_rows = chosen_rows.reshape((q_local, top_k) + chosen_rows.shape[1:])
    live_tokens = jnp.arange(token_slots).astype(jnp.float32) < chosen_len[..., None]
    dots = jnp.einsum("qtd,qkjd->qktj", queries, chosen_rows, preferred_element_type=jnp.float32)
    exact_scores = max_sum(dots, live_tokens)
    return (exact_scores, approx_scores)


def solution(mesh):
    placed = (
        P(("rep", "shard"), None, None),
        P("shard", None),
        P("shard", None),
        P("shard", None, None),
        P("shard"),
        P(),
        P(("rep", "shard"), None),
    )
    return jax.shard_map(
        per_device,
        mesh=mesh,
        in_specs=placed,
        out_specs=(P(("rep", "shard"), None), P(("rep", "shard"), None)),
        check_vma=False,
    )
```

profile of v0, /device:TPU:14, one launch (start us, length us, event | category | flops | bytes accessed | tf_op | source)
XLA Modules:
  0.0 421.5 jit_solution(4999527769095153378)
XLA Ops:
  0.7 0.9 reshape.228
  1.6 0.8 reshape.227
  2.8 1.0 scatter_custom_fusion
  4.5 7.1 %all-to-all-start = ((s32[16,1,16]{2,1,0:T(1,128)}), s32[16,1,16]{2,1,0:T(1,128)S(1)}, u32[]{:S(2)}, u32[]{:S(2)}) async-start(s32[16,1,16]{2,1,0:T(1,128)} %all_to_all.22), calls=%async_computation | async-start | bytes 16384 | tf_op jit(solution)/shard_map/all_to_all | solution.py:44
  11.6 1.5 fusion.6
  13.1 1.5 gather_fusion.6
  14.6 1.6 broadcast_in_dim.77
  16.2 13.7 %scatter_fusion = bf16[256,32,128]{2,1,0:T(8,128)(2,1)} fusion(bf16[256,32,128]{2,1,0:T(8,128)(2,1)} %broadcast_in_dim.77, s32[128]{0:T(128)S(1)} %fusion.3, bf16[128,32,128]{2,1,0:T(8,128)(2,1)S(1)} %gather_fusion.6), kind=kCustom, calls=%fused_computation.9 | custom fusion | bytes 3146240 | tf_op jit(solution)/shard_map/scatter | solution.py:42
  29.9 6.9 %all-to-all-start.3 = ((bf16[16,16,32,128]{3,2,1,0:T(8,128)(2,1)}), bf16[16,16,32,128]{3,2,1,0:T(8,128)(2,1)}, u32[]{:S(2)}, u32[]{:S(2)}) async-start(bf16[16,16,32,128]{3,2,1,0:T(8,128)(2,1)} %bitcast.36), calls=%async_computation.3 | async-start | bytes 4194304 | tf_op jit(solution)/shard_map/all_to_all | solution.py:45
  37.0 1.9 gather_fusion
  39.7 7.3 %gather_fusion.4 = s32[256,128,128]{2,1,0:T(8,128)} fusion(s32[32,128,128]{2,1,0:T(8,128)S(1)} %copy-done, s32[1024]{0:T(1024)S(1)} %pad_clamp_fusion.2), kind=kCustom, calls=%fused_computation.4 | custom fusion | bytes 33555456 | tf_op jit(solution)/shard_map/gather | solution.py:54
  47.8 114.1 %gather_fusion.3 = bf16[32768,128]{1,0:T(8,128)(2,1)} fusion(bf16[2048,128]{1,0:T(8,128)(2,1)S(1)} %copy-done.3, s32[32768]{0:T(1024)S(1)} %broadcast_clamp_fusion), kind=kCustom, calls=%fused_computation.3 | custom fusion | bytes 16908288 | tf_op jit(solution)/shard_map/gather | solution.py:47
  161.9 12.2 %add_add_fusion = f32[256,128,128]{2,1,0:T(8,128)S(1)} fusion(s32[256,128,128]{2,1,0:T(8,128)} %gather_fusion.4, f32[]{:T(128)} %bitcast.9, f32[]{:T(128)} %bitcast.8, f32[]{:T(128)} %bitcast.7, f32[]{:T(128)} %bitcast.6), kind=kLoop, calls=%fused_computation.10 | loop fusion | flops 46137344 | bytes 33554448 | tf_op jit(solution)/shard_map/add | solution.py:10
  174.1 4.7 %multiply_reduce_fusion = f32[16,16,128]{2,1,0:T(8,128)S(1)} fusion(f32[16,16,128,128]{3,2,1,0:T(8,128)S(1)} %bitcast.35, bf16[16,16,128,128]{3,2,1,0:T(8,128)(2,1)S(1)} %bitcast.34), kind=kLoop, calls=%fused_computation.12 | loop fusion | flops 16744448 | bytes 25296896 | tf_op jit(solution)/shard_map/reduce_sum | solution.py:14
  178.8 6.9 %all-to-all-start.1 = ((f32[16,1,16]{2,1,0:T(1,128)}), f32[16,1,16]{2,1,0:T(1,128)S(1)}, u32[]{:S(2)}, u32[]{:S(2)}) async-start(f32[16,1,16]{2,1,0:T(1,128)} %bitcast.2), calls=%async_computation.1 | async-start | bytes 16384 | tf_op jit(solution)/shard_map/all_to_all | solution.py:57
  185.8 8.6 %select_reduce_fusion = f32[16,16,32]{2,1,0:T(8,128)S(1)} fusion(bf16[16,16,32,128]{3,2,1,0:T(8,128)(2,1)} %all-to-all-done.3, bf16[16,16,128,128]{3,2,1,0:T(8,128)(2,1)} %bitcast.33, pred[16,16,128]{2,1,0:T(8,128)(4,1)S(1)} %iota_compare_fusion), kind=kOutput, calls=%fused_computation.14 | convolution fusion | flops 270524416 | bytes 10551296 | tf_op jit(solution)/shard_map/nctd,ncjd->nctj/dot_general | solution.py:51
  195.0 6.9 %all-to-all-start.4 = ((f32[16,1,16]{2,1,0:T(1,128)}), f32[16,1,16]{2,1,0:T(1,128)S(1)}, u32[]{:S(2)}, u32[]{:S(2)}) async-start(f32[16,1,16]{2,1,0:T(1,128)} %bitcast.18), calls=%async_computation.4 | async-start | bytes 16384 | tf_op jit(solution)/shard_map/all_to_all | solution.py:56
  202.0 18.8 %multiply_convert_fusion = bf16[16,16,128,128]{3,2,1,0:T(8,128)(2,1)} fusion(f32[16,16,128]{2,1,0:T(8,128)S(1)} %add_rsqrt_fusion, bf16[32768,128]{1,0:T(8,128)(2,1)} %gather_fusion.3, f32[]{:T(128)} %bitcast.9, s32[256,128,128]{2,1,0:T(8,128)} %gather_fusion.4, f32[]{:T(128)} %bitcast.8, f32[]{:T(128)} %bitcast.7, f32[]{:T(128)} %bitcast.6), kind=kLoop, calls=%fused_computation.11 | loop fusion | flops 62914560 | bytes 33685520 | tf_op jit(solution)/shard_map/convert_element_type | solution.py:14
  220.8 7.1 %all-to-all-start.2 = ((bf16[16,16,128,128]{3,2,1,0:T(8,128)(2,1)}), bf16[16,16,128,128]{3,2,1,0:T(8,128)(2,1)}, u32[]{:S(2)}, u32[]{:S(2)}) async-start(bf16[16,16,128,128]{3,2,1,0:T(8,128)(2,1)} %multiply_convert_fusion), calls=%async_computation.2 | async-start | bytes 16777216 | tf_op jit(solution)/shard_map/all_to_all | solution.py:61
  229.1 1.3 gather_fusion.1
  231.3 1.3 gather_fusion.7
  233.3 177.2 %all-to-all-done.2 = bf16[16,16,128,128]{3,2,1,0:T(8,128)(2,1)} async-done(((bf16[16,16,128,128]{3,2,1,0:T(8,128)(2,1)}), bf16[16,16,128,128]{3,2,1,0:T(8,128)(2,1)}, u32[]{:S(2)}, u32[]{:S(2)}) %all-to-all-start.2) | async-done | bytes 8388640 | tf_op jit(solution)/shard_map/all_to_all | solution.py:61
  410.5 6.4 %gather_fusion.5 = bf16[128,128,128]{2,1,0:T(8,128)(2,1)} fusion(bf16[256,128,128]{2,1,0:T(8,128)(2,1)} %bitcast.11, s32[1024]{0:T(1024)S(1)} %pad_clamp_fusion.1), kind=kCustom, calls=%fused_computation.5 | custom fusion | bytes 8389120 | tf_op jit(solution)/shard_map/gather | solution.py:64
  417.0 3.8 select_reduce_fusion.1
  (48 shorter events, 7.1 us)
Async XLA Ops:
  0.6 39.0 %copy-start = (s32[32,128,128]{2,1,0:T(8,128)S(1)}, s32[32,128,128]{2,1,0:T(8,128)}, u32[]{:S(2)}) copy-start(s32[32,128,128]{2,1,0:T(8,128)} %param.10) | copy-start | bytes 6291460
  0.6 36.3 %copy-start.2 = (s32[32]{0:T(128)S(1)}, s32[32]{0:T(128)}, u32[]{:S(2)}) copy-start(s32[32]{0:T(128)} %param.11) | copy-start | bytes 388
  4.5 25.4 %all-to-all-start = ((s32[16,1,16]{2,1,0:T(1,128)}), s32[16,1,16]{2,1,0:T(1,128)S(1)}, u32[]{:S(2)}, u32[]{:S(2)}) async-start(s32[16,1,16]{2,1,0:T(1,128)} %all_to_all.22), calls=%async_computation | async-start | bytes 16384 | tf_op jit(solution)/shard_map/all_to_all | solution.py:44
  29.9 148.9 %all-to-all-start.3 = ((bf16[16,16,32,128]{3,2,1,0:T(8,128)(2,1)}), bf16[16,16,32,128]{3,2,1,0:T(8,128)(2,1)}, u32[]{:S(2)}, u32[]{:S(2)}) async-start(bf16[16,16,32,128]{3,2,1,0:T(8,128)(2,1)} %bitcast.36), calls=%async_computation.3 | async-start | bytes 4194304 | tf_op jit(solution)/shard_map/all_to_all | solution.py:45
  39.6 7.4 %copy-start.5 = (s32[32,128]{1,0:T(8,128)S(1)}, s32[32,128]{1,0:T(8,128)}, u32[]{:S(2)}) copy-start(s32[32,128]{1,0:T(8,128)} %param.9) | copy-start | bytes 49156
  39.7 8.1 %copy-start.3 = (bf16[2048,128]{1,0:T(8,128)(2,1)S(1)}, bf16[2048,128]{1,0:T(8,128)(2,1)}, u32[]{:S(2)}) copy-start(bf16[2048,128]{1,0:T(8,128)(2,1)} %param.8) | copy-start | bytes 1572868
  161.9 12.2 %copy-start.4 = (bf16[32768,128]{1,0:T(8,128)(2,1)S(1)}, bf16[32768,128]{1,0:T(8,128)(2,1)}, u32[]{:S(2)}) copy-start(bf16[32768,128]{1,0:T(8,128)(2,1)} %gather_fusion.3) | copy-start | bytes 25165828
  178.8 16.2 %all-to-all-start.1 = ((f32[16,1,16]{2,1,0:T(1,128)}), f32[16,1,16]{2,1,0:T(1,128)S(1)}, u32[]{:S(2)}, u32[]{:S(2)}) async-start(f32[16,1,16]{2,1,0:T(1,128)} %bitcast.2), calls=%async_computation.1 | async-start | bytes 16384 | tf_op jit(solution)/shard_map/all_to_all | solution.py:57
  195.0 25.7 %all-to-all-start.4 = ((f32[16,1,16]{2,1,0:T(1,128)}), f32[16,1,16]{2,1,0:T(1,128)S(1)}, u32[]{:S(2)}, u32[]{:S(2)}) async-start(f32[16,1,16]{2,1,0:T(1,128)} %bitcast.18), calls=%async_computation.4 | async-start | bytes 16384 | tf_op jit(solution)/shard_map/all_to_all | solution.py:56
  202.0 219.5 %copy-start.1 = (s32[32,128,128]{2,1,0:T(8,128)S(1)}, s32[32,128,128]{2,1,0:T(8,128)}, u32[]{:S(2)}) copy-start(s32[32,128,128]{2,1,0:T(8,128)} %param.10) | copy-start | bytes 6291460
  220.8 196.2 %copy-start.6 = (bf16[4,32,128]{2,1,0:T(8,128)(2,1)S(1)}, bf16[4,32,128]{2,1,0:T(8,128)(2,1)}, u32[]{:S(2)}) copy-start(bf16[4,32,128]{2,1,0:T(8,128)(2,1)} %param.7) | copy-start | bytes 98308
  220.8 189.7 %all-to-all-start.2 = ((bf16[16,16,128,128]{3,2,1,0:T(8,128)(2,1)}), bf16[16,16,128,128]{3,2,1,0:T(8,128)(2,1)}, u32[]{:S(2)}, u32[]{:S(2)}) async-start(bf16[16,16,128,128]{3,2,1,0:T(8,128)(2,1)} %multiply_convert_fusion), calls=%async_computation.2 | async-start | bytes 16777216 | tf_op jit(solution)/shard_map/all_to_all | solution.py:61
where the time goes:
time: 423 us; the launch traced here: 421 us
  waiting for transfers between devices  177 us (42%)
  local copies, waits for them, and re-layouts  156 us (37%)
  other arithmetic  39.7 us (9%)
  starting transfers between devices  35 us (8%)
  matrix products  12.4 us (3%)
    all_to_all x1, waiting for transfers between devices, per_device(): lax.all_to_all(passage_rows, 'shard', split_axis=0, concat_axis=0, tiled=...  177 us
    gather x2, local copies, waits for them, and re-layouts, per_device(): cent_rows = centroids[codes[safe_ids]]  115 us
    convert_element_type x1, other arithmetic, decompress(): (values * lax.rsqrt(jnp.sum(values * values, axis=-1, keepdims=True) + 1e...  18.8 us
    scatter x1, local copies, waits for them, and re-layouts, per_device(): send_rows.at[bucket].set(queries[query_of])  13.7 us
    add x1, other arithmetic, decompress(): levels + jnp.where(residual_codes == bucket_index, bucket_weights[bucket_...  12.2 us
    dot_general x1, matrix products, per_device(): jnp.einsum('nctd,ncjd->nctj', query_rows, cent_rows, preferred_element_ty...  8.57 us
  transfers between devices with their start and end apart: 5, of which 1 were waited for; matrix products, arithmetic and copies ran while one was open for 46% of the time, Pallas kernels for 0%

commit v1 on v0

v1 whole, which is shorter than its diff:
```python
import functools

import jax
import jax.numpy as jnp
from jax import lax
from jax.experimental import pallas as pl
from jax.experimental.pallas import tpu as pltpu
from jax.sharding import PartitionSpec as P

GROUP = 256
STEP = 4
CHUNK = 256
TILE = 4


def decompress_kernel(lengths, weights, codes, residuals, centroids, rows_out, table):
    step = pl.program_id(0)
    passages, slots = codes.shape
    groups = centroids.shape[0] // GROUP
    width = centroids.shape[1]

    @pl.when(step == 0)
    def _():
        for g in range(groups):
            table[:, g * width : (g + 1) * width] = centroids[g * GROUP : (g + 1) * GROUP, :]

    code_rows = codes[...].astype(jnp.float32)
    code_cols = jnp.swapaxes(code_rows, 0, 1).astype(jnp.int32)
    lane = lax.broadcasted_iota(jnp.int32, (slots, GROUP), 1)
    token = lax.broadcasted_iota(jnp.int32, (slots, width), 0)
    hot = []
    high = []
    for p in range(passages):
        code = code_cols[:, p : p + 1]
        hot.append((lane == (code % GROUP)).astype(jnp.bfloat16))
        high.append(jnp.broadcast_to(code // GROUP, (slots, width)))
    spread = jnp.dot(
        jnp.concatenate(hot, 0), table[...], preferred_element_type=jnp.float32
    )
    for p in range(passages):
        part = spread[p * slots : (p + 1) * slots]
        cent = part[:, :width]
        for g in range(1, groups):
            cent = jnp.where(high[p] == g, part[:, g * width : (g + 1) * width], cent)
        code = residuals[p]
        odd = (code & 1) == 1
        low = jnp.where(odd, weights[1], weights[0])
        top = jnp.where(odd, weights[3], weights[2])
        values = cent + jnp.where(code >= 2, top, low)
        norm = lax.rsqrt(jnp.sum(values * values, axis=-1, keepdims=True) + 1e-06)
        exact = values * norm
        live = token < lengths[step * passages + p]
        exact = jnp.where(live, exact, exact[0:1, :])
        cent = jnp.where(live, cent, cent[0:1, :])
        rows_out[p, :slots, :] = exact.astype(jnp.bfloat16)
        rows_out[p, slots:, :] = cent.astype(jnp.bfloat16)


def decompress(centroids, codes, residual_codes, lengths, bucket_weights):
    passages, slots = codes.shape
    count, width = centroids.shape
    return pl.pallas_call(
        decompress_kernel,
        grid=(passages // STEP,),
        in_specs=[
            pl.BlockSpec(memory_space=pltpu.SMEM),
            pl.BlockSpec(memory_space=pltpu.SMEM),
            pl.BlockSpec((None, STEP, slots), lambda i: (i, 0, 0)),
            pl.BlockSpec((STEP, slots, width), lambda i: (i, 0, 0)),
            pl.BlockSpec((count, width), lambda i: (0, 0)),
        ],
        out_specs=pl.BlockSpec((STEP, 2 * slots, width), lambda i: (i, 0, 0)),
        out_shape=jax.ShapeDtypeStruct((passages, 2 * slots, width), jnp.bfloat16),
        scratch_shapes=[pltpu.VMEM((GROUP, count // GROUP * width), jnp.bfloat16)],
        compiler_params=pltpu.CompilerParams(vmem_limit_bytes=32 * 2**20),
        cost_estimate=pl.CostEstimate(
            flops=2 * passages * slots * count * width,
            bytes_accessed=4 * passages * slots * width * 2,
            transcendentals=0,
        ),
    )(
        lengths,
        bucket_weights,
        codes.reshape(passages // STEP, STEP, slots),
        residual_codes,
        centroids,
    )


def score_kernel(query_tokens, query_rows, rows, out, best):
    passages, doubled, width = rows.shape
    slots = doubled // 2
    tokens = query_rows.shape[0]
    shards = out.shape[0]
    per_shard = tokens // shards

    def one_chunk(c, carry):
        query = query_rows[pl.ds(pl.multiple_of(c * CHUNK, CHUNK), CHUNK), :]
        for t in range(passages // TILE):
            dots = lax.dot_general(
                rows[t * TILE : (t + 1) * TILE].reshape(TILE * doubled, width),
                query,
                (((1,), (1,)), ((), ())),
                preferred_element_type=jnp.float32,
            )
            tops = jnp.max(dots.reshape(2 * TILE, slots, CHUNK), axis=1)
            best[c, 2 * TILE * t : 2 * TILE * (t + 1), :] = tops
        return carry

    lax.fori_loop(0, tokens // CHUNK, one_chunk, 0)
    out[...] = jnp.zeros_like(out)
    per_chunk = CHUNK // query_tokens
    shape = (per_chunk, CHUNK)
    own = lax.broadcasted_iota(jnp.int32, shape, 1) // query_tokens
    own = (own == lax.broadcasted_iota(jnp.int32, shape, 0)).astype(jnp.float32)
    q_local = per_shard // query_tokens

    def one_sum(c, carry):
        sums = lax.dot_general(
            own,
            best[c],
            (((1,), (1,)), ((), ())),
            precision=lax.Precision.HIGHEST,
            preferred_element_type=jnp.float32,
        )
        for s in range(CHUNK // per_shard):
            out[c * (CHUNK // per_shard) + s, :q_local, : 2 * passages] = sums[
                s * q_local : (s + 1) * q_local
            ]
        return carry

    lax.fori_loop(0, tokens // CHUNK, one_sum, 0)


def score(query_rows, rows, shards, query_tokens):
    passages, doubled, width = rows.shape
    tokens = query_rows.shape[0]
    return pl.pallas_call(
        functools.partial(score_kernel, query_tokens),
        out_shape=jax.ShapeDtypeStruct((shards, 8, 128), jnp.float32),
        scratch_shapes=[pltpu.VMEM((tokens // CHUNK, 2 * passages, CHUNK), jnp.float32)],
        compiler_params=pltpu.CompilerParams(vmem_limit_bytes=48 * 2**20),
        cost_estimate=pl.CostEstimate(
            flops=2 * tokens * passages * doubled * width,
            bytes_accessed=2 * (tokens + passages * doubled) * width,
            transcendentals=0,
        ),
    )(query_rows, rows)


def pick_kernel(passages, candidates, scores, exact_out, approx_out):
    q_local, top_k = candidates.shape
    shards, padded, lanes = scores.shape
    cand = jnp.concatenate([candidates[q : q + 1, :] for q in range(q_local)], axis=1)
    slot_count = q_local * top_k
    shape = (shards * padded, slot_count)
    source = lax.broadcasted_iota(jnp.int32, shape, 0)
    query = lax.broadcasted_iota(jnp.int32, shape, 1) // top_k
    wanted = (cand // passages) * padded + query
    hot = (source == wanted).astype(jnp.float32)
    spread = lax.dot_general(
        scores[...].reshape(shards * padded, lanes),
        hot,
        (((0,), (0,)), ((), ())),
        precision=lax.Precision.HIGHEST,
        preferred_element_type=jnp.float32,
    )
    row = lax.broadcasted_iota(jnp.int32, (lanes, slot_count), 0)
    first = 2 * (cand % passages)
    exact = jnp.sum(jnp.where(row == first, spread, 0.0), axis=0, keepdims=True)
    approx = jnp.sum(jnp.where(row == first + 1, spread, 0.0), axis=0, keepdims=True)
    for q in range(q_local):
        exact_out[q : q + 1, :] = exact[:, q * top_k : (q + 1) * top_k]
        approx_out[q : q + 1, :] = approx[:, q * top_k : (q + 1) * top_k]


def pick(candidates, scores, passages):
    shape = jax.ShapeDtypeStruct(candidates.shape, jnp.float32)
    return pl.pallas_call(
        functools.partial(pick_kernel, passages), out_shape=(shape, shape)
    )(candidates, scores)


def per_device(queries, centroids, codes, residual_codes, lengths, bucket_weights, candidates):
    shards = lax.axis_size("shard")
    passages = codes.shape[0]
    q_local, query_tokens, width = queries.shape
    own_rows = queries.reshape(1, q_local * query_tokens, width)
    sent = jnp.broadcast_to(own_rows, (shards,) + own_rows.shape[1:])
    query_rows = lax.all_to_all(sent, "shard", split_axis=0, concat_axis=0, tiled=True)
    rows = decompress(centroids, codes, residual_codes, lengths, bucket_weights)
    scores = score(query_rows.reshape(-1, width), rows, shards, query_tokens)
    back = lax.all_to_all(scores, "shard", split_axis=0, concat_axis=0, tiled=True)
    return pick(candidates, back, passages)


def solution(mesh):
    placed = (
        P(("rep", "shard"), None, None),
        P("shard", None),
        P("shard", None),
        P("shard", None, None),
        P("shard"),
        P(),
        P(("rep", "shard"), None),
    )
    return jax.shard_map(
        per_device,
        mesh=mesh,
        in_specs=placed,
        out_specs=(P(("rep", "shard"), None), P(("rep", "shard"), None)),
        check_vma=False,
    )
```

time: 423 us -> 50.9 us (0.12)
  the two profiles are of different devices: /device:TPU:14 before, /device:TPU:0 now
where the time goes in v1:
time: 50.9 us; the launch traced here: 50.3 us
  Pallas kernels  19.8 us (39%)
  blocking collectives  11.3 us (22%)
  starting transfers between devices  8.31 us (16%)
  local copies, waits for them, and re-layouts  6.31 us (12%)
  waiting for transfers between devices  3.95 us (8%)
  between operations  0.66 us (1%)
    pallas_call x1, Pallas kernels, score(): pl.pallas_call(functools.partial(score_kernel, query_tokens), out_shape=j...  11.5 us
    all_to_all x1, blocking collectives, per_device(): lax.all_to_all(scores, 'shard', split_axis=0, concat_axis=0, tiled=True)  11.3 us
    all_to_all x1, starting transfers between devices, per_device(): lax.all_to_all(sent, 'shard', split_axis=0, concat_axis=0, tiled=True)  8.31 us
    pallas_call x1, Pallas kernels, decompress(): pl.pallas_call(decompress_kernel, grid=(passages // STEP,), in_specs=[pl....  6.51 us
    unnamed x10, local copies, waits for them, and re-layouts  4.65 us
    all_to_all x1, waiting for transfers between devices, per_device(): lax.all_to_all(sent, 'shard', split_axis=0, concat_axis=0, tiled=True)  3.95 us
    pallas_call x1, Pallas kernels, pick(): pl.pallas_call(functools.partial(pick_kernel, passages), out_shape=(shape...  1.81 us
    broadcast_in_dim x1, local copies, waits for them, and re-layouts, per_device(): sent = jnp.broadcast_to(own_rows, (shards,) + own_rows.shape[1:])  1.65 us
  transfers between devices with their start and end apart: 1, of which 1 were waited for; matrix products, arithmetic and copies ran while one was open for 0% of the time, Pallas kernels for 13%

profile of v1, /device:TPU:0, one launch (start us, length us, event | category | flops | bytes accessed | tf_op | source)
XLA Modules:
  0.0 50.3 jit_solution(5594271936936151523)
XLA Ops:
  0.6 1.7 %broadcast_in_dim.8 = bf16[16,128,128]{2,1,0:T(8,128)(2,1)} broadcast(bf16[128,128]{1,0:T(8,128)(2,1)} %bitcast.5), dimensions={1,2} | broadcast | bytes 557056 | tf_op jit(solution)/shard_map/broadcast_in_dim | solution.py:189
  2.3 8.3 %all-to-all-start = ((bf16[16,128,128]{2,1,0:T(8,128)(2,1)}), bf16[16,128,128]{2,1,0:T(8,128)(2,1)S(1)}, u32[]{:S(2)}, u32[]{:S(2)}) async-start(bf16[16,128,128]{2,1,0:T(8,128)(2,1)} %broadcast_in_dim.8), calls=%async_computation | async-start | bytes 1048576 | tf_op jit(solution)/shard_map/all_to_all | solution.py:190
  10.6 0.0 copy-start
  10.6 1.6 %copy-done = s32[32,128,128]{2,1,0:T(8,128)S(1)} copy-done((s32[32,128,128]{2,1,0:T(8,128)S(1)}, s32[32,128,128]{2,1,0:T(8,128)}, u32[]{:S(2)}) %copy-start) | copy-done | bytes 2097176
  12.2 0.0 copy-start.1
  12.2 1.0 %copy-done.1 = bf16[2048,128]{1,0:T(8,128)(2,1)S(1)} copy-done((bf16[2048,128]{1,0:T(8,128)(2,1)S(1)}, bf16[2048,128]{1,0:T(8,128)(2,1)}, u32[]{:S(2)}) %copy-start.1) | copy-done | bytes 524312
  13.2 0.0 copy-start.2
  13.2 0.7 %copy-done.2 = s32[32,128]{1,0:T(8,128)S(1)} copy-done((s32[32,128]{1,0:T(8,128)S(1)}, s32[32,128]{1,0:T(8,128)}, u32[]{:S(2)}) %copy-start.2) | copy-done | bytes 16408
  14.0 0.0 copy-start.3
  14.0 0.7 %copy-done.3 = s32[32]{0:T(128)S(1)} copy-done((s32[32]{0:T(128)S(1)}, s32[32]{0:T(128)}, u32[]{:S(2)}) %copy-start.3) | copy-done | bytes 152
  14.6 0.0 copy-start.4
  14.6 0.7 %copy-done.4 = f32[4]{0:T(128)S(1)} copy-done((f32[4]{0:T(128)S(1)}, f32[4]{0:T(128)}, u32[]{:S(2)}) %copy-start.4) | copy-done | bytes 40
  15.3 6.5 %shard_map.86.rows = bf16[32,256,128]{2,1,0:T(8,128)(2,1)S(1)} custom-call(s32[32]{0:T(128)S(1)} %copy-done.3, f32[4]{0:T(128)S(1)} %copy-done.4, s32[8,4,128]{2,1,0:T(4,128)S(1)} %bitcast.4, s32[32,128,128]{2,1,0:T(8,128)S(1)} %copy-done, bf16[2048,128]{1,0:T(8,128)(2,1)S(1)} %copy-done.1), custom_call_target="tpu_custom_call" | custom-call | flops 2147483648 | bytes 4194304 | tf_op jit(solution)/shard_map/pallas_call | solution.py:62
  21.8 4.0 %all-to-all-done = bf16[16,128,128]{2,1,0:T(8,128)(2,1)S(1)} async-done(((bf16[16,128,128]{2,1,0:T(8,128)(2,1)}), bf16[16,128,128]{2,1,0:T(8,128)(2,1)S(1)}, u32[]{:S(2)}, u32[]{:S(2)}) %all-to-all-start) | async-done | bytes 524320 | tf_op jit(solution)/shard_map/all_to_all | solution.py:190
  25.7 11.5 %shard_map.87 = f32[16,8,128]{2,1,0:T(8,128)S(1)} custom-call(bf16[2048,128]{1,0:T(8,128)(2,1)S(1)} %bitcast.3, bf16[32,256,128]{2,1,0:T(8,128)(2,1)S(1)} %shard_map.86.rows), custom_call_target="tpu_custom_call" | custom-call | flops 4294967296 | bytes 2621440 | tf_op jit(solution)/shard_map/pallas_call | solution.py:138
  37.2 11.3 %all_to_all.10.scores = f32[16,8,128]{2,1,0:T(8,128)} all-to-all(f32[16,8,128]{2,1,0:T(8,128)S(1)} %shard_map.87), channel_id=1, replica_groups=mesh['shard'=16,'rep'=2] {'shard'}, dimensions={0} | all-to-all | bytes 131072 | tf_op jit(solution)/shard_map/all_to_all | solution.py:193
  48.5 1.8 %shard_map.88 = (f32[4,32]{1,0:T(4,128)}, f32[4,32]{1,0:T(4,128)}) custom-call(s32[4,32]{1,0:T(4,128)} %candidates.1, f32[16,8,128]{2,1,0:T(8,128)} %all_to_all.10.scores), custom_call_target="tpu_custom_call" | custom-call | tf_op jit(solution)/shard_map/pallas_call | solution.py:179
Async XLA Ops:
  2.3 23.5 %all-to-all-start = ((bf16[16,128,128]{2,1,0:T(8,128)(2,1)}), bf16[16,128,128]{2,1,0:T(8,128)(2,1)S(1)}, u32[]{:S(2)}, u32[]{:S(2)}) async-start(bf16[16,128,128]{2,1,0:T(8,128)(2,1)} %broadcast_in_dim.8), calls=%async_computation | async-start | bytes 1048576 | tf_op jit(solution)/shard_map/all_to_all | solution.py:190
  10.6 1.6 %copy-start = (s32[32,128,128]{2,1,0:T(8,128)S(1)}, s32[32,128,128]{2,1,0:T(8,128)}, u32[]{:S(2)}) copy-start(s32[32,128,128]{2,1,0:T(8,128)} %residuals.1) | copy-start | bytes 6291460
  12.2 1.0 %copy-start.1 = (bf16[2048,128]{1,0:T(8,128)(2,1)S(1)}, bf16[2048,128]{1,0:T(8,128)(2,1)}, u32[]{:S(2)}) copy-start(bf16[2048,128]{1,0:T(8,128)(2,1)} %centroids.1) | copy-start | bytes 1572868
  13.2 0.7 %copy-start.2 = (s32[32,128]{1,0:T(8,128)S(1)}, s32[32,128]{1,0:T(8,128)}, u32[]{:S(2)}) copy-start(s32[32,128]{1,0:T(8,128)} %param.9) | copy-start | bytes 49156
  14.0 0.7 %copy-start.3 = (s32[32]{0:T(128)S(1)}, s32[32]{0:T(128)}, u32[]{:S(2)}) copy-start(s32[32]{0:T(128)} %lengths.1) | copy-start | bytes 388
  14.6 0.7 %copy-start.4 = (f32[4]{0:T(128)S(1)}, f32[4]{0:T(128)}, u32[]{:S(2)}) copy-start(f32[4]{0:T(128)} %weights.1) | copy-start | bytes 52

commit v2 on v1

v2 whole, which is shorter than its diff:
```python
import functools

import jax
import jax.numpy as jnp
from jax import lax
from jax.experimental import pallas as pl
from jax.experimental.pallas import tpu as pltpu
from jax.sharding import PartitionSpec as P

GROUP = 256
STEP = 16
CHUNK = 256
TILE = 4


def decompress_kernel(
    lengths_hbm, weights_hbm, codes_hbm, residuals_hbm, centroids_hbm, rows_out,
    lengths, weights, codes, residuals, centroids, table, sems, part_sems,
):
    passages, slots = codes.shape
    count, width = centroids.shape
    groups = count // GROUP
    small = [
        pltpu.make_async_copy(source, target, sems.at[i])
        for i, (source, target) in enumerate(
            (
                (codes_hbm, codes),
                (centroids_hbm, centroids),
                (lengths_hbm, lengths),
                (weights_hbm, weights),
            )
        )
    ]
    parts = [
        pltpu.make_async_copy(
            residuals_hbm.at[pl.ds(p, STEP)], residuals.at[pl.ds(p, STEP)], part_sems.at[p // STEP]
        )
        for p in range(0, passages, STEP)
    ]
    for copy in small + parts:
        copy.start()
    for copy in small:
        copy.wait()
    for g in range(groups):
        table[:, g * width : (g + 1) * width] = centroids[g * GROUP : (g + 1) * GROUP, :]
    code_cols = jnp.swapaxes(codes[...].astype(jnp.float32), 0, 1).astype(jnp.int32)
    lane = lax.broadcasted_iota(jnp.int32, (slots, GROUP), 1)
    token = lax.broadcasted_iota(jnp.int32, (slots, width), 0)
    for first in range(0, passages, STEP):
        parts[first // STEP].wait()
        hot = []
        high = []
        for p in range(first, first + STEP):
            code = code_cols[:, p : p + 1]
            hot.append((lane == (code % GROUP)).astype(jnp.bfloat16))
            high.append(jnp.broadcast_to(code // GROUP, (slots, width)))
        spread = jnp.dot(
            jnp.concatenate(hot, 0), table[...], preferred_element_type=jnp.float32
        )
        for p in range(first, first + STEP):
            at = p - first
            part = spread[at * slots : (at + 1) * slots]
            cent = part[:, :width]
            for g in range(1, groups):
                cent = jnp.where(high[at] == g, part[:, g * width : (g + 1) * width], cent)
            code = residuals[p]
            odd = (code & 1) == 1
            low = jnp.where(odd, weights[1], weights[0])
            top = jnp.where(odd, weights[3], weights[2])
            values = cent + jnp.where(code >= 2, top, low)
            norm = lax.rsqrt(jnp.sum(values * values, axis=-1, keepdims=True) + 1e-06)
            exact = values * norm
            live = token < lengths[p]
            exact = jnp.where(live, exact, exact[0:1, :])
            cent = jnp.where(live, cent, cent[0:1, :])
            rows_out[p, :slots, :] = exact.astype(jnp.bfloat16)
            rows_out[p, slots:, :] = cent.astype(jnp.bfloat16)


def decompress(centroids, codes, residual_codes, lengths, bucket_weights):
    passages, slots = codes.shape
    count, width = centroids.shape
    operands = (lengths, bucket_weights, codes, residual_codes, centroids)
    return pl.pallas_call(
        decompress_kernel,
        in_specs=[pl.BlockSpec(memory_space=pltpu.HBM)] * len(operands),
        out_specs=pl.BlockSpec(memory_space=pltpu.VMEM),
        out_shape=jax.ShapeDtypeStruct((passages, 2 * slots, width), jnp.bfloat16),
        scratch_shapes=[
            pltpu.SMEM(lengths.shape, lengths.dtype),
            pltpu.SMEM(bucket_weights.shape, bucket_weights.dtype),
            pltpu.VMEM(codes.shape, codes.dtype),
            pltpu.VMEM(residual_codes.shape, residual_codes.dtype),
            pltpu.VMEM(centroids.shape, centroids.dtype),
            pltpu.VMEM((GROUP, count // GROUP * width), jnp.bfloat16),
            pltpu.SemaphoreType.DMA((4,)),
            pltpu.SemaphoreType.DMA((passages // STEP,)),
        ],
        compiler_params=pltpu.CompilerParams(vmem_limit_bytes=48 * 2**20),
        cost_estimate=pl.CostEstimate(
            flops=2 * passages * slots * count * width,
            bytes_accessed=4 * passages * slots * width * 2,
            transcendentals=0,
        ),
    )(*[pltpu.with_memory_space_constraint(x, pltpu.HBM) for x in operands])


def score_kernel(query_tokens, offsets, query_rows, rows, out, best):
    passages, doubled, width = rows.shape
    slots = doubled // 2
    tokens = query_rows.shape[0]
    shards = out.shape[0]
    per_shard = tokens // shards
    me = lax.axis_index("shard")

    def one_chunk(c, carry):
        query = query_rows[pl.ds(pl.multiple_of(c * CHUNK, CHUNK), CHUNK), :]
        for t in range(passages // TILE):
            dots = lax.dot_general(
                rows[t * TILE : (t + 1) * TILE].reshape(TILE * doubled, width),
                query,
                (((1,), (1,)), ((), ())),
                preferred_element_type=jnp.float32,
            )
            tops = jnp.max(dots.reshape(2 * TILE, slots, CHUNK), axis=1)
            best[c, 2 * TILE * t : 2 * TILE * (t + 1), :] = tops
        return carry

    lax.fori_loop(0, tokens // CHUNK, one_chunk, 0)
    out[...] = jnp.zeros_like(out)
    per_chunk = CHUNK // query_tokens
    shape = (per_chunk, CHUNK)
    own = lax.broadcasted_iota(jnp.int32, shape, 1) // query_tokens
    own = (own == lax.broadcasted_iota(jnp.int32, shape, 0)).astype(jnp.float32)
    q_local = per_shard // query_tokens

    for c in range(tokens // CHUNK):
        sums = lax.dot_general(
            own,
            best[c],
            (((1,), (1,)), ((), ())),
            precision=lax.Precision.HIGHEST,
            preferred_element_type=jnp.float32,
        )
        for s in range(CHUNK // per_shard):
            source = jnp.bitwise_xor(me, offsets[c * (CHUNK // per_shard) + s])
            out[source, :q_local, : 2 * passages] = sums[s * q_local : (s + 1) * q_local]


def score(query_rows, rows, offsets, query_tokens):
    passages, doubled, width = rows.shape
    tokens = query_rows.shape[0]
    return pl.pallas_call(
        functools.partial(score_kernel, query_tokens, offsets),
        out_shape=jax.ShapeDtypeStruct((len(offsets), 8, 128), jnp.float32),
        scratch_shapes=[pltpu.VMEM((tokens // CHUNK, 2 * passages, CHUNK), jnp.float32)],
        compiler_params=pltpu.CompilerParams(vmem_limit_bytes=48 * 2**20),
        cost_estimate=pl.CostEstimate(
            flops=2 * tokens * passages * doubled * width,
            bytes_accessed=2 * (tokens + passages * doubled) * width,
            transcendentals=0,
        ),
    )(query_rows, rows)


def pick_kernel(passages, candidates, scores, exact_out, approx_out):
    q_local, top_k = candidates.shape
    shards, padded, lanes = scores.shape
    cand = jnp.concatenate([candidates[q : q + 1, :] for q in range(q_local)], axis=1)
    slot_count = q_local * top_k
    shape = (shards * padded, slot_count)
    source = lax.broadcasted_iota(jnp.int32, shape, 0)
    query = lax.broadcasted_iota(jnp.int32, shape, 1) // top_k
    wanted = (cand // passages) * padded + query
    hot = (source == wanted).astype(jnp.float32)
    spread = lax.dot_general(
        scores[...].reshape(shards * padded, lanes),
        hot,
        (((0,), (0,)), ((), ())),
        precision=lax.Precision.HIGHEST,
        preferred_element_type=jnp.float32,
    )
    row = lax.broadcasted_iota(jnp.int32, (lanes, slot_count), 0)
    first = 2 * (cand % passages)
    exact = jnp.sum(jnp.where(row == first, spread, 0.0), axis=0, keepdims=True)
    approx = jnp.sum(jnp.where(row == first + 1, spread, 0.0), axis=0, keepdims=True)
    for q in range(q_local):
        exact_out[q : q + 1, :] = exact[:, q * top_k : (q + 1) * top_k]
        approx_out[q : q + 1, :] = approx[:, q * top_k : (q + 1) * top_k]


def pick(candidates, scores, passages):
    shape = jax.ShapeDtypeStruct(candidates.shape, jnp.float32)
    return pl.pallas_call(
        functools.partial(pick_kernel, passages), out_shape=(shape, shape)
    )(candidates, scores)


def exchange(block, steps, shards):
    others = [
        lax.ppermute(block, "shard", [(i, i ^ step) for i in range(shards)]) for step in steps
    ]
    return jnp.concatenate([block] + others, axis=0)


def per_device(queries, centroids, codes, residual_codes, lengths, bucket_weights, candidates):
    shards = lax.axis_size("shard")
    passages = codes.shape[0]
    q_local, query_tokens, width = queries.shape
    query_rows = queries.reshape(q_local * query_tokens, width)
    offsets = [0]
    stride = shards
    while stride > 1:
        ways = 4 if stride % 4 == 0 else 2
        stride //= ways
        steps = [stride * k for k in range(1, ways)]
        query_rows = exchange(query_rows, steps, shards)
        offsets = [k ^ at for k in [0] + steps for at in offsets]
        if stride > 1:
            query_rows, codes = lax.optimization_barrier((query_rows, codes))
    rows = decompress(centroids, codes, residual_codes, lengths, bucket_weights)
    scores = score(query_rows, rows, offsets, query_tokens)
    back = lax.all_to_all(scores, "shard", split_axis=0, concat_axis=0, tiled=True)
    return pick(candidates, back, passages)


def solution(mesh):
    placed = (
        P(("rep", "shard"), None, None),
        P("shard", None),
        P("shard", None),
        P("shard", None, None),
        P("shard"),
        P(),
        P(("rep", "shard"), None),
    )
    return jax.shard_map(
        per_device,
        mesh=mesh,
        in_specs=placed,
        out_specs=(P(("rep", "shard"), None), P(("rep", "shard"), None)),
        check_vma=False,
    )
```

time: 50.9 us -> 45.7 us (0.90)
  local copies, waits for them, and re-layouts: 6.31 us -> 0 us
  Pallas kernels: 19.8 us -> 17.4 us
  blocking collectives: 11.3 us -> 12.7 us
  starting transfers between devices: 8.31 us -> 9.31 us
  other arithmetic: 0 us -> 0.8 us
    ppermute x0 -> x6, starting transfers between devices: none -> 9.31 us  [exchange(): lax.ppermute(block, 'shard', [(i, i ^ step) for i in range(shards)])]
    all_to_all x1 -> x0, starting transfers between devices: 8.31 us -> none  [per_device(): lax.all_to_all(sent, 'shard', split_axis=0, concat_axis=0, tiled=True)]
    unnamed x10 -> x0, local copies, waits for them, and re-layouts: 4.65 us -> none
    ppermute x0 -> x6, waiting for transfers between devices: none -> 4.39 us  [exchange(): lax.ppermute(block, 'shard', [(i, i ^ step) for i in range(shards)])]
    all_to_all x1 -> x0, waiting for transfers between devices: 3.95 us -> none  [per_device(): lax.all_to_all(sent, 'shard', split_axis=0, concat_axis=0, tiled=True)]
    pallas_call x2, Pallas kernels: 18 us -> 15.6 us  [the longest x1 10.6 us: score(): pl.pallas_call(functools.partial(score_kernel, query_tokens, offsets), ou...]
    broadcast_in_dim x1 -> x0, local copies, waits for them, and re-layouts: 1.65 us -> none  [per_device(): sent = jnp.broadcast_to(own_rows, (shards,) + own_rows.shape[1:])]
    all_to_all x1, blocking collectives: 11.3 us -> 12.7 us  [per_device(): lax.all_to_all(scores, 'shard', split_axis=0, concat_axis=0, tiled=True)]
  transfers between devices with their start and end apart: 1 -> 6, of which waited for: 1 -> 2; matrix products, arithmetic and copies ran while one was open for 0% -> 0% of each run, Pallas kernels for 13% -> 11%
where the time goes in v2:
time: 45.7 us; the launch traced here: 45.4 us
  Pallas kernels  17.4 us (38%)
  blocking collectives  12.7 us (28%)
  starting transfers between devices  9.31 us (20%)
  waiting for transfers between devices  4.39 us (10%)
  other arithmetic  0.8 us (2%)
  between operations  0.68 us (1%)
    all_to_all x1, blocking collectives, per_device(): lax.all_to_all(scores, 'shard', split_axis=0, concat_axis=0, tiled=True)  12.7 us
    pallas_call x1, Pallas kernels, score(): pl.pallas_call(functools.partial(score_kernel, query_tokens, offsets), ou...  10.6 us
    ppermute x6, starting transfers between devices, exchange(): lax.ppermute(block, 'shard', [(i, i ^ step) for i in range(shards)])  9.31 us
    pallas_call x1, Pallas kernels, decompress(): pl.pallas_call(decompress_kernel, in_specs=[pl.BlockSpec(memory_space=plt...  5.01 us
    ppermute x6, waiting for transfers between devices, exchange(): lax.ppermute(block, 'shard', [(i, i ^ step) for i in range(shards)])  4.39 us
    pallas_call x1, Pallas kernels, pick(): pl.pallas_call(functools.partial(pick_kernel, passages), out_shape=(shape...  1.81 us
  transfers between devices with their start and end apart: 6, of which 2 were waited for; matrix products, arithmetic and copies ran while one was open for 0% of the time, Pallas kernels for 11%

profile of v2, /device:TPU:0, one launch (start us, length us, event | category | flops | bytes accessed | tf_op | source)
XLA Modules:
  0.0 45.4 jit_solution(1796090189110326730)
XLA Ops:
  0.6 5.1 %collective-permute-start.2 = (bf16[128,128]{1,0:T(8,128)(2,1)}, bf16[128,128]{1,0:T(8,128)(2,1)S(1)}, u32[]{:S(2)}, u32[]{:S(2)}) collective-permute-start(bf16[128,128]{1,0:T(8,128)(2,1)} %bitcast.1), channel_id=1, source_target_pairs={{0,24},{2,26},{4,28},{6,30},{8,16},{10,18},{12,20},{14,22},{16,8},... | collective-permute-start | bytes 98312 | tf_op jit(solution)/shard_map/ppermute | solution.py:201
  5.7 0.0 collective-permute-start.1
  5.7 0.6 %collective-permute-start = (bf16[128,128]{1,0:T(8,128)(2,1)}, bf16[128,128]{1,0:T(8,128)(2,1)S(1)}, u32[]{:S(2)}, u32[]{:S(2)}) collective-permute-start(bf16[128,128]{1,0:T(8,128)(2,1)} %bitcast.3), channel_id=1, source_target_pairs={{0,8},{2,10},{4,12},{6,14},{8,0},{10,2},{12,4},{14,6},{16,24},{18,... | collective-permute-start | bytes 98312 | tf_op jit(solution)/shard_map/ppermute | solution.py:201
  6.4 1.5 %collective-permute-done.2 = bf16[128,128]{1,0:T(8,128)(2,1)S(1)} collective-permute-done((bf16[128,128]{1,0:T(8,128)(2,1)}, bf16[128,128]{1,0:T(8,128)(2,1)S(1)}, u32[]{:S(2)}, u32[]{:S(2)}) %collective-permute-start.2) | collective-permute-done | bytes 32800 | tf_op jit(solution)/shard_map/ppermute | solution.py:201
  7.8 2.9 %collective-permute-done.1 = bf16[128,128]{1,0:T(8,128)(2,1)S(1)} collective-permute-done((bf16[128,128]{1,0:T(8,128)(2,1)}, bf16[128,128]{1,0:T(8,128)(2,1)S(1)}, u32[]{:S(2)}, u32[]{:S(2)}) %collective-permute-start.1) | collective-permute-done | bytes 32800 | tf_op jit(solution)/shard_map/ppermute | solution.py:201
  10.8 0.0 collective-permute-done
  10.8 0.8 %pad_maximum_fusion.1 = bf16[512,128]{1,0:T(8,128)(2,1)S(1)} fusion(bf16[128,128]{1,0:T(8,128)(2,1)S(1)} %collective-permute-done.2, bf16[128,128]{1,0:T(8,128)(2,1)S(1)} %collective-permute-done.1, bf16[128,128]{1,0:T(8,128)(2,1)S(1)} %collective-permute-done, bf16[128,128]{1,0:T(8,128)(2,1)} %bitcast.4), kind=kLoop, calls=%fused_computation.1 | loop fusion | flops 524288 | bytes 262144 | tf_op jit(solution)/shard_map/concatenate | solution.py:203
  11.5 2.5 %collective-permute-start.5 = (bf16[512,128]{1,0:T(8,128)(2,1)S(1)}, bf16[512,128]{1,0:T(8,128)(2,1)S(1)}, u32[]{:S(2)}, u32[]{:S(2)}) collective-permute-start(bf16[512,128]{1,0:T(8,128)(2,1)S(1)} %pad_maximum_fusion.1), channel_id=1, source_target_pairs={{0,6},{2,4},{4,2},{6,0},{8,14},{10,12},{12,10},{14,8},{16,22},{18,... | collective-permute-start | bytes 393224 | tf_op jit(solution)/shard_map/ppermute | solution.py:201
  14.1 0.5 %collective-permute-start.4 = (bf16[512,128]{1,0:T(8,128)(2,1)S(1)}, bf16[512,128]{1,0:T(8,128)(2,1)S(1)}, u32[]{:S(2)}, u32[]{:S(2)}) collective-permute-start(bf16[512,128]{1,0:T(8,128)(2,1)S(1)} %pad_maximum_fusion.1), channel_id=1, source_target_pairs={{0,4},{2,6},{4,0},{6,2},{8,12},{10,14},{12,8},{14,10},{16,20},{18,... | collective-permute-start | bytes 393224 | tf_op jit(solution)/shard_map/ppermute | solution.py:201
  14.6 0.5 %collective-permute-start.3 = (bf16[512,128]{1,0:T(8,128)(2,1)S(1)}, bf16[512,128]{1,0:T(8,128)(2,1)S(1)}, u32[]{:S(2)}, u32[]{:S(2)}) collective-permute-start(bf16[512,128]{1,0:T(8,128)(2,1)S(1)} %pad_maximum_fusion.1), channel_id=1, source_target_pairs={{0,2},{2,0},{4,6},{6,4},{8,10},{10,8},{12,14},{14,12},{16,18},{18,... | collective-permute-start | bytes 393224 | tf_op jit(solution)/shard_map/ppermute | solution.py:201
  15.1 5.0 %shard_map.86.rows = bf16[32,256,128]{2,1,0:T(8,128)(2,1)S(1)} custom-call(s32[32]{0:T(128)} %lengths_hbm.1, f32[4]{0:T(128)} %weights_hbm.1, s32[32,128]{1,0:T(8,128)} %codes_hbm, s32[32,128,128]{2,1,0:T(8,128)} %residuals_hbm.1, bf16[2048,128]{1,0:T(8,128)(2,1)} %centroids_hbm.1), custom_call_target="tpu_custom_call" | custom-call | flops 2147483648 | bytes 4194304 | tf_op jit(solution)/shard_map/pallas_call | solution.py:84
  20.1 0.0 collective-permute-done.5
  20.1 0.0 collective-permute-done.4
  20.1 0.0 collective-permute-done.3
  20.2 10.6 %shard_map.87 = f32[16,8,128]{2,1,0:T(8,128)S(1)} custom-call(bf16[2048,128]{1,0:T(8,128)(2,1)S(1)} %pad_maximum_fusion.query_rows, bf16[32,256,128]{2,1,0:T(8,128)(2,1)S(1)} %shard_map.86.rows), custom_call_target="tpu_custom_call" | custom-call | flops 4294967296 | bytes 2621440 | tf_op jit(solution)/shard_map/pallas_call | solution.py:153
  30.8 12.7 %all_to_all.5.scores = f32[16,8,128]{2,1,0:T(8,128)} all-to-all(f32[16,8,128]{2,1,0:T(8,128)S(1)} %shard_map.87), channel_id=1, replica_groups=mesh['shard'=16,'rep'=2] {'shard'}, dimensions={0} | all-to-all | bytes 131072 | tf_op jit(solution)/shard_map/all_to_all | solution.py:223
  43.6 1.8 %shard_map.88 = (f32[4,32]{1,0:T(4,128)}, f32[4,32]{1,0:T(4,128)}) custom-call(s32[4,32]{1,0:T(4,128)} %candidates.1, f32[16,8,128]{2,1,0:T(8,128)} %all_to_all.5.scores), custom_call_target="tpu_custom_call" | custom-call | tf_op jit(solution)/shard_map/pallas_call | solution.py:194
  (1 shorter events, 0.0 us)
Async XLA Ops:
  0.6 7.2 %collective-permute-start.2 = (bf16[128,128]{1,0:T(8,128)(2,1)}, bf16[128,128]{1,0:T(8,128)(2,1)S(1)}, u32[]{:S(2)}, u32[]{:S(2)}) collective-permute-start(bf16[128,128]{1,0:T(8,128)(2,1)} %bitcast.1), channel_id=1, source_target_pairs={{0,24},{2,26},{4,28},{6,30},{8,16},{10,18},{12,20},{14,22},{16,8},... | collective-permute-start | bytes 98312 | tf_op jit(solution)/shard_map/ppermute | solution.py:201
  5.7 5.0 %collective-permute-start.1 = (bf16[128,128]{1,0:T(8,128)(2,1)}, bf16[128,128]{1,0:T(8,128)(2,1)S(1)}, u32[]{:S(2)}, u32[]{:S(2)}) collective-permute-start(bf16[128,128]{1,0:T(8,128)(2,1)} %bitcast.2), channel_id=1, source_target_pairs={{0,16},{2,18},{4,20},{6,22},{8,24},{10,26},{12,28},{14,30},{16,0},... | collective-permute-start | bytes 98312 | tf_op jit(solution)/shard_map/ppermute | solution.py:201
  5.7 5.0 %collective-permute-start = (bf16[128,128]{1,0:T(8,128)(2,1)}, bf16[128,128]{1,0:T(8,128)(2,1)S(1)}, u32[]{:S(2)}, u32[]{:S(2)}) collective-permute-start(bf16[128,128]{1,0:T(8,128)(2,1)} %bitcast.3), channel_id=1, source_target_pairs={{0,8},{2,10},{4,12},{6,14},{8,0},{10,2},{12,4},{14,6},{16,24},{18,... | collective-permute-start | bytes 98312 | tf_op jit(solution)/shard_map/ppermute | solution.py:201
  11.5 8.6 %collective-permute-start.5 = (bf16[512,128]{1,0:T(8,128)(2,1)S(1)}, bf16[512,128]{1,0:T(8,128)(2,1)S(1)}, u32[]{:S(2)}, u32[]{:S(2)}) collective-permute-start(bf16[512,128]{1,0:T(8,128)(2,1)S(1)} %pad_maximum_fusion.1), channel_id=1, source_target_pairs={{0,6},{2,4},{4,2},{6,0},{8,14},{10,12},{12,10},{14,8},{16,22},{18,... | collective-permute-start | bytes 393224 | tf_op jit(solution)/shard_map/ppermute | solution.py:201
  14.1 6.1 %collective-permute-start.4 = (bf16[512,128]{1,0:T(8,128)(2,1)S(1)}, bf16[512,128]{1,0:T(8,128)(2,1)S(1)}, u32[]{:S(2)}, u32[]{:S(2)}) collective-permute-start(bf16[512,128]{1,0:T(8,128)(2,1)S(1)} %pad_maximum_fusion.1), channel_id=1, source_target_pairs={{0,4},{2,6},{4,0},{6,2},{8,12},{10,14},{12,8},{14,10},{16,20},{18,... | collective-permute-start | bytes 393224 | tf_op jit(solution)/shard_map/ppermute | solution.py:201
  14.6 5.6 %collective-permute-start.3 = (bf16[512,128]{1,0:T(8,128)(2,1)S(1)}, bf16[512,128]{1,0:T(8,128)(2,1)S(1)}, u32[]{:S(2)}, u32[]{:S(2)}) collective-permute-start(bf16[512,128]{1,0:T(8,128)(2,1)S(1)} %pad_maximum_fusion.1), channel_id=1, source_target_pairs={{0,2},{2,0},{4,6},{6,4},{8,10},{10,8},{12,14},{14,12},{16,18},{18,... | collective-permute-start | bytes 393224 | tf_op jit(solution)/shard_map/ppermute | solution.py:201

commit v3 on v2

--- a/solution.py
+++ b/solution.py
@@ -9,8 +9,10 @@
 
 GROUP = 256
 STEP = 16
-CHUNK = 256
-TILE = 4
+META = 16
+LANES = 128
+PACK = 8
+CUTS = (0, 32, 48)
 
 
 def decompress_kernel(
@@ -105,95 +107,225 @@
     )(*[pltpu.with_memory_space_constraint(x, pltpu.HBM) for x in operands])
 
 
-def score_kernel(query_tokens, offsets, query_rows, rows, out, best):
+def plan_kernel(shards, cap, passages, queries_hbm, candidates_hbm, block, plan, candidates, query_sem, cand_sem):
+    q_local, top_k = candidates.shape
+    tokens = queries_hbm.shape[0]
+    send_queries = pltpu.make_async_copy(queries_hbm, block.at[pl.ds(0, tokens)], query_sem)
+    get_candidates = pltpu.make_async_copy(candidates_hbm, candidates, cand_sem)
+    get_candidates.start()
+    send_queries.start()
+    get_candidates.wait()
+    slots = q_local * top_k
+    per_row = shards // META
+    cand = jnp.concatenate([candidates[q : q + 1, :] for q in range(q_local)], axis=1)
+    target = cand // passages
+    value = lax.broadcasted_iota(jnp.int32, (1, slots), 1) // top_k * passages + cand % passages + 1
+    square = (slots, slots)
+    wide = jnp.broadcast_to(target.astype(jnp.float32), square)
+    earlier = lax.broadcasted_iota(jnp.int32, square, 0) < lax.broadcasted_iota(
+        jnp.int32, square, 1
+    )
+    same = (jnp.swapaxes(wide, 0, 1) == wide) & earlier
+    rank = jnp.sum(same.astype(jnp.int32), axis=0, keepdims=True)
+    row = lax.broadcasted_iota(jnp.int32, (META, slots), 0)
+    left = jnp.where(row == target // per_row, value.astype(jnp.float32), 0.0)
+    lane = lax.broadcasted_iota(jnp.int32, (LANES, slots), 0)
+    right = (lane == target % per_row * cap + rank).astype(jnp.float32)
+    lists = lax.dot_general(
+        left.astype(jnp.bfloat16),
+        right.astype(jnp.bfloat16),
+        (((1,), (1,)), ((), ())),
+        preferred_element_type=jnp.float32,
+    )
+    block[tokens:, :] = lists.astype(jnp.bfloat16)
+    plan[0:1, :] = target
+    plan[1:2, :] = rank
+    send_queries.wait()
+
+
+def make_plan(queries, candidates, shards, cap, passages):
+    tokens, width = queries.shape
+    operands = (queries, candidates)
+    return pl.pallas_call(
+        functools.partial(plan_kernel, shards, cap, passages),
+        in_specs=[pl.BlockSpec(memory_space=pltpu.HBM)] * 2,
+        out_specs=[pl.BlockSpec(memory_space=pltpu.VMEM)] * 2,
+        out_shape=(
+            jax.ShapeDtypeStruct((tokens + META, width), jnp.bfloat16),
+            jax.ShapeDtypeStruct((8, candidates.size), jnp.int32),
+        ),
+        scratch_shapes=[
+            pltpu.VMEM(candidates.shape, candidates.dtype),
+            pltpu.SemaphoreType.DMA,
+            pltpu.SemaphoreType.DMA,
+        ],
+    )(*[pltpu.with_memory_space_constraint(x, pltpu.HBM) for x in operands])
+
+
+def exact_dot(a, b, dims):
+    return lax.dot_general(
+        a,
+        b,
+        (dims, ((), ())),
+        precision=lax.Precision.HIGHEST,
+        preferred_element_type=jnp.float32,
+    )
+
+
+def score_kernel(query_tokens, cap, offsets, blocks, rows, out, listed, steps, tops, sem):
     passages, doubled, width = rows.shape
     slots = doubled // 2
-    tokens = query_rows.shape[0]
-    shards = out.shape[0]
-    per_shard = tokens // shards
+    shards, block_rows, _ = blocks.shape
+    per_row = shards // META
     me = lax.axis_index("shard")
-
-    def one_chunk(c, carry):
-        query = query_rows[pl.ds(pl.multiple_of(c * CHUNK, CHUNK), CHUNK), :]
-        for t in range(passages // TILE):
-            dots = lax.dot_general(
-                rows[t * TILE : (t + 1) * TILE].reshape(TILE * doubled, width),
-                query,
-                (((1,), (1,)), ((), ())),
-                preferred_element_type=jnp.float32,
-            )
-            tops = jnp.max(dots.reshape(2 * TILE, slots, CHUNK), axis=1)
-            best[c, 2 * TILE * t : 2 * TILE * (t + 1), :] = tops
-        return carry
-
-    lax.fori_loop(0, tokens // CHUNK, one_chunk, 0)
-    out[...] = jnp.zeros_like(out)
-    per_chunk = CHUNK // query_tokens
-    shape = (per_chunk, CHUNK)
+    pairs = shards * cap
+    max_steps = listed.shape[0]
+
+    lists = blocks[:, block_rows - META :, :].reshape(shards * META, LANES)
+    shape = (pairs, shards * META)
+    pair = lax.broadcasted_iota(jnp.int32, shape, 0)
+    wanted = pair // cap * META + me // per_row
+    pick = (lax.broadcasted_iota(jnp.int32, shape, 1) == wanted).astype(jnp.bfloat16)
+    found = jnp.dot(pick, lists, preferred_element_type=jnp.float32)
+    shape = (pairs, LANES)
+    lane = me % per_row * cap + lax.broadcasted_iota(jnp.int32, shape, 0) % cap
+    own = lax.broadcasted_iota(jnp.int32, shape, 1) == lane
+    column = jnp.sum(jnp.where(own, found, 0.0), axis=1, keepdims=True)
+    wide = jnp.broadcast_to(column, shape)
+    code_row = jnp.swapaxes(wide, 0, 1)[0:1, :].astype(jnp.int32)
+    code_col = wide.astype(jnp.int32)
+
+    def passage_of(code):
+        return jnp.where(code > 0, (code - 1) % passages, passages)
+
+    valid = code_row > 0
+    p_row = passage_of(code_row)
+    p_col = passage_of(code_col)[:, 0:1]
+    square = (pairs, pairs)
+    earlier = lax.broadcasted_iota(jnp.int32, square, 0) < lax.broadcasted_iota(
+        jnp.int32, square, 1
+    )
+    rank = jnp.sum(((p_col == p_row) & earlier).astype(jnp.int32), axis=0, keepdims=True)
+    shape = (passages, pairs)
+    p_iota = lax.broadcasted_iota(jnp.int32, shape, 0)
+    count = jnp.sum((p_iota == p_row).astype(jnp.int32), axis=1, keepdims=True)
+    need = (count + PACK - 1) // PACK
+    start = jnp.sum(jnp.where(p_iota < p_row, need, 0), axis=0, keepdims=True)
+    step_row = jnp.where(valid, start + rank // PACK, max_steps)
+    place_row = rank % PACK
+    pair_row = lax.broadcasted_iota(jnp.int32, (1, pairs), 1)
+    query_row = pair_row // cap * (block_rows // 16) + (code_row - 1) // passages * (
+        query_tokens // 16
+    )
+    shape = (max_steps, pairs)
+    in_step = lax.broadcasted_iota(jnp.int32, shape, 0) == step_row
+    at_place = lax.broadcasted_iota(jnp.int32, (LANES, pairs), 0) == place_row
+    queries = exact_dot(
+        jnp.where(in_step, query_row.astype(jnp.float32), 0.0),
+        at_place.astype(jnp.float32),
+        ((1,), (1,)),
+    )
+    first = in_step & (place_row == 0)
+    passage = jnp.sum(jnp.where(first, p_row, 0), axis=1, keepdims=True)
+    lane = lax.broadcasted_iota(jnp.int32, (max_steps, LANES), 1)
+    total = jnp.sum(need, axis=0, keepdims=True)
+    table = jnp.where(lane == PACK, passage, queries.astype(jnp.int32))
+    listed[...] = jnp.where(lane == PACK + 1, total, table)
+    copy = pltpu.make_async_copy(listed, steps, sem)
+    copy.start()
+    tops[...] = jnp.zeros_like(tops)
+    copy.wait()
+
+    flat = blocks.reshape(shards * block_rows, width)
+
+    def one_step(step):
+        packed = [
+            flat[pl.ds(pl.multiple_of(steps[step, k] * 16, 16), query_tokens), :]
+            for k in range(PACK)
+        ]
+        dots = lax.dot_general(
+            rows[steps[step, PACK]],
+            jnp.concatenate(packed, axis=0),
+            (((1,), (1,)), ((), ())),
+            preferred_element_type=jnp.float32,
+        )
+        best = jnp.max(dots.reshape(2, slots, PACK * query_tokens), axis=1)
+        tops[step : step + 1, :] = best[0:1]
+        tops[max_steps + step : max_steps + step + 1, :] = best[1:2]
+
+    taken = steps[0, PACK + 1]
+    for begin, end in zip(CUTS, CUTS[1:] + (max_steps,)):
+
+        @pl.when(taken > begin)
+        def _():
+            for step in range(begin, end):
+                one_step(step)
+
+    shape = (PACK, PACK * query_tokens)
     own = lax.broadcasted_iota(jnp.int32, shape, 1) // query_tokens
     own = (own == lax.broadcasted_iota(jnp.int32, shape, 0)).astype(jnp.float32)
-    q_local = per_shard // query_tokens
-
-    for c in range(tokens // CHUNK):
-        sums = lax.dot_general(
-            own,
-            best[c],
-            (((1,), (1,)), ((), ())),
-            precision=lax.Precision.HIGHEST,
-            preferred_element_type=jnp.float32,
-        )
-        for s in range(CHUNK // per_shard):
-            source = jnp.bitwise_xor(me, offsets[c * (CHUNK // per_shard) + s])
-            out[source, :q_local, : 2 * passages] = sums[s * q_local : (s + 1) * q_local]
-
-
-def score(query_rows, rows, offsets, query_tokens):
+    sums = exact_dot(own, tops[...], ((1,), (1,)))
+    both = jnp.concatenate([sums[:, :max_steps], sums[:, max_steps:]], axis=0)
+    spread = exact_dot(both, in_step.astype(jnp.float32), ((1,), (0,)))
+    here = lax.broadcasted_iota(jnp.int32, (PACK, pairs), 0) == place_row
+    exact = jnp.sum(jnp.where(here, spread[:PACK], 0.0), axis=0, keepdims=True)
+    approx = jnp.sum(jnp.where(here, spread[PACK:], 0.0), axis=0, keepdims=True)
+    shape = (shards, 2 * pairs)
+    pair = lax.broadcasted_iota(jnp.int32, shape, 1)
+    from_shard = pair % pairs // cap == lax.broadcasted_iota(jnp.int32, shape, 0)
+    scores = jnp.where(from_shard, jnp.concatenate([exact, approx], axis=1), 0.0)
+    shape = (LANES, 2 * pairs)
+    pair = lax.broadcasted_iota(jnp.int32, shape, 1)
+    lane = pair // pairs * (LANES // 2) + pair % cap
+    to_lane = (lax.broadcasted_iota(jnp.int32, shape, 0) == lane).astype(jnp.float32)
+    back = exact_dot(scores, to_lane, ((1,), (1,)))
+    out[...] = jnp.zeros_like(out)
+    for k, offset in enumerate(offsets):
+        out[jnp.bitwise_xor(me, offset), 0:1, :] = back[k : k + 1, :]
+
+
+def score(blocks, rows, offsets, query_tokens, cap):
     passages, doubled, width = rows.shape
-    tokens = query_rows.shape[0]
+    shards = len(offsets)
+    max_steps = -(-(shards * cap + (PACK - 1) * passages) // (8 * PACK)) * 8
     return pl.pallas_call(
-        functools.partial(score_kernel, query_tokens, offsets),
-        out_shape=jax.ShapeDtypeStruct((len(offsets), 8, 128), jnp.float32),
-        scratch_shapes=[pltpu.VMEM((tokens // CHUNK, 2 * passages, CHUNK), jnp.float32)],
+        functools.partial(score_kernel, query_tokens, cap, offsets),
+        out_shape=jax.ShapeDtypeStruct((shards, 8, LANES), jnp.float32),
+        scratch_shapes=[
+            pltpu.VMEM((max_steps, LANES), jnp.int32),
+            pltpu.SMEM((max_steps, LANES), jnp.int32),
+            pltpu.VMEM((2 * max_steps, PACK * query_tokens), jnp.float32),
+            pltpu.SemaphoreType.DMA,
+        ],
         compiler_params=pltpu.CompilerParams(vmem_limit_bytes=48 * 2**20),
         cost_estimate=pl.CostEstimate(
-            flops=2 * tokens * passages * doubled * width,
-            bytes_accessed=2 * (tokens + passages * doubled) * width,
+            flops=2 * max_steps * PACK * query_tokens * doubled * width,
+            bytes_accessed=2 * (blocks.size + rows.size),
             transcendentals=0,
         ),
-    )(query_rows, rows)
-
-
-def pick_kernel(passages, candidates, scores, exact_out, approx_out):
-    q_local, top_k = candidates.shape
+    )(blocks, rows)
+
+
+def pick_kernel(plan, scores, exact_out, approx_out):
+    q_local, top_k = exact_out.shape
     shards, padded, lanes = scores.shape
-    cand = jnp.concatenate([candidates[q : q + 1, :] for q in range(q_local)], axis=1)
-    slot_count = q_local * top_k
-    shape = (shards * padded, slot_count)
-    source = lax.broadcasted_iota(jnp.int32, shape, 0)
-    query = lax.broadcasted_iota(jnp.int32, shape, 1) // top_k
-    wanted = (cand // passages) * padded + query
-    hot = (source == wanted).astype(jnp.float32)
-    spread = lax.dot_general(
-        scores[...].reshape(shards * padded, lanes),
-        hot,
-        (((0,), (0,)), ((), ())),
-        precision=lax.Precision.HIGHEST,
-        preferred_element_type=jnp.float32,
-    )
-    row = lax.broadcasted_iota(jnp.int32, (lanes, slot_count), 0)
-    first = 2 * (cand % passages)
-    exact = jnp.sum(jnp.where(row == first, spread, 0.0), axis=0, keepdims=True)
-    approx = jnp.sum(jnp.where(row == first + 1, spread, 0.0), axis=0, keepdims=True)
+    slots = q_local * top_k
+    target = plan[0:1, :]
+    rank = plan[1:2, :]
+    source = lax.broadcasted_iota(jnp.int32, (shards * padded, slots), 0)
+    hot = (source == target * padded).astype(jnp.float32)
+    spread = exact_dot(scores[...].reshape(shards * padded, lanes), hot, ((0,), (0,)))
+    lane = lax.broadcasted_iota(jnp.int32, (lanes, slots), 0)
+    exact = jnp.sum(jnp.where(lane == rank, spread, 0.0), axis=0, keepdims=True)
+    approx = jnp.sum(jnp.where(lane == rank + lanes // 2, spread, 0.0), axis=0, keepdims=True)
     for q in range(q_local):
         exact_out[q : q + 1, :] = exact[:, q * top_k : (q + 1) * top_k]
         approx_out[q : q + 1, :] = approx[:, q * top_k : (q + 1) * top_k]
 
 
-def pick(candidates, scores, passages):
-    shape = jax.ShapeDtypeStruct(candidates.shape, jnp.float32)
-    return pl.pallas_call(
-        functools.partial(pick_kernel, passages), out_shape=(shape, shape)
-    )(candidates, scores)
+def pick(plan, scores, shape):
+    result = jax.ShapeDtypeStruct(shape, jnp.float32)
+    return pl.pallas_call(pick_kernel, out_shape=(result, result))(plan, scores)
 
 
 def exchange(block, steps, shards):
@@ -207,21 +339,25 @@
     shards = lax.axis_size("shard")
     passages = codes.shape[0]
     q_local, query_tokens, width = queries.shape
-    query_rows = queries.reshape(q_local * query_tokens, width)
+    cap = max(2, 2 * candidates.size // shards)
+    block, plan = make_plan(
+        queries.reshape(q_local * query_tokens, width), candidates, shards, cap, passages
+    )
+    block_rows = block.shape[0]
     offsets = [0]
     stride = shards
     while stride > 1:
         ways = 4 if stride % 4 == 0 else 2
         stride //= ways
         steps = [stride * k for k in range(1, ways)]
-        query_rows = exchange(query_rows, steps, shards)
+        block = exchange(block, steps, shards)
         offsets = [k ^ at for k in [0] + steps for at in offsets]
         if stride > 1:
-            query_rows, codes = lax.optimization_barrier((query_rows, codes))
+            block, codes = lax.optimization_barrier((block, codes))
     rows = decompress(centroids, codes, residual_codes, lengths, bucket_weights)
-    scores = score(query_rows, rows, offsets, query_tokens)
+    scores = score(block.reshape(shards, block_rows, width), rows, offsets, query_tokens, cap)
     back = lax.all_to_all(scores, "shard", split_axis=0, concat_axis=0, tiled=True)
-    return pick(candidates, back, passages)
+    return pick(plan, back, candidates.shape)
 
 
 def solution(mesh):

time: 45.7 us -> 41.1 us (0.90)
  Pallas kernels: 17.4 us -> 13.1 us
    pallas_call x2 -> x3, Pallas kernels: 12.4 us -> 8.13 us  [the longest x1 4.7 us: score(): pl.pallas_call(functools.partial(score_kernel, query_tokens, cap, offsets...]
  transfers between devices with their start and end apart: 6 -> 6, of which waited for: 2 -> 2; matrix products, arithmetic and copies ran while one was open for 0% -> 0% of each run, Pallas kernels for 11% -> 12%
where the time goes in v3:
time: 41.1 us
  Pallas kernels  13.1 us (32%)
  blocking collectives  12.7 us (31%)
  starting transfers between devices  9.31 us (23%)
  waiting for transfers between devices  4.44 us (11%)
  other arithmetic  0.82 us (2%)
  between operations  0.69 us (2%)
    all_to_all x1, blocking collectives, per_device(): lax.all_to_all(scores, 'shard', split_axis=0, concat_axis=0, tiled=True)  12.7 us
    ppermute x6, starting transfers between devices, exchange(): lax.ppermute(block, 'shard', [(i, i ^ step) for i in range(shards)])  9.31 us
    pallas_call x1, Pallas kernels, decompress(): pl.pallas_call(decompress_kernel, in_specs=[pl.BlockSpec(memory_space=plt...  5.01 us
    pallas_call x1, Pallas kernels, score(): pl.pallas_call(functools.partial(score_kernel, query_tokens, cap, offsets...  4.7 us
    ppermute x6, waiting for transfers between devices, exchange(): lax.ppermute(block, 'shard', [(i, i ^ step) for i in range(shards)])  4.44 us
    pallas_call x1, Pallas kernels, pick(): return pl.pallas_call(pick_kernel, out_shape=(result, result))(plan, scores)  1.77 us
    pallas_call x1, Pallas kernels, make_plan(): pl.pallas_call(functools.partial(plan_kernel, shards, cap, passages), in_...  1.66 us
  transfers between devices with their start and end apart: 6, of which 2 were waited for; matrix products, arithmetic and copies ran while one was open for 0% of the time, Pallas kernels for 12%

profile of v3, /device:TPU:0, one launch (start us, length us, event | category | flops | bytes accessed | tf_op | source)
XLA Modules:
  0.0 41.1 jit_solution(3876076782182984229)
XLA Ops:
  0.6 1.7 %shard_map.86 = (bf16[144,128]{1,0:T(8,128)(2,1)}, s32[8,128]{1,0:T(8,128)}) custom-call(bf16[128,128]{1,0:T(8,128)(2,1)} %bitcast.3, s32[4,32]{1,0:T(4,128)} %candidates_hbm.1), custom_call_target="tpu_custom_call" | custom-call | tf_op jit(solution)/shard_map/pallas_call | solution.py:149
  2.3 5.1 %collective-permute-start.2 = (bf16[144,128]{1,0:T(8,128)(2,1)}, bf16[144,128]{1,0:T(8,128)(2,1)S(1)}, u32[]{:S(2)}, u32[]{:S(2)}) collective-permute-start(bf16[144,128]{1,0:T(8,128)(2,1)} %get-tuple-element.7), channel_id=1, source_target_pairs={{0,24},{2,26},{4,28},{6,30},{8,16},{10,18},{12,20},{14,22},{16,8},... | collective-permute-start | bytes 110600 | tf_op jit(solution)/shard_map/ppermute | solution.py:333
  7.4 0.0 collective-permute-start.1
  7.4 0.6 %collective-permute-start = (bf16[144,128]{1,0:T(8,128)(2,1)}, bf16[144,128]{1,0:T(8,128)(2,1)S(1)}, u32[]{:S(2)}, u32[]{:S(2)}) collective-permute-start(bf16[144,128]{1,0:T(8,128)(2,1)} %get-tuple-element.7), channel_id=1, source_target_pairs={{0,8},{2,10},{4,12},{6,14},{8,0},{10,2},{12,4},{14,6},{16,24},{18,... | collective-permute-start | bytes 110600 | tf_op jit(solution)/shard_map/ppermute | solution.py:333
  8.1 1.5 %collective-permute-done.2 = bf16[144,128]{1,0:T(8,128)(2,1)S(1)} collective-permute-done((bf16[144,128]{1,0:T(8,128)(2,1)}, bf16[144,128]{1,0:T(8,128)(2,1)S(1)}, u32[]{:S(2)}, u32[]{:S(2)}) %collective-permute-start.2) | collective-permute-done | bytes 36896 | tf_op jit(solution)/shard_map/ppermute | solution.py:333
  9.6 2.9 %collective-permute-done.1 = bf16[144,128]{1,0:T(8,128)(2,1)S(1)} collective-permute-done((bf16[144,128]{1,0:T(8,128)(2,1)}, bf16[144,128]{1,0:T(8,128)(2,1)S(1)}, u32[]{:S(2)}, u32[]{:S(2)}) %collective-permute-start.1) | collective-permute-done | bytes 36896 | tf_op jit(solution)/shard_map/ppermute | solution.py:333
  12.5 0.0 collective-permute-done
  12.5 0.8 %pad_maximum_fusion.1 = bf16[576,128]{1,0:T(8,128)(2,1)S(1)} fusion(bf16[144,128]{1,0:T(8,128)(2,1)S(1)} %collective-permute-done.2, bf16[144,128]{1,0:T(8,128)(2,1)S(1)} %collective-permute-done.1, bf16[144,128]{1,0:T(8,128)(2,1)S(1)} %collective-permute-done, bf16[144,128]{1,0:T(8,128)(2,1)} %get-tuple-element.7), kind=kLoop, calls=%fused_computation.1 | loop fusion | flops 589824 | bytes 294912 | tf_op jit(solution)/shard_map/concatenate | solution.py:335
  13.3 2.5 %collective-permute-start.5 = (bf16[576,128]{1,0:T(8,128)(2,1)S(1)}, bf16[576,128]{1,0:T(8,128)(2,1)S(1)}, u32[]{:S(2)}, u32[]{:S(2)}) collective-permute-start(bf16[576,128]{1,0:T(8,128)(2,1)S(1)} %pad_maximum_fusion.1), channel_id=1, source_target_pairs={{0,6},{2,4},{4,2},{6,0},{8,14},{10,12},{12,10},{14,8},{16,22},{18,... | collective-permute-start | bytes 442376 | tf_op jit(solution)/shard_map/ppermute | solution.py:333
  15.8 0.5 %collective-permute-start.4 = (bf16[576,128]{1,0:T(8,128)(2,1)S(1)}, bf16[576,128]{1,0:T(8,128)(2,1)S(1)}, u32[]{:S(2)}, u32[]{:S(2)}) collective-permute-start(bf16[576,128]{1,0:T(8,128)(2,1)S(1)} %pad_maximum_fusion.1), channel_id=1, source_target_pairs={{0,4},{2,6},{4,0},{6,2},{8,12},{10,14},{12,8},{14,10},{16,20},{18,... | collective-permute-start | bytes 442376 | tf_op jit(solution)/shard_map/ppermute | solution.py:333
  16.3 0.5 %collective-permute-start.3 = (bf16[576,128]{1,0:T(8,128)(2,1)S(1)}, bf16[576,128]{1,0:T(8,128)(2,1)S(1)}, u32[]{:S(2)}, u32[]{:S(2)}) collective-permute-start(bf16[576,128]{1,0:T(8,128)(2,1)S(1)} %pad_maximum_fusion.1), channel_id=1, source_target_pairs={{0,2},{2,0},{4,6},{6,4},{8,10},{10,8},{12,14},{14,12},{16,18},{18,... | collective-permute-start | bytes 442376 | tf_op jit(solution)/shard_map/ppermute | solution.py:333
  16.8 5.0 %shard_map.87.rows = bf16[32,256,128]{2,1,0:T(8,128)(2,1)S(1)} custom-call(s32[32]{0:T(128)} %lengths_hbm.1, f32[4]{0:T(128)} %weights_hbm.1, s32[32,128]{1,0:T(8,128)} %codes_hbm, s32[32,128,128]{2,1,0:T(8,128)} %residuals_hbm.1, bf16[2048,128]{1,0:T(8,128)(2,1)} %centroids_hbm.1), custom_call_target="tpu_custom_call" | custom-call | flops 2147483648 | bytes 4194304 | tf_op jit(solution)/shard_map/pallas_call | solution.py:86
  21.8 0.0 collective-permute-done.5
  21.8 0.0 collective-permute-done.4
  21.9 0.0 collective-permute-done.3
  21.9 4.7 %shard_map.88 = f32[16,8,128]{2,1,0:T(8,128)S(1)} custom-call(bf16[16,144,128]{2,1,0:T(8,128)(2,1)S(1)} %bitcast.2, bf16[32,256,128]{2,1,0:T(8,128)(2,1)S(1)} %shard_map.87.rows), custom_call_target="tpu_custom_call" | custom-call | flops 1073741824 | bytes 2686976 | tf_op jit(solution)/shard_map/pallas_call | solution.py:291
  26.6 12.7 %all_to_all.5.scores = f32[16,8,128]{2,1,0:T(8,128)} all-to-all(f32[16,8,128]{2,1,0:T(8,128)S(1)} %shard_map.88), channel_id=1, replica_groups=mesh['shard'=16,'rep'=2] {'shard'}, dimensions={0} | all-to-all | bytes 131072 | tf_op jit(solution)/shard_map/all_to_all | solution.py:359
  39.3 1.8 %shard_map.89 = (f32[4,32]{1,0:T(4,128)}, f32[4,32]{1,0:T(4,128)}) custom-call(s32[8,128]{1,0:T(8,128)} %get-tuple-element.6.plan, f32[16,8,128]{2,1,0:T(8,128)} %all_to_all.5.scores), custom_call_target="tpu_custom_call" | custom-call | tf_op jit(solution)/shard_map/pallas_call | solution.py:328
  (1 shorter events, 0.0 us)
Async XLA Ops:
  2.3 7.3 %collective-permute-start.2 = (bf16[144,128]{1,0:T(8,128)(2,1)}, bf16[144,128]{1,0:T(8,128)(2,1)S(1)}, u32[]{:S(2)}, u32[]{:S(2)}) collective-permute-start(bf16[144,128]{1,0:T(8,128)(2,1)} %get-tuple-element.7), channel_id=1, source_target_pairs={{0,24},{2,26},{4,28},{6,30},{8,16},{10,18},{12,20},{14,22},{16,8},... | collective-permute-start | bytes 110600 | tf_op jit(solution)/shard_map/ppermute | solution.py:333
  7.4 5.1 %collective-permute-start.1 = (bf16[144,128]{1,0:T(8,128)(2,1)}, bf16[144,128]{1,0:T(8,128)(2,1)S(1)}, u32[]{:S(2)}, u32[]{:S(2)}) collective-permute-start(bf16[144,128]{1,0:T(8,128)(2,1)} %get-tuple-element.7), channel_id=1, source_target_pairs={{0,16},{2,18},{4,20},{6,22},{8,24},{10,26},{12,28},{14,30},{16,0},... | collective-permute-start | bytes 110600 | tf_op jit(solution)/shard_map/ppermute | solution.py:333
  7.4 5.1 %collective-permute-start = (bf16[144,128]{1,0:T(8,128)(2,1)}, bf16[144,128]{1,0:T(8,128)(2,1)S(1)}, u32[]{:S(2)}, u32[]{:S(2)}) collective-permute-start(bf16[144,128]{1,0:T(8,128)(2,1)} %get-tuple-element.7), channel_id=1, source_target_pairs={{0,8},{2,10},{4,12},{6,14},{8,0},{10,2},{12,4},{14,6},{16,24},{18,... | collective-permute-start | bytes 110600 | tf_op jit(solution)/shard_map/ppermute | solution.py:333
  13.3 8.6 %collective-permute-start.5 = (bf16[576,128]{1,0:T(8,128)(2,1)S(1)}, bf16[576,128]{1,0:T(8,128)(2,1)S(1)}, u32[]{:S(2)}, u32[]{:S(2)}) collective-permute-start(bf16[576,128]{1,0:T(8,128)(2,1)S(1)} %pad_maximum_fusion.1), channel_id=1, source_target_pairs={{0,6},{2,4},{4,2},{6,0},{8,14},{10,12},{12,10},{14,8},{16,22},{18,... | collective-permute-start | bytes 442376 | tf_op jit(solution)/shard_map/ppermute | solution.py:333
  15.8 6.1 %collective-permute-start.4 = (bf16[576,128]{1,0:T(8,128)(2,1)S(1)}, bf16[576,128]{1,0:T(8,128)(2,1)S(1)}, u32[]{:S(2)}, u32[]{:S(2)}) collective-permute-start(bf16[576,128]{1,0:T(8,128)(2,1)S(1)} %pad_maximum_fusion.1), channel_id=1, source_target_pairs={{0,4},{2,6},{4,0},{6,2},{8,12},{10,14},{12,8},{14,10},{16,20},{18,... | collective-permute-start | bytes 442376 | tf_op jit(solution)/shard_map/ppermute | solution.py:333
  16.3 5.6 %collective-permute-start.3 = (bf16[576,128]{1,0:T(8,128)(2,1)S(1)}, bf16[576,128]{1,0:T(8,128)(2,1)S(1)}, u32[]{:S(2)}, u32[]{:S(2)}) collective-permute-start(bf16[576,128]{1,0:T(8,128)(2,1)S(1)} %pad_maximum_fusion.1), channel_id=1, source_target_pairs={{0,2},{2,0},{4,6},{6,4},{8,10},{10,8},{12,14},{14,12},{16,18},{18,... | collective-permute-start | bytes 442376 | tf_op jit(solution)/shard_map/ppermute | solution.py:333

commit v4 on v3

--- a/solution.py
+++ b/solution.py
@@ -151,8 +151,8 @@
         in_specs=[pl.BlockSpec(memory_space=pltpu.HBM)] * 2,
         out_specs=[pl.BlockSpec(memory_space=pltpu.VMEM)] * 2,
         out_shape=(
-            jax.ShapeDtypeStruct((tokens + META, width), jnp.bfloat16),
-            jax.ShapeDtypeStruct((8, candidates.size), jnp.int32),
+            pltpu.VMEM((tokens + META, width), jnp.bfloat16),
+            pltpu.VMEM((8, candidates.size), jnp.int32),
         ),
         scratch_shapes=[
             pltpu.VMEM(candidates.shape, candidates.dtype),
@@ -325,7 +325,8 @@
 
 def pick(plan, scores, shape):
     result = jax.ShapeDtypeStruct(shape, jnp.float32)
-    return pl.pallas_call(pick_kernel, out_shape=(result, result))(plan, scores)
+    operands = [pltpu.with_memory_space_constraint(x, pltpu.VMEM) for x in (plan, scores)]
+    return pl.pallas_call(pick_kernel, out_shape=(result, result))(*operands)
 
 
 def exchange(block, steps, shards):

time: 41.1 us -> 38.9 us (0.946)
  Pallas kernels: 13.1 us -> 11 us
  other arithmetic: 0.82 us -> 0.05 us
  blocking collectives: 12.7 us -> 13.3 us
    pallas_call x1, Pallas kernels: 1.77 us -> 0.93 us  [pick(): return pl.pallas_call(pick_kernel, out_shape=(result, result))(*operands)]
    concatenate x2, other arithmetic: 0.82 us -> 0.05 us  [exchange(): return jnp.concatenate([block] + others, axis=0)]
    pallas_call x1, Pallas kernels: 4.7 us -> 3.98 us  [score(): pl.pallas_call(functools.partial(score_kernel, query_tokens, cap, offsets...]
    all_to_all x1, blocking collectives: 12.7 us -> 13.3 us  [per_device(): lax.all_to_all(scores, 'shard', split_axis=0, concat_axis=0, tiled=True)]
    pallas_call x1, Pallas kernels: 1.66 us -> 1.04 us  [make_plan(): pl.pallas_call(functools.partial(plan_kernel, shards, cap, passages), in_...]
  transfers between devices with their start and end apart: 6 -> 6, of which waited for: 2 -> 2; matrix products, arithmetic and copies ran while one was open for 0% -> 0% of each run, Pallas kernels for 12% -> 13%
where the time goes in v4:
time: 38.9 us; the launch traced here: 38.6 us
  blocking collectives  13.3 us (34%)
  Pallas kernels  11 us (28%)
  starting transfers between devices  9.31 us (24%)
  waiting for transfers between devices  4.22 us (11%)
  between operations  0.69 us (2%)
    all_to_all x1, blocking collectives, per_device(): lax.all_to_all(scores, 'shard', split_axis=0, concat_axis=0, tiled=True)  13.3 us
    ppermute x6, starting transfers between devices, exchange(): lax.ppermute(block, 'shard', [(i, i ^ step) for i in range(shards)])  9.31 us
    pallas_call x1, Pallas kernels, decompress(): pl.pallas_call(decompress_kernel, in_specs=[pl.BlockSpec(memory_space=plt...  5.01 us
    ppermute x6, waiting for transfers between devices, exchange(): lax.ppermute(block, 'shard', [(i, i ^ step) for i in range(shards)])  4.22 us
    pallas_call x1, Pallas kernels, score(): pl.pallas_call(functools.partial(score_kernel, query_tokens, cap, offsets...  3.98 us
    pallas_call x1, Pallas kernels, make_plan(): pl.pallas_call(functools.partial(plan_kernel, shards, cap, passages), in_...  1.04 us
    pallas_call x1, Pallas kernels, pick(): return pl.pallas_call(pick_kernel, out_shape=(result, result))(*operands)  0.93 us
  transfers between devices with their start and end apart: 6, of which 2 were waited for; matrix products, arithmetic and copies ran while one was open for 0% of the time, Pallas kernels for 13%

profile of v4, /device:TPU:0, one launch (start us, length us, event | category | flops | bytes accessed | tf_op | source)
XLA Modules:
  0.0 38.6 jit_solution(15522117487663175004)
XLA Ops:
  0.6 1.0 %shard_map.86 = (bf16[144,128]{1,0:T(8,128)(2,1)S(1)}, s32[8,128]{1,0:T(8,128)S(1)}) custom-call(bf16[128,128]{1,0:T(8,128)(2,1)} %bitcast.3, s32[4,32]{1,0:T(4,128)} %candidates_hbm.1), custom_call_target="tpu_custom_call" | custom-call | tf_op jit(solution)/shard_map/pallas_call | solution.py:149
  1.7 5.1 %collective-permute-start.2 = (bf16[144,128]{1,0:T(8,128)(2,1)S(1)}, bf16[144,128]{1,0:T(8,128)(2,1)S(1)}, u32[]{:S(2)}, u32[]{:S(2)}) collective-permute-start(bf16[144,128]{1,0:T(8,128)(2,1)S(1)} %get-tuple-element.7), channel_id=1, source_target_pairs={{0,24},{2,26},{4,28},{6,30},{8,16},{10,18},{12,20},{14,22},{16,8},... | collective-permute-start | bytes 110600 | tf_op jit(solution)/shard_map/ppermute | solution.py:334
  6.8 0.0 collective-permute-start.1
  6.8 0.6 %collective-permute-start = (bf16[144,128]{1,0:T(8,128)(2,1)S(1)}, bf16[144,128]{1,0:T(8,128)(2,1)S(1)}, u32[]{:S(2)}, u32[]{:S(2)}) collective-permute-start(bf16[144,128]{1,0:T(8,128)(2,1)S(1)} %get-tuple-element.7), channel_id=1, source_target_pairs={{0,8},{2,10},{4,12},{6,14},{8,0},{10,2},{12,4},{14,6},{16,24},{18,... | collective-permute-start | bytes 110600 | tf_op jit(solution)/shard_map/ppermute | solution.py:334
  7.4 1.3 %collective-permute-done.2 = bf16[144,128]{1,0:T(8,128)(2,1)S(1)} collective-permute-done((bf16[144,128]{1,0:T(8,128)(2,1)S(1)}, bf16[144,128]{1,0:T(8,128)(2,1)S(1)}, u32[]{:S(2)}, u32[]{:S(2)}) %collective-permute-start.2) | collective-permute-done | bytes 36896 | tf_op jit(solution)/shard_map/ppermute | solution.py:334
  8.7 2.9 %collective-permute-done.1 = bf16[144,128]{1,0:T(8,128)(2,1)S(1)} collective-permute-done((bf16[144,128]{1,0:T(8,128)(2,1)S(1)}, bf16[144,128]{1,0:T(8,128)(2,1)S(1)}, u32[]{:S(2)}, u32[]{:S(2)}) %collective-permute-start.1) | collective-permute-done | bytes 36896 | tf_op jit(solution)/shard_map/ppermute | solution.py:334
  11.7 0.0 collective-permute-done
  11.7 2.5 %collective-permute-start.5 = (bf16[576,128]{1,0:T(8,128)(2,1)S(1)}, bf16[576,128]{1,0:T(8,128)(2,1)S(1)}, u32[]{:S(2)}, u32[]{:S(2)}) collective-permute-start(bf16[576,128]{1,0:T(8,128)(2,1)S(1)} %pad_maximum_fusion.1), channel_id=1, source_target_pairs={{0,6},{2,4},{4,2},{6,0},{8,14},{10,12},{12,10},{14,8},{16,22},{18,... | collective-permute-start | bytes 442376 | tf_op jit(solution)/shard_map/ppermute | solution.py:334
  14.2 0.5 %collective-permute-start.4 = (bf16[576,128]{1,0:T(8,128)(2,1)S(1)}, bf16[576,128]{1,0:T(8,128)(2,1)S(1)}, u32[]{:S(2)}, u32[]{:S(2)}) collective-permute-start(bf16[576,128]{1,0:T(8,128)(2,1)S(1)} %pad_maximum_fusion.1), channel_id=1, source_target_pairs={{0,4},{2,6},{4,0},{6,2},{8,12},{10,14},{12,8},{14,10},{16,20},{18,... | collective-permute-start | bytes 442376 | tf_op jit(solution)/shard_map/ppermute | solution.py:334
  14.7 0.5 %collective-permute-start.3 = (bf16[576,128]{1,0:T(8,128)(2,1)S(1)}, bf16[576,128]{1,0:T(8,128)(2,1)S(1)}, u32[]{:S(2)}, u32[]{:S(2)}) collective-permute-start(bf16[576,128]{1,0:T(8,128)(2,1)S(1)} %pad_maximum_fusion.1), channel_id=1, source_target_pairs={{0,2},{2,0},{4,6},{6,4},{8,10},{10,8},{12,14},{14,12},{16,18},{18,... | collective-permute-start | bytes 442376 | tf_op jit(solution)/shard_map/ppermute | solution.py:334
  15.2 5.0 %shard_map.87.rows = bf16[32,256,128]{2,1,0:T(8,128)(2,1)S(1)} custom-call(s32[32]{0:T(128)} %lengths_hbm.1, f32[4]{0:T(128)} %weights_hbm.1, s32[32,128]{1,0:T(8,128)} %codes_hbm, s32[32,128,128]{2,1,0:T(8,128)} %residuals_hbm.1, bf16[2048,128]{1,0:T(8,128)(2,1)} %centroids_hbm.1), custom_call_target="tpu_custom_call" | custom-call | flops 2147483648 | bytes 4194304 | tf_op jit(solution)/shard_map/pallas_call | solution.py:86
  20.2 0.0 collective-permute-done.5
  20.2 0.0 collective-permute-done.4
  20.3 0.0 collective-permute-done.3
  20.3 4.0 %shard_map.88 = f32[16,8,128]{2,1,0:T(8,128)S(1)} custom-call(bf16[16,144,128]{2,1,0:T(8,128)(2,1)S(1)} %bitcast.2, bf16[32,256,128]{2,1,0:T(8,128)(2,1)S(1)} %shard_map.87.rows), custom_call_target="tpu_custom_call" | custom-call | flops 1073741824 | bytes 2686976 | tf_op jit(solution)/shard_map/pallas_call | solution.py:291
  24.3 13.3 %all_to_all.5.scores = f32[16,8,128]{2,1,0:T(8,128)S(1)} all-to-all(f32[16,8,128]{2,1,0:T(8,128)S(1)} %shard_map.88), channel_id=1, replica_groups=mesh['shard'=16,'rep'=2] {'shard'}, dimensions={0} | all-to-all | bytes 131072 | tf_op jit(solution)/shard_map/all_to_all | solution.py:360
  37.7 0.9 %shard_map.89 = (f32[4,32]{1,0:T(4,128)}, f32[4,32]{1,0:T(4,128)}) custom-call(s32[8,128]{1,0:T(8,128)S(1)} %get-tuple-element.6.plan, f32[16,8,128]{2,1,0:T(8,128)S(1)} %all_to_all.5.scores), custom_call_target="tpu_custom_call" | custom-call | tf_op jit(solution)/shard_map/pallas_call | solution.py:329
  (2 shorter events, 0.1 us)
Async XLA Ops:
  1.7 7.1 %collective-permute-start.2 = (bf16[144,128]{1,0:T(8,128)(2,1)S(1)}, bf16[144,128]{1,0:T(8,128)(2,1)S(1)}, u32[]{:S(2)}, u32[]{:S(2)}) collective-permute-start(bf16[144,128]{1,0:T(8,128)(2,1)S(1)} %get-tuple-element.7), channel_id=1, source_target_pairs={{0,24},{2,26},{4,28},{6,30},{8,16},{10,18},{12,20},{14,22},{16,8},... | collective-permute-start | bytes 110600 | tf_op jit(solution)/shard_map/ppermute | solution.py:334
  6.8 4.9 %collective-permute-start.1 = (bf16[144,128]{1,0:T(8,128)(2,1)S(1)}, bf16[144,128]{1,0:T(8,128)(2,1)S(1)}, u32[]{:S(2)}, u32[]{:S(2)}) collective-permute-start(bf16[144,128]{1,0:T(8,128)(2,1)S(1)} %get-tuple-element.7), channel_id=1, source_target_pairs={{0,16},{2,18},{4,20},{6,22},{8,24},{10,26},{12,28},{14,30},{16,0},... | collective-permute-start | bytes 110600 | tf_op jit(solution)/shard_map/ppermute | solution.py:334
  6.8 4.9 %collective-permute-start = (bf16[144,128]{1,0:T(8,128)(2,1)S(1)}, bf16[144,128]{1,0:T(8,128)(2,1)S(1)}, u32[]{:S(2)}, u32[]{:S(2)}) collective-permute-start(bf16[144,128]{1,0:T(8,128)(2,1)S(1)} %get-tuple-element.7), channel_id=1, source_target_pairs={{0,8},{2,10},{4,12},{6,14},{8,0},{10,2},{12,4},{14,6},{16,24},{18,... | collective-permute-start | bytes 110600 | tf_op jit(solution)/shard_map/ppermute | solution.py:334
  11.7 8.6 %collective-permute-start.5 = (bf16[576,128]{1,0:T(8,128)(2,1)S(1)}, bf16[576,128]{1,0:T(8,128)(2,1)S(1)}, u32[]{:S(2)}, u32[]{:S(2)}) collective-permute-start(bf16[576,128]{1,0:T(8,128)(2,1)S(1)} %pad_maximum_fusion.1), channel_id=1, source_target_pairs={{0,6},{2,4},{4,2},{6,0},{8,14},{10,12},{12,10},{14,8},{16,22},{18,... | collective-permute-start | bytes 442376 | tf_op jit(solution)/shard_map/ppermute | solution.py:334
  14.2 6.1 %collective-permute-start.4 = (bf16[576,128]{1,0:T(8,128)(2,1)S(1)}, bf16[576,128]{1,0:T(8,128)(2,1)S(1)}, u32[]{:S(2)}, u32[]{:S(2)}) collective-permute-start(bf16[576,128]{1,0:T(8,128)(2,1)S(1)} %pad_maximum_fusion.1), channel_id=1, source_target_pairs={{0,4},{2,6},{4,0},{6,2},{8,12},{10,14},{12,8},{14,10},{16,20},{18,... | collective-permute-start | bytes 442376 | tf_op jit(solution)/shard_map/ppermute | solution.py:334
  14.7 5.6 %collective-permute-start.3 = (bf16[576,128]{1,0:T(8,128)(2,1)S(1)}, bf16[576,128]{1,0:T(8,128)(2,1)S(1)}, u32[]{:S(2)}, u32[]{:S(2)}) collective-permute-start(bf16[576,128]{1,0:T(8,128)(2,1)S(1)} %pad_maximum_fusion.1), channel_id=1, source_target_pairs={{0,2},{2,0},{4,6},{6,4},{8,10},{10,8},{12,14},{14,12},{16,18},{18,... | collective-permute-start | bytes 442376 | tf_op jit(solution)/shard_map/ppermute | solution.py:334

commit v5 on v4

--- a/solution.py
+++ b/solution.py
@@ -15,41 +15,49 @@
 CUTS = (0, 32, 48)
 
 
+def fetch_kernel(*refs):
+    count = len(refs) // 2
+    copies = [
+        pltpu.make_async_copy(refs[i], refs[count + i], refs[-1].at[i]) for i in range(count)
+    ]
+    for copy in copies:
+        copy.start()
+    for copy in copies:
+        copy.wait()
+
+
+def fetch(*arrays):
+    return pl.pallas_call(
+        fetch_kernel,
+        in_specs=[pl.BlockSpec(memory_space=pltpu.HBM)] * len(arrays),
+        out_specs=[pl.BlockSpec(memory_space=pltpu.VMEM)] * len(arrays),
+        out_shape=[pltpu.VMEM(x.shape, x.dtype) for x in arrays],
+        scratch_shapes=[pltpu.SemaphoreType.DMA((len(arrays),))],
+        compiler_params=pltpu.CompilerParams(vmem_limit_bytes=16 * 2**20),
+        cost_estimate=pl.CostEstimate(
+            flops=0, bytes_accessed=2 * sum(x.nbytes for x in arrays), transcendentals=0
+        ),
+    )(*[pltpu.with_memory_space_constraint(x, pltpu.HBM) for x in arrays])
+
+
 def decompress_kernel(
-    lengths_hbm, weights_hbm, codes_hbm, residuals_hbm, centroids_hbm, rows_out,
-    lengths, weights, codes, residuals, centroids, table, sems, part_sems,
+    lengths_hbm, weights_hbm, codes, residuals, centroids, rows_out, lengths, weights, table, sems
 ):
     passages, slots = codes.shape
     count, width = centroids.shape
     groups = count // GROUP
     small = [
-        pltpu.make_async_copy(source, target, sems.at[i])
-        for i, (source, target) in enumerate(
-            (
-                (codes_hbm, codes),
-                (centroids_hbm, centroids),
-                (lengths_hbm, lengths),
-                (weights_hbm, weights),
-            )
-        )
+        pltpu.make_async_copy(lengths_hbm, lengths, sems.at[0]),
+        pltpu.make_async_copy(weights_hbm, weights, sems.at[1]),
     ]
-    parts = [
-        pltpu.make_async_copy(
-            residuals_hbm.at[pl.ds(p, STEP)], residuals.at[pl.ds(p, STEP)], part_sems.at[p // STEP]
-        )
-        for p in range(0, passages, STEP)
-    ]
-    for copy in small + parts:
+    for copy in small:
         copy.start()
-    for copy in small:
-        copy.wait()
     for g in range(groups):
         table[:, g * width : (g + 1) * width] = centroids[g * GROUP : (g + 1) * GROUP, :]
     code_cols = jnp.swapaxes(codes[...].astype(jnp.float32), 0, 1).astype(jnp.int32)
     lane = lax.broadcasted_iota(jnp.int32, (slots, GROUP), 1)
     token = lax.broadcasted_iota(jnp.int32, (slots, width), 0)
     for first in range(0, passages, STEP):
-        parts[first // STEP].wait()
         hot = []
         high = []
         for p in range(first, first + STEP):
@@ -59,6 +67,9 @@
         spread = jnp.dot(
             jnp.concatenate(hot, 0), table[...], preferred_element_type=jnp.float32
         )
+        if first == 0:
+            for copy in small:
+                copy.wait()
         for p in range(first, first + STEP):
             at = p - first
             part = spread[at * slots : (at + 1) * slots]
@@ -82,29 +93,30 @@
 def decompress(centroids, codes, residual_codes, lengths, bucket_weights):
     passages, slots = codes.shape
     count, width = centroids.shape
-    operands = (lengths, bucket_weights, codes, residual_codes, centroids)
+    scalars = [pltpu.with_memory_space_constraint(x, pltpu.HBM) for x in (lengths, bucket_weights)]
+    arrays = [
+        pltpu.with_memory_space_constraint(x, pltpu.VMEM)
+        for x in (codes, residual_codes, centroids)
+    ]
     return pl.pallas_call(
         decompress_kernel,
-        in_specs=[pl.BlockSpec(memory_space=pltpu.HBM)] * len(operands),
+        in_specs=[pl.BlockSpec(memory_space=pltpu.HBM)] * 2
+        + [pl.BlockSpec(memory_space=pltpu.VMEM)] * 3,
         out_specs=pl.BlockSpec(memory_space=pltpu.VMEM),
-        out_shape=jax.ShapeDtypeStruct((passages, 2 * slots, width), jnp.bfloat16),
+        out_shape=pltpu.VMEM((passages, 2 * slots, width), jnp.bfloat16),
         scratch_shapes=[
             pltpu.SMEM(lengths.shape, lengths.dtype),
             pltpu.SMEM(bucket_weights.shape, bucket_weights.dtype),
-            pltpu.VMEM(codes.shape, codes.dtype),
-            pltpu.VMEM(residual_codes.shape, residual_codes.dtype),
-            pltpu.VMEM(centroids.shape, centroids.dtype),
             pltpu.VMEM((GROUP, count // GROUP * width), jnp.bfloat16),
-            pltpu.SemaphoreType.DMA((4,)),
-            pltpu.SemaphoreType.DMA((passages // STEP,)),
+            pltpu.SemaphoreType.DMA((2,)),
         ],
-        compiler_params=pltpu.CompilerParams(vmem_limit_bytes=48 * 2**20),
+        compiler_params=pltpu.CompilerParams(vmem_limit_bytes=44 * 2**20),
         cost_estimate=pl.CostEstimate(
             flops=2 * passages * slots * count * width,
             bytes_accessed=4 * passages * slots * width * 2,
             transcendentals=0,
         ),
-    )(*[pltpu.with_memory_space_constraint(x, pltpu.HBM) for x in operands])
+    )(*scalars, *arrays)
 
 
 def plan_kernel(shards, cap, passages, queries_hbm, candidates_hbm, block, plan, candidates, query_sem, cand_sem):
@@ -162,14 +174,23 @@
     )(*[pltpu.with_memory_space_constraint(x, pltpu.HBM) for x in operands])
 
 
-def exact_dot(a, b, dims):
-    return lax.dot_general(
-        a,
-        b,
+def pieces(values):
+    high = values.astype(jnp.bfloat16)
+    rest = values - high.astype(jnp.float32)
+    middle = rest.astype(jnp.bfloat16)
+    low = (rest - middle.astype(jnp.float32)).astype(jnp.bfloat16)
+    return [high, middle, low]
+
+
+def exact_dot(values, mask, dims):
+    rows = values.shape[0]
+    parts = lax.dot_general(
+        jnp.concatenate(pieces(values), axis=0),
+        mask.astype(jnp.bfloat16),
         (dims, ((), ())),
-        precision=lax.Precision.HIGHEST,
         preferred_element_type=jnp.float32,
     )
+    return parts[:rows] + parts[rows : 2 * rows] + parts[2 * rows :]
 
 
 def score_kernel(query_tokens, cap, offsets, blocks, rows, out, listed, steps, tops, sem):
@@ -179,7 +200,9 @@
     per_row = shards // META
     me = lax.axis_index("shard")
     pairs = shards * cap
-    max_steps = listed.shape[0]
+    max_steps = tops.shape[0] // 2
+    bits = (passages - 1).bit_length()
+    span = 1 << bits
 
     lists = blocks[:, block_rows - META :, :].reshape(shards * META, LANES)
     shape = (pairs, shards * META)
@@ -217,20 +240,14 @@
     query_row = pair_row // cap * (block_rows // 16) + (code_row - 1) // passages * (
         query_tokens // 16
     )
-    shape = (max_steps, pairs)
-    in_step = lax.broadcasted_iota(jnp.int32, shape, 0) == step_row
-    at_place = lax.broadcasted_iota(jnp.int32, (LANES, pairs), 0) == place_row
-    queries = exact_dot(
-        jnp.where(in_step, query_row.astype(jnp.float32), 0.0),
-        at_place.astype(jnp.float32),
-        ((1,), (1,)),
-    )
-    first = in_step & (place_row == 0)
-    passage = jnp.sum(jnp.where(first, p_row, 0), axis=1, keepdims=True)
-    lane = lax.broadcasted_iota(jnp.int32, (max_steps, LANES), 1)
+    entry = jnp.where(valid, query_row * span + p_row, 0).astype(jnp.float32)
+    in_step = lax.broadcasted_iota(jnp.int32, (LANES, pairs), 0) == step_row
+    in_step = in_step.astype(jnp.float32)
+    here = lax.broadcasted_iota(jnp.int32, (PACK, pairs), 0) == place_row
+    entries = exact_dot(jnp.where(here, entry, 0.0), in_step, ((1,), (1,)))
     total = jnp.sum(need, axis=0, keepdims=True)
-    table = jnp.where(lane == PACK, passage, queries.astype(jnp.int32))
-    listed[...] = jnp.where(lane == PACK + 1, total, table)
+    lane = lax.broadcasted_iota(jnp.int32, (PACK, LANES), 1)
+    listed[...] = jnp.where(lane == LANES - 1, total, entries.astype(jnp.int32))
     copy = pltpu.make_async_copy(listed, steps, sem)
     copy.start()
     tops[...] = jnp.zeros_like(tops)
@@ -240,11 +257,11 @@
 
     def one_step(step):
         packed = [
-            flat[pl.ds(pl.multiple_of(steps[step, k] * 16, 16), query_tokens), :]
+            flat[pl.ds(pl.multiple_of((steps[k, step] >> bits) * 16, 16), query_tokens), :]
             for k in range(PACK)
         ]
         dots = lax.dot_general(
-            rows[steps[step, PACK]],
+            rows[steps[0, step] & (span - 1)],
             jnp.concatenate(packed, axis=0),
             (((1,), (1,)), ((), ())),
             preferred_element_type=jnp.float32,
@@ -253,7 +270,7 @@
         tops[step : step + 1, :] = best[0:1]
         tops[max_steps + step : max_steps + step + 1, :] = best[1:2]
 
-    taken = steps[0, PACK + 1]
+    taken = steps[0, LANES - 1]
     for begin, end in zip(CUTS, CUTS[1:] + (max_steps,)):
 
         @pl.when(taken > begin)
@@ -264,12 +281,18 @@
     shape = (PACK, PACK * query_tokens)
     own = lax.broadcasted_iota(jnp.int32, shape, 1) // query_tokens
     own = (own == lax.broadcasted_iota(jnp.int32, shape, 0)).astype(jnp.float32)
-    sums = exact_dot(own, tops[...], ((1,), (1,)))
-    both = jnp.concatenate([sums[:, :max_steps], sums[:, max_steps:]], axis=0)
-    spread = exact_dot(both, in_step.astype(jnp.float32), ((1,), (0,)))
-    here = lax.broadcasted_iota(jnp.int32, (PACK, pairs), 0) == place_row
-    exact = jnp.sum(jnp.where(here, spread[:PACK], 0.0), axis=0, keepdims=True)
-    approx = jnp.sum(jnp.where(here, spread[PACK:], 0.0), axis=0, keepdims=True)
+    sums = exact_dot(tops[...], own, ((1,), (1,)))
+    spread = [
+        lax.dot_general(
+            jnp.concatenate(pieces(sums[at * max_steps : (at + 1) * max_steps]), axis=1),
+            in_step[:max_steps].astype(jnp.bfloat16),
+            (((0,), (0,)), ((), ())),
+            preferred_element_type=jnp.float32,
+        )
+        for at in range(2)
+    ]
+    exact = jnp.sum(jnp.where(here, spread[0][:PACK] + spread[0][PACK:2*PACK] + spread[0][2*PACK:], 0.0), axis=0, keepdims=True)
+    approx = jnp.sum(jnp.where(here, spread[1][:PACK] + spread[1][PACK:2*PACK] + spread[1][2*PACK:], 0.0), axis=0, keepdims=True)
     shape = (shards, 2 * pairs)
     pair = lax.broadcasted_iota(jnp.int32, shape, 1)
     from_shard = pair % pairs // cap == lax.broadcasted_iota(jnp.int32, shape, 0)
@@ -292,8 +315,8 @@
         functools.partial(score_kernel, query_tokens, cap, offsets),
         out_shape=jax.ShapeDtypeStruct((shards, 8, LANES), jnp.float32),
         scratch_shapes=[
-            pltpu.VMEM((max_steps, LANES), jnp.int32),
-            pltpu.SMEM((max_steps, LANES), jnp.int32),
+            pltpu.VMEM((PACK, LANES), jnp.int32),
+            pltpu.SMEM((PACK, LANES), jnp.int32),
             pltpu.VMEM((2 * max_steps, PACK * query_tokens), jnp.float32),
             pltpu.SemaphoreType.DMA,
         ],
@@ -313,8 +336,14 @@
     target = plan[0:1, :]
     rank = plan[1:2, :]
     source = lax.broadcasted_iota(jnp.int32, (shards * padded, slots), 0)
-    hot = (source == target * padded).astype(jnp.float32)
-    spread = exact_dot(scores[...].reshape(shards * padded, lanes), hot, ((0,), (0,)))
+    hot = (source == target * padded).astype(jnp.bfloat16)
+    values = scores[...].reshape(shards * padded, lanes)
+    spread = sum(
+        lax.dot_general(
+            part, hot, (((0,), (0,)), ((), ())), preferred_element_type=jnp.float32
+        )
+        for part in pieces(values)
+    )
     lane = lax.broadcasted_iota(jnp.int32, (lanes, slots), 0)
     exact = jnp.sum(jnp.where(lane == rank, spread, 0.0), axis=0, keepdims=True)
     approx = jnp.sum(jnp.where(lane == rank + lanes // 2, spread, 0.0), axis=0, keepdims=True)
@@ -345,6 +374,8 @@
         queries.reshape(q_local * query_tokens, width), candidates, shards, cap, passages
     )
     block_rows = block.shape[0]
+    block, codes = lax.optimization_barrier((block, codes))
+    codes, residual_codes, centroids = fetch(codes, residual_codes, centroids)
     offsets = [0]
     stride = shards
     while stride > 1:
@@ -354,7 +385,7 @@
         block = exchange(block, steps, shards)
         offsets = [k ^ at for k in [0] + steps for at in offsets]
         if stride > 1:
-            block, codes = lax.optimization_barrier((block, codes))
+            block, lengths = lax.optimization_barrier((block, lengths))
     rows = decompress(centroids, codes, residual_codes, lengths, bucket_weights)
     scores = score(block.reshape(shards, block_rows, width), rows, offsets, query_tokens, cap)
     back = lax.all_to_all(scores, "shard", split_axis=0, concat_axis=0, tiled=True)

time: 38.9 us -> 37 us (0.951); the launches traced: 38.6 us -> 37.2 us
  waiting for transfers between devices: 4.22 us -> 3.05 us
    pallas_call x0 -> x1, Pallas kernels: none -> 1.71 us  [fetch(): pl.pallas_call(fetch_kernel, in_specs=[pl.BlockSpec(memory_space=pltpu.HB...]
    ppermute x6, waiting for transfers between devices: 4.22 us -> 3.05 us  [exchange(): lax.ppermute(block, 'shard', [(i, i ^ step) for i in range(shards)])]
    pallas_call x1, Pallas kernels: 3.98 us -> 3.13 us  [score(): pl.pallas_call(functools.partial(score_kernel, query_tokens, cap, offsets...]
    pallas_call x1, Pallas kernels: 5.01 us -> 4.33 us  [decompress(): pl.pallas_call(decompress_kernel, in_specs=[pl.BlockSpec(memory_space=plt...]
  transfers between devices with their start and end apart: 6 -> 6, of which waited for: 2 -> 2; matrix products, arithmetic and copies ran while one was open for 0% -> 0% of each run, Pallas kernels for 13% -> 16%
where the time goes in v5:
time: 37 us; the launch traced here: 37.2 us
  blocking collectives  13 us (35%)
  Pallas kernels  11.1 us (30%)
  starting transfers between devices  9.31 us (25%)
  waiting for transfers between devices  3.05 us (8%)
  between operations  0.69 us (2%)
    all_to_all x1, blocking collectives, per_device(): lax.all_to_all(scores, 'shard', split_axis=0, concat_axis=0, tiled=True)  13 us
    ppermute x6, starting transfers between devices, exchange(): lax.ppermute(block, 'shard', [(i, i ^ step) for i in range(shards)])  9.31 us
    pallas_call x1, Pallas kernels, decompress(): pl.pallas_call(decompress_kernel, in_specs=[pl.BlockSpec(memory_space=plt...  4.33 us
    pallas_call x1, Pallas kernels, score(): pl.pallas_call(functools.partial(score_kernel, query_tokens, cap, offsets...  3.13 us
    ppermute x6, waiting for transfers between devices, exchange(): lax.ppermute(block, 'shard', [(i, i ^ step) for i in range(shards)])  3.05 us
    pallas_call x1, Pallas kernels, fetch(): pl.pallas_call(fetch_kernel, in_specs=[pl.BlockSpec(memory_space=pltpu.HB...  1.71 us
    pallas_call x1, Pallas kernels, make_plan(): pl.pallas_call(functools.partial(plan_kernel, shards, cap, passages), in_...  1.04 us
    pallas_call x1, Pallas kernels, pick(): return pl.pallas_call(pick_kernel, out_shape=(result, result))(*operands)  0.88 us
  transfers between devices with their start and end apart: 6, of which 2 were waited for; matrix products, arithmetic and copies ran while one was open for 0% of the time, Pallas kernels for 16%

profile of v5, /device:TPU:0, one launch (start us, length us, event | category | flops | bytes accessed | tf_op | source)
XLA Modules:
  0.0 37.2 jit_solution(14927168055419943577)
XLA Ops:
  0.6 1.0 %shard_map.86 = (bf16[144,128]{1,0:T(8,128)(2,1)S(1)}, s32[8,128]{1,0:T(8,128)S(1)}) custom-call(bf16[128,128]{1,0:T(8,128)(2,1)} %bitcast.3, s32[4,32]{1,0:T(4,128)} %candidates_hbm.1), custom_call_target="tpu_custom_call" | custom-call | tf_op jit(solution)/shard_map/pallas_call | solution.py:161
  1.7 5.1 %collective-permute-start.2 = (bf16[144,128]{1,0:T(8,128)(2,1)S(1)}, bf16[144,128]{1,0:T(8,128)(2,1)S(1)}, u32[]{:S(2)}, u32[]{:S(2)}) collective-permute-start(bf16[144,128]{1,0:T(8,128)(2,1)S(1)} %get-tuple-element.13), channel_id=1, source_target_pairs={{0,24},{2,26},{4,28},{6,30},{8,16},{10,18},{12,20},{14,22},{16,8},... | collective-permute-start | bytes 110600 | tf_op jit(solution)/shard_map/ppermute | solution.py:363
  6.8 0.0 collective-permute-start.1
  6.8 0.6 %collective-permute-start = (bf16[144,128]{1,0:T(8,128)(2,1)S(1)}, bf16[144,128]{1,0:T(8,128)(2,1)S(1)}, u32[]{:S(2)}, u32[]{:S(2)}) collective-permute-start(bf16[144,128]{1,0:T(8,128)(2,1)S(1)} %get-tuple-element.13), channel_id=1, source_target_pairs={{0,8},{2,10},{4,12},{6,14},{8,0},{10,2},{12,4},{14,6},{16,24},{18,... | collective-permute-start | bytes 110600 | tf_op jit(solution)/shard_map/ppermute | solution.py:363
  7.4 1.7 %shard_map.87 = (s32[32,128]{1,0:T(8,128)S(1)}, s32[32,128,128]{2,1,0:T(8,128)S(1)}, bf16[2048,128]{1,0:T(8,128)(2,1)S(1)}) custom-call(s32[32,128]{1,0:T(8,128)} %refs_0_, s32[32,128,128]{2,1,0:T(8,128)} %refs_1_.1, bf16[2048,128]{1,0:T(8,128)(2,1)} %refs_2_.1), custom_call_target="tpu_custom_call" | custom-call | bytes 5275648 | tf_op jit(solution)/shard_map/pallas_call | solution.py:30
  9.2 0.0 collective-permute-done.2
  9.2 2.5 %collective-permute-done.1 = bf16[144,128]{1,0:T(8,128)(2,1)S(1)} collective-permute-done((bf16[144,128]{1,0:T(8,128)(2,1)S(1)}, bf16[144,128]{1,0:T(8,128)(2,1)S(1)}, u32[]{:S(2)}, u32[]{:S(2)}) %collective-permute-start.1) | collective-permute-done | bytes 36896 | tf_op jit(solution)/shard_map/ppermute | solution.py:363
  11.7 0.0 collective-permute-done
  11.7 2.5 %collective-permute-start.5 = (bf16[576,128]{1,0:T(8,128)(2,1)S(1)}, bf16[576,128]{1,0:T(8,128)(2,1)S(1)}, u32[]{:S(2)}, u32[]{:S(2)}) collective-permute-start(bf16[576,128]{1,0:T(8,128)(2,1)S(1)} %pad_maximum_fusion.1), channel_id=1, source_target_pairs={{0,6},{2,4},{4,2},{6,0},{8,14},{10,12},{12,10},{14,8},{16,22},{18,... | collective-permute-start | bytes 442376 | tf_op jit(solution)/shard_map/ppermute | solution.py:363
  14.2 0.5 %collective-permute-start.4 = (bf16[576,128]{1,0:T(8,128)(2,1)S(1)}, bf16[576,128]{1,0:T(8,128)(2,1)S(1)}, u32[]{:S(2)}, u32[]{:S(2)}) collective-permute-start(bf16[576,128]{1,0:T(8,128)(2,1)S(1)} %pad_maximum_fusion.1), channel_id=1, source_target_pairs={{0,4},{2,6},{4,0},{6,2},{8,12},{10,14},{12,8},{14,10},{16,20},{18,... | collective-permute-start | bytes 442376 | tf_op jit(solution)/shard_map/ppermute | solution.py:363
  14.7 0.5 %collective-permute-start.3 = (bf16[576,128]{1,0:T(8,128)(2,1)S(1)}, bf16[576,128]{1,0:T(8,128)(2,1)S(1)}, u32[]{:S(2)}, u32[]{:S(2)}) collective-permute-start(bf16[576,128]{1,0:T(8,128)(2,1)S(1)} %pad_maximum_fusion.1), channel_id=1, source_target_pairs={{0,2},{2,0},{4,6},{6,4},{8,10},{10,8},{12,14},{14,12},{16,18},{18,... | collective-permute-start | bytes 442376 | tf_op jit(solution)/shard_map/ppermute | solution.py:363
  15.2 4.3 %shard_map.88.rows = bf16[32,256,128]{2,1,0:T(8,128)(2,1)S(1)} custom-call(s32[32]{0:T(128)} %lengths_hbm, f32[4]{0:T(128)} %weights_hbm.1, s32[32,128]{1,0:T(8,128)S(1)} %get-tuple-element.17.codes, s32[32,128,128]{2,1,0:T(8,128)S(1)} %get-tuple-element.18.residuals, bf16[2048,128]{1,0:T(8,128)(2,1)S(1)} %get-tuple-element.19.centroids), custom_call_target="tpu_custom_call" | custom-call | flops 2147483648 | bytes 4194304 | tf_op jit(solution)/shard_map/pallas_call | solution.py:101
  19.6 0.0 collective-permute-done.5
  19.6 0.6 %collective-permute-done.4 = bf16[576,128]{1,0:T(8,128)(2,1)S(1)} collective-permute-done((bf16[576,128]{1,0:T(8,128)(2,1)S(1)}, bf16[576,128]{1,0:T(8,128)(2,1)S(1)}, u32[]{:S(2)}, u32[]{:S(2)}) %collective-permute-start.4) | collective-permute-done | bytes 147488 | tf_op jit(solution)/shard_map/ppermute | solution.py:363
  20.1 0.0 collective-permute-done.3
  20.2 3.1 %shard_map.89 = f32[16,8,128]{2,1,0:T(8,128)S(1)} custom-call(bf16[16,144,128]{2,1,0:T(8,128)(2,1)S(1)} %bitcast.2, bf16[32,256,128]{2,1,0:T(8,128)(2,1)S(1)} %shard_map.88.rows), custom_call_target="tpu_custom_call" | custom-call | flops 1073741824 | bytes 2686976 | tf_op jit(solution)/shard_map/pallas_call | solution.py:314
  23.3 13.0 %all_to_all.5.scores = f32[16,8,128]{2,1,0:T(8,128)S(1)} all-to-all(f32[16,8,128]{2,1,0:T(8,128)S(1)} %shard_map.89), channel_id=1, replica_groups=mesh['shard'=16,'rep'=2] {'shard'}, dimensions={0} | all-to-all | bytes 131072 | tf_op jit(solution)/shard_map/all_to_all | solution.py:391
  36.3 0.9 %shard_map.90 = (f32[4,32]{1,0:T(4,128)}, f32[4,32]{1,0:T(4,128)}) custom-call(s32[8,128]{1,0:T(8,128)S(1)} %get-tuple-element.11.plan, f32[16,8,128]{2,1,0:T(8,128)S(1)} %all_to_all.5.scores), custom_call_target="tpu_custom_call" | custom-call | tf_op jit(solution)/shard_map/pallas_call | solution.py:358
  (2 shorter events, 0.1 us)
Async XLA Ops:
  1.7 7.5 %collective-permute-start.2 = (bf16[144,128]{1,0:T(8,128)(2,1)S(1)}, bf16[144,128]{1,0:T(8,128)(2,1)S(1)}, u32[]{:S(2)}, u32[]{:S(2)}) collective-permute-start(bf16[144,128]{1,0:T(8,128)(2,1)S(1)} %get-tuple-element.13), channel_id=1, source_target_pairs={{0,24},{2,26},{4,28},{6,30},{8,16},{10,18},{12,20},{14,22},{16,8},... | collective-permute-start | bytes 110600 | tf_op jit(solution)/shard_map/ppermute | solution.py:363
  6.8 4.9 %collective-permute-start.1 = (bf16[144,128]{1,0:T(8,128)(2,1)S(1)}, bf16[144,128]{1,0:T(8,128)(2,1)S(1)}, u32[]{:S(2)}, u32[]{:S(2)}) collective-permute-start(bf16[144,128]{1,0:T(8,128)(2,1)S(1)} %get-tuple-element.13), channel_id=1, source_target_pairs={{0,16},{2,18},{4,20},{6,22},{8,24},{10,26},{12,28},{14,30},{16,0},... | collective-permute-start | bytes 110600 | tf_op jit(solution)/shard_map/ppermute | solution.py:363
  6.8 4.9 %collective-permute-start = (bf16[144,128]{1,0:T(8,128)(2,1)S(1)}, bf16[144,128]{1,0:T(8,128)(2,1)S(1)}, u32[]{:S(2)}, u32[]{:S(2)}) collective-permute-start(bf16[144,128]{1,0:T(8,128)(2,1)S(1)} %get-tuple-element.13), channel_id=1, source_target_pairs={{0,8},{2,10},{4,12},{6,14},{8,0},{10,2},{12,4},{14,6},{16,24},{18,... | collective-permute-start | bytes 110600 | tf_op jit(solution)/shard_map/ppermute | solution.py:363
  11.7 7.9 %collective-permute-start.5 = (bf16[576,128]{1,0:T(8,128)(2,1)S(1)}, bf16[576,128]{1,0:T(8,128)(2,1)S(1)}, u32[]{:S(2)}, u32[]{:S(2)}) collective-permute-start(bf16[576,128]{1,0:T(8,128)(2,1)S(1)} %pad_maximum_fusion.1), channel_id=1, source_target_pairs={{0,6},{2,4},{4,2},{6,0},{8,14},{10,12},{12,10},{14,8},{16,22},{18,... | collective-permute-start | bytes 442376 | tf_op jit(solution)/shard_map/ppermute | solution.py:363
  14.2 6.0 %collective-permute-start.4 = (bf16[576,128]{1,0:T(8,128)(2,1)S(1)}, bf16[576,128]{1,0:T(8,128)(2,1)S(1)}, u32[]{:S(2)}, u32[]{:S(2)}) collective-permute-start(bf16[576,128]{1,0:T(8,128)(2,1)S(1)} %pad_maximum_fusion.1), channel_id=1, source_target_pairs={{0,4},{2,6},{4,0},{6,2},{8,12},{10,14},{12,8},{14,10},{16,20},{18,... | collective-permute-start | bytes 442376 | tf_op jit(solution)/shard_map/ppermute | solution.py:363
  14.7 5.4 %collective-permute-start.3 = (bf16[576,128]{1,0:T(8,128)(2,1)S(1)}, bf16[576,128]{1,0:T(8,128)(2,1)S(1)}, u32[]{:S(2)}, u32[]{:S(2)}) collective-permute-start(bf16[576,128]{1,0:T(8,128)(2,1)S(1)} %pad_maximum_fusion.1), channel_id=1, source_target_pairs={{0,2},{2,0},{4,6},{6,4},{8,10},{10,8},{12,14},{14,12},{16,18},{18,... | collective-permute-start | bytes 442376 | tf_op jit(solution)/shard_map/ppermute | solution.py:363

commit v6 on v5

--- a/solution.py
+++ b/solution.py
@@ -8,64 +8,94 @@
 from jax.sharding import PartitionSpec as P
 
 GROUP = 256
-STEP = 16
+STEP = 4
 META = 16
 LANES = 128
 PACK = 8
 CUTS = (0, 32, 48)
 
 
-def fetch_kernel(*refs):
-    count = len(refs) // 2
+def fetch_kernel(
+    lengths_hbm, codes_hbm, residuals_hbm, centroids_hbm,
+    residuals, hot, high, table, lengths, codes, centroids, sems,
+):
+    passages, slots = codes.shape
+    count, width = centroids.shape
     copies = [
-        pltpu.make_async_copy(refs[i], refs[count + i], refs[-1].at[i]) for i in range(count)
+        pltpu.make_async_copy(source, target, sems.at[i])
+        for i, (source, target) in enumerate(
+            (
+                (lengths_hbm, lengths),
+                (codes_hbm, codes),
+                (centroids_hbm, centroids),
+                (residuals_hbm, residuals),
+            )
+        )
     ]
     for copy in copies:
         copy.start()
-    for copy in copies:
-        copy.wait()
-
-
-def fetch(*arrays):
+    copies[0].wait()
+    copies[1].wait()
+    columns = jnp.swapaxes(codes[...].astype(jnp.float32), 0, 1).astype(jnp.int32)
+    live = lax.broadcasted_iota(jnp.int32, columns.shape, 0) < lengths[...]
+    columns = jnp.where(live, columns, columns[0:1, :])
+    low = columns % GROUP
+    top = columns // GROUP
+    lane = lax.broadcasted_iota(jnp.int32, (slots, GROUP), 1)
+    for p in range(passages):
+        at = slice(p * slots, (p + 1) * slots)
+        hot[at, :] = (lane == low[:, p : p + 1]).astype(jnp.bfloat16)
+        high[at, :] = jnp.broadcast_to(top[:, p : p + 1], (slots, width))
+    copies[2].wait()
+    for g in range(count // GROUP):
+        table[:, g * width : (g + 1) * width] = centroids[g * GROUP : (g + 1) * GROUP, :]
+    copies[3].wait()
+
+
+def fetch(lengths, codes, residual_codes, centroids):
+    passages, slots = codes.shape
+    count, width = centroids.shape
+    operands = (lengths.reshape(1, passages), codes, residual_codes, centroids)
     return pl.pallas_call(
         fetch_kernel,
-        in_specs=[pl.BlockSpec(memory_space=pltpu.HBM)] * len(arrays),
-        out_specs=[pl.BlockSpec(memory_space=pltpu.VMEM)] * len(arrays),
-        out_shape=[pltpu.VMEM(x.shape, x.dtype) for x in arrays],
-        scratch_shapes=[pltpu.SemaphoreType.DMA((len(arrays),))],
-        compiler_params=pltpu.CompilerParams(vmem_limit_bytes=16 * 2**20),
+        in_specs=[pl.BlockSpec(memory_space=pltpu.HBM)] * len(operands),
+        out_specs=[pl.BlockSpec(memory_space=pltpu.VMEM)] * 4,
+        out_shape=(
+            pltpu.VMEM(residual_codes.shape, residual_codes.dtype),
+            pltpu.VMEM((passages * slots, GROUP), jnp.bfloat16),
+            pltpu.VMEM((passages * slots, width), jnp.int32),
+            pltpu.VMEM((GROUP, count // GROUP * width), jnp.bfloat16),
+        ),
+        scratch_shapes=[
+            pltpu.VMEM((1, passages), lengths.dtype),
+            pltpu.VMEM(codes.shape, codes.dtype),
+            pltpu.VMEM(centroids.shape, centroids.dtype),
+            pltpu.SemaphoreType.DMA((len(operands),)),
+        ],
+        compiler_params=pltpu.CompilerParams(vmem_limit_bytes=24 * 2**20),
         cost_estimate=pl.CostEstimate(
-            flops=0, bytes_accessed=2 * sum(x.nbytes for x in arrays), transcendentals=0
+            flops=0, bytes_accessed=2 * residual_codes.nbytes, transcendentals=0
         ),
-    )(*[pltpu.with_memory_space_constraint(x, pltpu.HBM) for x in arrays])
+    )(*[pltpu.with_memory_space_constraint(x, pltpu.HBM) for x in operands])
 
 
 def decompress_kernel(
-    lengths_hbm, weights_hbm, codes, residuals, centroids, rows_out, lengths, weights, table, sems
+    lengths_hbm, weights_hbm, residuals, hot, high, table, rows_out, lengths, weights, sems
 ):
-    passages, slots = codes.shape
-    count, width = centroids.shape
-    groups = count // GROUP
+    passages, slots, width = residuals.shape
+    groups = table.shape[1] // width
     small = [
         pltpu.make_async_copy(lengths_hbm, lengths, sems.at[0]),
         pltpu.make_async_copy(weights_hbm, weights, sems.at[1]),
     ]
     for copy in small:
         copy.start()
-    for g in range(groups):
-        table[:, g * width : (g + 1) * width] = centroids[g * GROUP : (g + 1) * GROUP, :]
-    code_cols = jnp.swapaxes(codes[...].astype(jnp.float32), 0, 1).astype(jnp.int32)
-    lane = lax.broadcasted_iota(jnp.int32, (slots, GROUP), 1)
     token = lax.broadcasted_iota(jnp.int32, (slots, width), 0)
     for first in range(0, passages, STEP):
-        hot = []
-        high = []
-        for p in range(first, first + STEP):
-            code = code_cols[:, p : p + 1]
-            hot.append((lane == (code % GROUP)).astype(jnp.bfloat16))
-            high.append(jnp.broadcast_to(code // GROUP, (slots, width)))
         spread = jnp.dot(
-            jnp.concatenate(hot, 0), table[...], preferred_element_type=jnp.float32
+            hot[first * slots : (first + STEP) * slots, :],
+            table[...],
+            preferred_element_type=jnp.float32,
         )
         if first == 0:
             for copy in small:
@@ -73,53 +103,55 @@
         for p in range(first, first + STEP):
             at = p - first
             part = spread[at * slots : (at + 1) * slots]
-            cent = part[:, :width]
-            for g in range(1, groups):
-                cent = jnp.where(high[at] == g, part[:, g * width : (g + 1) * width], cent)
+            choice = [part[:, g * width : (g + 1) * width] for g in range(groups)]
+            group = high[p * slots : (p + 1) * slots, :]
+            bit = 1
+            while len(choice) > 1:
+                odd = (group & bit) != 0
+                choice = [
+                    jnp.where(odd, choice[k + 1], choice[k]) for k in range(0, len(choice), 2)
+                ]
+                bit *= 2
+            cent = choice[0]
             code = residuals[p]
+            code = jnp.where(token < lengths[p], code, code[0:1, :])
             odd = (code & 1) == 1
             low = jnp.where(odd, weights[1], weights[0])
             top = jnp.where(odd, weights[3], weights[2])
             values = cent + jnp.where(code >= 2, top, low)
             norm = lax.rsqrt(jnp.sum(values * values, axis=-1, keepdims=True) + 1e-06)
-            exact = values * norm
-            live = token < lengths[p]
-            exact = jnp.where(live, exact, exact[0:1, :])
-            cent = jnp.where(live, cent, cent[0:1, :])
-            rows_out[p, :slots, :] = exact.astype(jnp.bfloat16)
+            rows_out[p, :slots, :] = (values * norm).astype(jnp.bfloat16)
             rows_out[p, slots:, :] = cent.astype(jnp.bfloat16)
 
 
-def decompress(centroids, codes, residual_codes, lengths, bucket_weights):
-    passages, slots = codes.shape
-    count, width = centroids.shape
+def decompress(lengths, bucket_weights, residual_codes, hot, high, table):
+    passages, slots, width = residual_codes.shape
     scalars = [pltpu.with_memory_space_constraint(x, pltpu.HBM) for x in (lengths, bucket_weights)]
     arrays = [
         pltpu.with_memory_space_constraint(x, pltpu.VMEM)
-        for x in (codes, residual_codes, centroids)
+        for x in (residual_codes, hot, high, table)
     ]
     return pl.pallas_call(
         decompress_kernel,
         in_specs=[pl.BlockSpec(memory_space=pltpu.HBM)] * 2
-        + [pl.BlockSpec(memory_space=pltpu.VMEM)] * 3,
+        + [pl.BlockSpec(memory_space=pltpu.VMEM)] * 4,
         out_specs=pl.BlockSpec(memory_space=pltpu.VMEM),
         out_shape=pltpu.VMEM((passages, 2 * slots, width), jnp.bfloat16),
         scratch_shapes=[
             pltpu.SMEM(lengths.shape, lengths.dtype),
             pltpu.SMEM(bucket_weights.shape, bucket_weights.dtype),
-            pltpu.VMEM((GROUP, count // GROUP * width), jnp.bfloat16),
             pltpu.SemaphoreType.DMA((2,)),
         ],
-        compiler_params=pltpu.CompilerParams(vmem_limit_bytes=44 * 2**20),
+        compiler_params=pltpu.CompilerParams(vmem_limit_bytes=40 * 2**20),
         cost_estimate=pl.CostEstimate(
-            flops=2 * passages * slots * count * width,
+            flops=2 * hot.size * table.shape[1],
             bytes_accessed=4 * passages * slots * width * 2,
             transcendentals=0,
         ),
     )(*scalars, *arrays)
 
 
-def plan_kernel(shards, cap, passages, queries_hbm, candidates_hbm, block, plan, candidates, query_sem, cand_sem):
+def plan_kernel(shards, cap, passages, ways, queries_hbm, candidates_hbm, block, plan, candidates, query_sem, cand_sem):
     q_local, top_k = candidates.shape
     tokens = queries_hbm.shape[0]
     send_queries = pltpu.make_async_copy(queries_hbm, block.at[pl.ds(0, tokens)], query_sem)
@@ -141,7 +173,8 @@
     rank = jnp.sum(same.astype(jnp.int32), axis=0, keepdims=True)
     row = lax.broadcasted_iota(jnp.int32, (META, slots), 0)
     left = jnp.where(row == target // per_row, value.astype(jnp.float32), 0.0)
-    lane = lax.broadcasted_iota(jnp.int32, (LANES, slots), 0)
+    digit = lax.axis_index("shard") // (shards // ways)
+    lane = lax.broadcasted_iota(jnp.int32, (LANES, slots), 0) - digit * (per_row * cap)
     right = (lane == target % per_row * cap + rank).astype(jnp.float32)
     lists = lax.dot_general(
         left.astype(jnp.bfloat16),
@@ -155,11 +188,11 @@
     send_queries.wait()
 
 
-def make_plan(queries, candidates, shards, cap, passages):
+def make_plan(queries, candidates, shards, cap, passages, ways):
     tokens, width = queries.shape
     operands = (queries, candidates)
     return pl.pallas_call(
-        functools.partial(plan_kernel, shards, cap, passages),
+        functools.partial(plan_kernel, shards, cap, passages, ways),
         in_specs=[pl.BlockSpec(memory_space=pltpu.HBM)] * 2,
         out_specs=[pl.BlockSpec(memory_space=pltpu.VMEM)] * 2,
         out_shape=(
@@ -193,10 +226,12 @@
     return parts[:rows] + parts[rows : 2 * rows] + parts[2 * rows :]
 
 
-def score_kernel(query_tokens, cap, offsets, blocks, rows, out, listed, steps, tops, sem):
+def score_kernel(query_tokens, cap, ways, offsets, blocks, rows, out, listed, steps, tops, sem):
     passages, doubled, width = rows.shape
     slots = doubled // 2
-    shards, block_rows, _ = blocks.shape
+    outer, block_rows, _ = blocks.shape
+    shards = len(offsets)
+    shard_rows = (block_rows - META) // ways
     per_row = shards // META
     me = lax.axis_index("shard")
     pairs = shards * cap
@@ -204,14 +239,16 @@
     bits = (passages - 1).bit_length()
     span = 1 << bits
 
-    lists = blocks[:, block_rows - META :, :].reshape(shards * META, LANES)
-    shape = (pairs, shards * META)
+    lists = blocks[:, block_rows - META :, :].reshape(outer * META, LANES)
+    shape = (pairs, outer * META)
     pair = lax.broadcasted_iota(jnp.int32, shape, 0)
-    wanted = pair // cap * META + me // per_row
+    wanted = pair // (cap * ways) * META + me // per_row
     pick = (lax.broadcasted_iota(jnp.int32, shape, 1) == wanted).astype(jnp.bfloat16)
     found = jnp.dot(pick, lists, preferred_element_type=jnp.float32)
     shape = (pairs, LANES)
-    lane = me % per_row * cap + lax.broadcasted_iota(jnp.int32, shape, 0) % cap
+    pair = lax.broadcasted_iota(jnp.int32, shape, 0)
+    digit = jnp.bitwise_xor(me // (shards // ways), (ways - pair // cap % ways) % ways)
+    lane = (digit * per_row + me % per_row) * cap + pair % cap
     own = lax.broadcasted_iota(jnp.int32, shape, 1) == lane
     column = jnp.sum(jnp.where(own, found, 0.0), axis=1, keepdims=True)
     wide = jnp.broadcast_to(column, shape)
@@ -237,8 +274,10 @@
     step_row = jnp.where(valid, start + rank // PACK, max_steps)
     place_row = rank % PACK
     pair_row = lax.broadcasted_iota(jnp.int32, (1, pairs), 1)
-    query_row = pair_row // cap * (block_rows // 16) + (code_row - 1) // passages * (
-        query_tokens // 16
+    query_row = (
+        pair_row // (cap * ways) * (block_rows // 16)
+        + pair_row // cap % ways * (shard_rows // 16)
+        + (code_row - 1) // passages * (query_tokens // 16)
     )
     entry = jnp.where(valid, query_row * span + p_row, 0).astype(jnp.float32)
     in_step = lax.broadcasted_iota(jnp.int32, (LANES, pairs), 0) == step_row
@@ -253,7 +292,7 @@
     tops[...] = jnp.zeros_like(tops)
     copy.wait()
 
-    flat = blocks.reshape(shards * block_rows, width)
+    flat = blocks.reshape(outer * block_rows, width)
 
     def one_step(step):
         packed = [
@@ -302,18 +341,17 @@
     lane = pair // pairs * (LANES // 2) + pair % cap
     to_lane = (lax.broadcasted_iota(jnp.int32, shape, 0) == lane).astype(jnp.float32)
     back = exact_dot(scores, to_lane, ((1,), (1,)))
-    out[...] = jnp.zeros_like(out)
     for k, offset in enumerate(offsets):
-        out[jnp.bitwise_xor(me, offset), 0:1, :] = back[k : k + 1, :]
-
-
-def score(blocks, rows, offsets, query_tokens, cap):
+        out[jnp.bitwise_xor(me, offset)] = back[k : k + 1, :]
+
+
+def score(blocks, rows, offsets, query_tokens, cap, ways):
     passages, doubled, width = rows.shape
     shards = len(offsets)
     max_steps = -(-(shards * cap + (PACK - 1) * passages) // (8 * PACK)) * 8
     return pl.pallas_call(
-        functools.partial(score_kernel, query_tokens, cap, offsets),
-        out_shape=jax.ShapeDtypeStruct((shards, 8, LANES), jnp.float32),
+        functools.partial(score_kernel, query_tokens, cap, ways, offsets),
+        out_shape=pltpu.VMEM((shards, 1, LANES), jnp.float32),
         scratch_shapes=[
             pltpu.VMEM((PACK, LANES), jnp.int32),
             pltpu.SMEM((PACK, LANES), jnp.int32),
@@ -362,32 +400,38 @@
     others = [
         lax.ppermute(block, "shard", [(i, i ^ step) for i in range(shards)]) for step in steps
     ]
-    return jnp.concatenate([block] + others, axis=0)
+    return [block] + others
 
 
 def per_device(queries, centroids, codes, residual_codes, lengths, bucket_weights, candidates):
     shards = lax.axis_size("shard")
     passages = codes.shape[0]
     q_local, query_tokens, width = queries.shape
+    tokens = q_local * query_tokens
     cap = max(2, 2 * candidates.size // shards)
+    first_ways = 4 if shards % 4 == 0 else 2
     block, plan = make_plan(
-        queries.reshape(q_local * query_tokens, width), candidates, shards, cap, passages
-    )
-    block_rows = block.shape[0]
+        queries.reshape(tokens, width), candidates, shards, cap, passages, first_ways
+    )
     block, codes = lax.optimization_barrier((block, codes))
-    codes, residual_codes, centroids = fetch(codes, residual_codes, centroids)
+    residual_codes, hot, high, table = fetch(lengths, codes, residual_codes, centroids)
     offsets = [0]
     stride = shards
     while stride > 1:
         ways = 4 if stride % 4 == 0 else 2
+        steps = [stride // ways * k for k in range(ways - 1, 0, -1)]
+        blocks = exchange(block, steps, shards)
+        if stride == shards:
+            block = jnp.concatenate([x[:tokens] for x in blocks] + [sum(x[tokens:] for x in blocks)])
+        else:
+            block = jnp.concatenate(blocks)
+        offsets = [k ^ at for k in [0] + steps for at in offsets]
         stride //= ways
-        steps = [stride * k for k in range(1, ways)]
-        block = exchange(block, steps, shards)
-        offsets = [k ^ at for k in [0] + steps for at in offsets]
         if stride > 1:
             block, lengths = lax.optimization_barrier((block, lengths))
-    rows = decompress(centroids, codes, residual_codes, lengths, bucket_weights)
-    scores = score(block.reshape(shards, block_rows, width), rows, offsets, query_tokens, cap)
+    rows = decompress(lengths, bucket_weights, residual_codes, hot, high, table)
+    blocks = block.reshape(shards // first_ways, first_ways * tokens + META, width)
+    scores = score(blocks, rows, offsets, query_tokens, cap, first_ways)
     back = lax.all_to_all(scores, "shard", split_axis=0, concat_axis=0, tiled=True)
     return pick(plan, back, candidates.shape)
 

time: 37 us -> 36.2 us (0.978)
  blocking collectives: 13 us -> 12.1 us
  Pallas kernels: 11.1 us -> 10.7 us
    pallas_call x1, Pallas kernels: 4.33 us -> 3.38 us  [decompress(): pl.pallas_call(decompress_kernel, in_specs=[pl.BlockSpec(memory_space=plt...]
    all_to_all x1, blocking collectives: 13 us -> 12.1 us  [per_device(): lax.all_to_all(scores, 'shard', split_axis=0, concat_axis=0, tiled=True)]
    pallas_call x1, Pallas kernels: 1.71 us -> 2.22 us  [fetch(): pl.pallas_call(fetch_kernel, in_specs=[pl.BlockSpec(memory_space=pltpu.HB...]
  transfers between devices with their start and end apart: 6 -> 6, of which waited for: 2 -> 3; matrix products, arithmetic and copies ran while one was open for 0% -> 0% of each run, Pallas kernels for 16% -> 16%
where the time goes in v6:
time: 36.2 us; the launch traced here: 36.1 us
  blocking collectives  12.1 us (33%)
  Pallas kernels  10.7 us (30%)
  starting transfers between devices  9.31 us (26%)
  waiting for transfers between devices  3.22 us (9%)
  between operations  0.69 us (2%)
    all_to_all x1, blocking collectives, per_device(): lax.all_to_all(scores, 'shard', split_axis=0, concat_axis=0, tiled=True)  12.1 us
    ppermute x6, starting transfers between devices, exchange(): lax.ppermute(block, 'shard', [(i, i ^ step) for i in range(shards)])  9.31 us
    pallas_call x1, Pallas kernels, decompress(): pl.pallas_call(decompress_kernel, in_specs=[pl.BlockSpec(memory_space=plt...  3.38 us
    ppermute x6, waiting for transfers between devices, exchange(): lax.ppermute(block, 'shard', [(i, i ^ step) for i in range(shards)])  3.22 us
    pallas_call x1, Pallas kernels, score(): pl.pallas_call(functools.partial(score_kernel, query_tokens, cap, ways, o...  3.12 us
    pallas_call x1, Pallas kernels, fetch(): pl.pallas_call(fetch_kernel, in_specs=[pl.BlockSpec(memory_space=pltpu.HB...  2.22 us
    pallas_call x1, Pallas kernels, make_plan(): pl.pallas_call(functools.partial(plan_kernel, shards, cap, passages, ways...  1.04 us
    pallas_call x1, Pallas kernels, pick(): return pl.pallas_call(pick_kernel, out_shape=(result, result))(*operands)  0.9 us
  transfers between devices with their start and end apart: 6, of which 3 were waited for; matrix products, arithmetic and copies ran while one was open for 0% of the time, Pallas kernels for 16%

profile of v6, /device:TPU:0, one launch (start us, length us, event | category | flops | bytes accessed | tf_op | source)
XLA Modules:
  0.0 36.1 jit_solution(8960222035400868087)
XLA Ops:
  0.6 1.0 %shard_map.86 = (bf16[144,128]{1,0:T(8,128)(2,1)S(1)}, s32[8,128]{1,0:T(8,128)S(1)}) custom-call(bf16[128,128]{1,0:T(8,128)(2,1)} %bitcast.4, s32[4,32]{1,0:T(4,128)} %candidates_hbm.1), custom_call_target="tpu_custom_call" | custom-call | tf_op jit(solution)/shard_map/pallas_call | solution.py:194
  1.7 5.1 %collective-permute-start = (bf16[144,128]{1,0:T(8,128)(2,1)S(1)}, bf16[144,128]{1,0:T(8,128)(2,1)S(1)}, u32[]{:S(2)}, u32[]{:S(2)}) collective-permute-start(bf16[144,128]{1,0:T(8,128)(2,1)S(1)} %get-tuple-element.14), channel_id=1, source_target_pairs={{0,24},{2,26},{4,28},{6,30},{8,16},{10,18},{12,20},{14,22},{16,8},... | collective-permute-start | bytes 110600 | tf_op jit(solution)/shard_map/ppermute | solution.py:401
  6.8 0.0 collective-permute-start.1
  6.8 0.6 %collective-permute-start.2 = (bf16[144,128]{1,0:T(8,128)(2,1)S(1)}, bf16[144,128]{1,0:T(8,128)(2,1)S(1)}, u32[]{:S(2)}, u32[]{:S(2)}) collective-permute-start(bf16[144,128]{1,0:T(8,128)(2,1)S(1)} %get-tuple-element.14), channel_id=1, source_target_pairs={{0,8},{2,10},{4,12},{6,14},{8,0},{10,2},{12,4},{14,6},{16,24},{18,... | collective-permute-start | bytes 110600 | tf_op jit(solution)/shard_map/ppermute | solution.py:401
  7.4 2.2 %shard_map.87 = (s32[32,128,128]{2,1,0:T(8,128)S(1)}, bf16[4096,256]{1,0:T(8,128)(2,1)S(1)}, s32[4096,128]{1,0:T(8,128)S(1)}, bf16[256,1024]{1,0:T(8,128)(2,1)S(1)}) custom-call(s32[1,32]{1,0:T(1,128)} %bitcast.5, s32[32,128]{1,0:T(8,128)} %codes_hbm, s32[32,128,128]{2,1,0:T(8,128)} %residuals_hbm.1, bf16[2048,128]{1,0:T(8,128)(2,1)} %centroids_hbm.1), custom_call_target="tpu_custom_call" | custom-call | bytes 4194304 | tf_op jit(solution)/shard_map/pallas_call | solution.py:59
  9.7 0.0 collective-permute-done
  9.7 2.0 %collective-permute-done.1 = bf16[144,128]{1,0:T(8,128)(2,1)S(1)} collective-permute-done((bf16[144,128]{1,0:T(8,128)(2,1)S(1)}, bf16[144,128]{1,0:T(8,128)(2,1)S(1)}, u32[]{:S(2)}, u32[]{:S(2)}) %collective-permute-start.1) | collective-permute-done | bytes 36896 | tf_op jit(solution)/shard_map/ppermute | solution.py:401
  11.7 0.0 collective-permute-done.2
  11.7 2.5 %collective-permute-start.3 = (bf16[528,128]{1,0:T(8,128)(2,1)S(1)}, bf16[528,128]{1,0:T(8,128)(2,1)S(1)}, u32[]{:S(2)}, u32[]{:S(2)}) collective-permute-start(bf16[528,128]{1,0:T(8,128)(2,1)S(1)} %constant_dynamic-update-slice_fusion), channel_id=1, source_target_pairs={{0,6},{2,4},{4,2},{6,0},{8,14},{10,12},{12,10},{14,8},{16,22},{18,... | collective-permute-start | bytes 405512 | tf_op jit(solution)/shard_map/ppermute | solution.py:401
  14.2 0.5 %collective-permute-start.4 = (bf16[528,128]{1,0:T(8,128)(2,1)S(1)}, bf16[528,128]{1,0:T(8,128)(2,1)S(1)}, u32[]{:S(2)}, u32[]{:S(2)}) collective-permute-start(bf16[528,128]{1,0:T(8,128)(2,1)S(1)} %constant_dynamic-update-slice_fusion), channel_id=1, source_target_pairs={{0,4},{2,6},{4,0},{6,2},{8,12},{10,14},{12,8},{14,10},{16,20},{18,... | collective-permute-start | bytes 405512 | tf_op jit(solution)/shard_map/ppermute | solution.py:401
  14.7 0.5 %collective-permute-start.5 = (bf16[528,128]{1,0:T(8,128)(2,1)S(1)}, bf16[528,128]{1,0:T(8,128)(2,1)S(1)}, u32[]{:S(2)}, u32[]{:S(2)}) collective-permute-start(bf16[528,128]{1,0:T(8,128)(2,1)S(1)} %constant_dynamic-update-slice_fusion), channel_id=1, source_target_pairs={{0,2},{2,0},{4,6},{6,4},{8,10},{10,8},{12,14},{14,12},{16,18},{18,... | collective-permute-start | bytes 405512 | tf_op jit(solution)/shard_map/ppermute | solution.py:401
  15.2 3.4 %shard_map.88.rows = bf16[32,256,128]{2,1,0:T(8,128)(2,1)S(1)} custom-call(s32[32]{0:T(128)} %lengths_hbm, f32[4]{0:T(128)} %weights_hbm.1, s32[32,128,128]{2,1,0:T(8,128)S(1)} %get-tuple-element.18.residuals, bf16[4096,256]{1,0:T(8,128)(2,1)S(1)} %get-tuple-element.19.hot, s32[4096,128]{1,0:T(8,128)S(1)} %get-tuple-element.20.high, ...), custom_call_target="tpu_custom_call" | custom-call | flops 2147483648 | bytes 4194304 | tf_op jit(solution)/shard_map/pallas_call | solution.py:134
  18.6 0.5 %collective-permute-done.3 = bf16[528,128]{1,0:T(8,128)(2,1)S(1)} collective-permute-done((bf16[528,128]{1,0:T(8,128)(2,1)S(1)}, bf16[528,128]{1,0:T(8,128)(2,1)S(1)}, u32[]{:S(2)}, u32[]{:S(2)}) %collective-permute-start.3) | collective-permute-done | bytes 135200 | tf_op jit(solution)/shard_map/ppermute | solution.py:401
  19.1 0.8 %collective-permute-done.4 = bf16[528,128]{1,0:T(8,128)(2,1)S(1)} collective-permute-done((bf16[528,128]{1,0:T(8,128)(2,1)S(1)}, bf16[528,128]{1,0:T(8,128)(2,1)S(1)}, u32[]{:S(2)}, u32[]{:S(2)}) %collective-permute-start.4) | collective-permute-done | bytes 135200 | tf_op jit(solution)/shard_map/ppermute | solution.py:401
  19.9 0.0 collective-permute-done.5
  19.9 3.1 %shard_map.89 = f32[16,1,128]{2,1,0:T(1,128)S(1)} custom-call(bf16[4,528,128]{2,1,0:T(8,128)(2,1)S(1)} %bitcast.3, bf16[32,256,128]{2,1,0:T(8,128)(2,1)S(1)} %shard_map.88.rows), custom_call_target="tpu_custom_call" | custom-call | flops 1073741824 | bytes 2637824 | tf_op jit(solution)/shard_map/pallas_call | solution.py:352
  23.1 12.1 %all_to_all.5.scores = f32[16,1,128]{2,1,0:T(1,128)S(1)} all-to-all(f32[16,1,128]{2,1,0:T(1,128)S(1)} %shard_map.89), channel_id=1, replica_groups=mesh['shard'=16,'rep'=2] {'shard'}, dimensions={0} | all-to-all | bytes 16384 | tf_op jit(solution)/shard_map/all_to_all | solution.py:435
  35.2 0.9 %shard_map.90 = (f32[4,32]{1,0:T(4,128)}, f32[4,32]{1,0:T(4,128)}) custom-call(s32[8,128]{1,0:T(8,128)S(1)} %get-tuple-element.12.plan, f32[16,1,128]{2,1,0:T(1,128)S(1)} %all_to_all.5.scores), custom_call_target="tpu_custom_call" | custom-call | tf_op jit(solution)/shard_map/pallas_call | solution.py:396
  (6 shorter events, 0.1 us)
Async XLA Ops:
  1.7 8.0 %collective-permute-start = (bf16[144,128]{1,0:T(8,128)(2,1)S(1)}, bf16[144,128]{1,0:T(8,128)(2,1)S(1)}, u32[]{:S(2)}, u32[]{:S(2)}) collective-permute-start(bf16[144,128]{1,0:T(8,128)(2,1)S(1)} %get-tuple-element.14), channel_id=1, source_target_pairs={{0,24},{2,26},{4,28},{6,30},{8,16},{10,18},{12,20},{14,22},{16,8},... | collective-permute-start | bytes 110600 | tf_op jit(solution)/shard_map/ppermute | solution.py:401
  6.8 4.9 %collective-permute-start.1 = (bf16[144,128]{1,0:T(8,128)(2,1)S(1)}, bf16[144,128]{1,0:T(8,128)(2,1)S(1)}, u32[]{:S(2)}, u32[]{:S(2)}) collective-permute-start(bf16[144,128]{1,0:T(8,128)(2,1)S(1)} %get-tuple-element.14), channel_id=1, source_target_pairs={{0,16},{2,18},{4,20},{6,22},{8,24},{10,26},{12,28},{14,30},{16,0},... | collective-permute-start | bytes 110600 | tf_op jit(solution)/shard_map/ppermute | solution.py:401
  6.8 4.9 %collective-permute-start.2 = (bf16[144,128]{1,0:T(8,128)(2,1)S(1)}, bf16[144,128]{1,0:T(8,128)(2,1)S(1)}, u32[]{:S(2)}, u32[]{:S(2)}) collective-permute-start(bf16[144,128]{1,0:T(8,128)(2,1)S(1)} %get-tuple-element.14), channel_id=1, source_target_pairs={{0,8},{2,10},{4,12},{6,14},{8,0},{10,2},{12,4},{14,6},{16,24},{18,... | collective-permute-start | bytes 110600 | tf_op jit(solution)/shard_map/ppermute | solution.py:401
  11.7 7.4 %collective-permute-start.3 = (bf16[528,128]{1,0:T(8,128)(2,1)S(1)}, bf16[528,128]{1,0:T(8,128)(2,1)S(1)}, u32[]{:S(2)}, u32[]{:S(2)}) collective-permute-start(bf16[528,128]{1,0:T(8,128)(2,1)S(1)} %constant_dynamic-update-slice_fusion), channel_id=1, source_target_pairs={{0,6},{2,4},{4,2},{6,0},{8,14},{10,12},{12,10},{14,8},{16,22},{18,... | collective-permute-start | bytes 405512 | tf_op jit(solution)/shard_map/ppermute | solution.py:401
  14.2 5.7 %collective-permute-start.4 = (bf16[528,128]{1,0:T(8,128)(2,1)S(1)}, bf16[528,128]{1,0:T(8,128)(2,1)S(1)}, u32[]{:S(2)}, u32[]{:S(2)}) collective-permute-start(bf16[528,128]{1,0:T(8,128)(2,1)S(1)} %constant_dynamic-update-slice_fusion), channel_id=1, source_target_pairs={{0,4},{2,6},{4,0},{6,2},{8,12},{10,14},{12,8},{14,10},{16,20},{18,... | collective-permute-start | bytes 405512 | tf_op jit(solution)/shard_map/ppermute | solution.py:401
  14.7 5.2 %collective-permute-start.5 = (bf16[528,128]{1,0:T(8,128)(2,1)S(1)}, bf16[528,128]{1,0:T(8,128)(2,1)S(1)}, u32[]{:S(2)}, u32[]{:S(2)}) collective-permute-start(bf16[528,128]{1,0:T(8,128)(2,1)S(1)} %constant_dynamic-update-slice_fusion), channel_id=1, source_target_pairs={{0,2},{2,0},{4,6},{6,4},{8,10},{10,8},{12,14},{14,12},{16,18},{18,... | collective-permute-start | bytes 405512 | tf_op jit(solution)/shard_map/ppermute | solution.py:401

commit v7 on v6

--- a/solution.py
+++ b/solution.py
@@ -11,8 +11,9 @@
 STEP = 4
 META = 16
 LANES = 128
-PACK = 8
-CUTS = (0, 32, 48)
+PACK = 4
+SIDES = 2
+CUTS = (0, 24, 40)
 
 
 def fetch_kernel(
@@ -271,8 +272,9 @@
     count = jnp.sum((p_iota == p_row).astype(jnp.int32), axis=1, keepdims=True)
     need = (count + PACK - 1) // PACK
     start = jnp.sum(jnp.where(p_iota < p_row, need, 0), axis=0, keepdims=True)
-    step_row = jnp.where(valid, start + rank // PACK, max_steps)
-    place_row = rank % PACK
+    half = start + rank // PACK
+    step_row = jnp.where(valid, half // SIDES, max_steps)
+    place_row = half % SIDES * PACK + rank % PACK
     pair_row = lax.broadcasted_iota(jnp.int32, (1, pairs), 1)
     query_row = (
         pair_row // (cap * ways) * (block_rows // 16)
@@ -282,10 +284,12 @@
     entry = jnp.where(valid, query_row * span + p_row, 0).astype(jnp.float32)
     in_step = lax.broadcasted_iota(jnp.int32, (LANES, pairs), 0) == step_row
     in_step = in_step.astype(jnp.float32)
-    here = lax.broadcasted_iota(jnp.int32, (PACK, pairs), 0) == place_row
+    places = SIDES * PACK
+    here = lax.broadcasted_iota(jnp.int32, (places, pairs), 0) == place_row
     entries = exact_dot(jnp.where(here, entry, 0.0), in_step, ((1,), (1,)))
     total = jnp.sum(need, axis=0, keepdims=True)
-    lane = lax.broadcasted_iota(jnp.int32, (PACK, LANES), 1)
+    lane = lax.broadcasted_iota(jnp.int32, (places, LANES), 1)
+    total = (total + SIDES - 1) // SIDES
     listed[...] = jnp.where(lane == LANES - 1, total, entries.astype(jnp.int32))
     copy = pltpu.make_async_copy(listed, steps, sem)
     copy.start()
@@ -294,18 +298,31 @@
 
     flat = blocks.reshape(outer * block_rows, width)
 
+    blank = jnp.zeros((PACK * query_tokens, width), jnp.bfloat16)
+
     def one_step(step):
-        packed = [
-            flat[pl.ds(pl.multiple_of((steps[k, step] >> bits) * 16, 16), query_tokens), :]
-            for k in range(PACK)
-        ]
+        sides = []
+        packed = []
+        for side in range(SIDES):
+            first = side * PACK
+            sides.append(rows[steps[first, step] & (span - 1)])
+            queries = jnp.concatenate(
+                [
+                    flat[pl.ds(pl.multiple_of((steps[k, step] >> bits) * 16, 16), query_tokens), :]
+                    for k in range(first, first + PACK)
+                ],
+                axis=0,
+            )
+            packed.append(
+                jnp.concatenate([queries if at == side else blank for at in range(SIDES)], axis=1)
+            )
         dots = lax.dot_general(
-            rows[steps[0, step] & (span - 1)],
+            jnp.concatenate(sides, axis=1),
             jnp.concatenate(packed, axis=0),
             (((1,), (1,)), ((), ())),
             preferred_element_type=jnp.float32,
         )
-        best = jnp.max(dots.reshape(2, slots, PACK * query_tokens), axis=1)
+        best = jnp.max(dots.reshape(2, slots, places * query_tokens), axis=1)
         tops[step : step + 1, :] = best[0:1]
         tops[max_steps + step : max_steps + step + 1, :] = best[1:2]
 
@@ -317,21 +334,24 @@
             for step in range(begin, end):
                 one_step(step)
 
-    shape = (PACK, PACK * query_tokens)
+    shape = (places, places * query_tokens)
     own = lax.broadcasted_iota(jnp.int32, shape, 1) // query_tokens
     own = (own == lax.broadcasted_iota(jnp.int32, shape, 0)).astype(jnp.float32)
-    sums = exact_dot(tops[...], own, ((1,), (1,)))
+    parts = lax.dot_general(
+        own.astype(jnp.bfloat16),
+        jnp.concatenate(pieces(tops[...]), axis=0),
+        (((1,), (1,)), ((), ())),
+        preferred_element_type=jnp.float32,
+    )
+    rows_of = 2 * max_steps
+    sums = parts[:, :rows_of] + parts[:, rows_of : 2 * rows_of] + parts[:, 2 * rows_of :]
+    by_step = in_step[:max_steps]
     spread = [
-        lax.dot_general(
-            jnp.concatenate(pieces(sums[at * max_steps : (at + 1) * max_steps]), axis=1),
-            in_step[:max_steps].astype(jnp.bfloat16),
-            (((0,), (0,)), ((), ())),
-            preferred_element_type=jnp.float32,
-        )
+        exact_dot(sums[:, at * max_steps : (at + 1) * max_steps], by_step, ((1,), (0,)))
         for at in range(2)
     ]
-    exact = jnp.sum(jnp.where(here, spread[0][:PACK] + spread[0][PACK:2*PACK] + spread[0][2*PACK:], 0.0), axis=0, keepdims=True)
-    approx = jnp.sum(jnp.where(here, spread[1][:PACK] + spread[1][PACK:2*PACK] + spread[1][2*PACK:], 0.0), axis=0, keepdims=True)
+    exact = jnp.sum(jnp.where(here, spread[0], 0.0), axis=0, keepdims=True)
+    approx = jnp.sum(jnp.where(here, spread[1], 0.0), axis=0, keepdims=True)
     shape = (shards, 2 * pairs)
     pair = lax.broadcasted_iota(jnp.int32, shape, 1)
     from_shard = pair % pairs // cap == lax.broadcasted_iota(jnp.int32, shape, 0)
@@ -348,19 +368,20 @@
 def score(blocks, rows, offsets, query_tokens, cap, ways):
     passages, doubled, width = rows.shape
     shards = len(offsets)
-    max_steps = -(-(shards * cap + (PACK - 1) * passages) // (8 * PACK)) * 8
+    places = SIDES * PACK
+    max_steps = -(-(shards * cap + (PACK - 1) * passages) // (8 * places)) * 8
     return pl.pallas_call(
         functools.partial(score_kernel, query_tokens, cap, ways, offsets),
         out_shape=pltpu.VMEM((shards, 1, LANES), jnp.float32),
         scratch_shapes=[
-            pltpu.VMEM((PACK, LANES), jnp.int32),
-            pltpu.SMEM((PACK, LANES), jnp.int32),
-            pltpu.VMEM((2 * max_steps, PACK * query_tokens), jnp.float32),
+            pltpu.VMEM((places, LANES), jnp.int32),
+            pltpu.SMEM((places, LANES), jnp.int32),
+            pltpu.VMEM((2 * max_steps, places * query_tokens), jnp.float32),
             pltpu.SemaphoreType.DMA,
         ],
         compiler_params=pltpu.CompilerParams(vmem_limit_bytes=48 * 2**20),
         cost_estimate=pl.CostEstimate(
-            flops=2 * max_steps * PACK * query_tokens * doubled * width,
+            flops=2 * max_steps * places * query_tokens * doubled * width,
             bytes_accessed=2 * (blocks.size + rows.size),
             transcendentals=0,
         ),

time: 36.2 us -> 35.5 us (0.981)
  blocking collectives: 12.1 us -> 11.6 us
    all_to_all x1, blocking collectives: 12.1 us -> 11.6 us  [per_device(): lax.all_to_all(scores, 'shard', split_axis=0, concat_axis=0, tiled=True)]
where the time goes in v7:
time: 35.5 us; the launch traced here: 35.3 us
  blocking collectives  11.6 us (33%)
  Pallas kernels  10.4 us (29%)
  starting transfers between devices  9.31 us (26%)
  waiting for transfers between devices  3.22 us (9%)
  between operations  0.69 us (2%)
    all_to_all x1, blocking collectives, per_device(): lax.all_to_all(scores, 'shard', split_axis=0, concat_axis=0, tiled=True)  11.6 us
    ppermute x6, starting transfers between devices, exchange(): lax.ppermute(block, 'shard', [(i, i ^ step) for i in range(shards)])  9.31 us
    pallas_call x1, Pallas kernels, decompress(): pl.pallas_call(decompress_kernel, in_specs=[pl.BlockSpec(memory_space=plt...  3.38 us
    ppermute x6, waiting for transfers between devices, exchange(): lax.ppermute(block, 'shard', [(i, i ^ step) for i in range(shards)])  3.22 us
    pallas_call x1, Pallas kernels, score(): pl.pallas_call(functools.partial(score_kernel, query_tokens, cap, ways, o...  2.87 us
    pallas_call x1, Pallas kernels, fetch(): pl.pallas_call(fetch_kernel, in_specs=[pl.BlockSpec(memory_space=pltpu.HB...  2.22 us
    pallas_call x1, Pallas kernels, make_plan(): pl.pallas_call(functools.partial(plan_kernel, shards, cap, passages, ways...  1.04 us
    pallas_call x1, Pallas kernels, pick(): return pl.pallas_call(pick_kernel, out_shape=(result, result))(*operands)  0.9 us
  transfers between devices with their start and end apart: 6, of which 3 were waited for; matrix products, arithmetic and copies ran while one was open for 0% of the time, Pallas kernels for 16%

profile of v7, /device:TPU:0, one launch (start us, length us, event | category | flops | bytes accessed | tf_op | source)
XLA Modules:
  0.0 35.3 jit_solution(261097713630896885)
XLA Ops:
  0.6 1.0 %shard_map.86 = (bf16[144,128]{1,0:T(8,128)(2,1)S(1)}, s32[8,128]{1,0:T(8,128)S(1)}) custom-call(bf16[128,128]{1,0:T(8,128)(2,1)} %bitcast.4, s32[4,32]{1,0:T(4,128)} %candidates_hbm.1), custom_call_target="tpu_custom_call" | custom-call | tf_op jit(solution)/shard_map/pallas_call | solution.py:195
  1.7 5.1 %collective-permute-start = (bf16[144,128]{1,0:T(8,128)(2,1)S(1)}, bf16[144,128]{1,0:T(8,128)(2,1)S(1)}, u32[]{:S(2)}, u32[]{:S(2)}) collective-permute-start(bf16[144,128]{1,0:T(8,128)(2,1)S(1)} %get-tuple-element.14), channel_id=1, source_target_pairs={{0,24},{2,26},{4,28},{6,30},{8,16},{10,18},{12,20},{14,22},{16,8},... | collective-permute-start | bytes 110600 | tf_op jit(solution)/shard_map/ppermute | solution.py:422
  6.8 0.0 collective-permute-start.1
  6.8 0.6 %collective-permute-start.2 = (bf16[144,128]{1,0:T(8,128)(2,1)S(1)}, bf16[144,128]{1,0:T(8,128)(2,1)S(1)}, u32[]{:S(2)}, u32[]{:S(2)}) collective-permute-start(bf16[144,128]{1,0:T(8,128)(2,1)S(1)} %get-tuple-element.14), channel_id=1, source_target_pairs={{0,8},{2,10},{4,12},{6,14},{8,0},{10,2},{12,4},{14,6},{16,24},{18,... | collective-permute-start | bytes 110600 | tf_op jit(solution)/shard_map/ppermute | solution.py:422
  7.4 2.2 %shard_map.87 = (s32[32,128,128]{2,1,0:T(8,128)S(1)}, bf16[4096,256]{1,0:T(8,128)(2,1)S(1)}, s32[4096,128]{1,0:T(8,128)S(1)}, bf16[256,1024]{1,0:T(8,128)(2,1)S(1)}) custom-call(s32[1,32]{1,0:T(1,128)} %bitcast.5, s32[32,128]{1,0:T(8,128)} %codes_hbm, s32[32,128,128]{2,1,0:T(8,128)} %residuals_hbm.1, bf16[2048,128]{1,0:T(8,128)(2,1)} %centroids_hbm.1), custom_call_target="tpu_custom_call" | custom-call | bytes 4194304 | tf_op jit(solution)/shard_map/pallas_call | solution.py:60
  9.7 0.0 collective-permute-done
  9.7 2.0 %collective-permute-done.1 = bf16[144,128]{1,0:T(8,128)(2,1)S(1)} collective-permute-done((bf16[144,128]{1,0:T(8,128)(2,1)S(1)}, bf16[144,128]{1,0:T(8,128)(2,1)S(1)}, u32[]{:S(2)}, u32[]{:S(2)}) %collective-permute-start.1) | collective-permute-done | bytes 36896 | tf_op jit(solution)/shard_map/ppermute | solution.py:422
  11.7 0.0 collective-permute-done.2
  11.7 2.5 %collective-permute-start.3 = (bf16[528,128]{1,0:T(8,128)(2,1)S(1)}, bf16[528,128]{1,0:T(8,128)(2,1)S(1)}, u32[]{:S(2)}, u32[]{:S(2)}) collective-permute-start(bf16[528,128]{1,0:T(8,128)(2,1)S(1)} %constant_dynamic-update-slice_fusion), channel_id=1, source_target_pairs={{0,6},{2,4},{4,2},{6,0},{8,14},{10,12},{12,10},{14,8},{16,22},{18,... | collective-permute-start | bytes 405512 | tf_op jit(solution)/shard_map/ppermute | solution.py:422
  14.2 0.5 %collective-permute-start.4 = (bf16[528,128]{1,0:T(8,128)(2,1)S(1)}, bf16[528,128]{1,0:T(8,128)(2,1)S(1)}, u32[]{:S(2)}, u32[]{:S(2)}) collective-permute-start(bf16[528,128]{1,0:T(8,128)(2,1)S(1)} %constant_dynamic-update-slice_fusion), channel_id=1, source_target_pairs={{0,4},{2,6},{4,0},{6,2},{8,12},{10,14},{12,8},{14,10},{16,20},{18,... | collective-permute-start | bytes 405512 | tf_op jit(solution)/shard_map/ppermute | solution.py:422
  14.7 0.5 %collective-permute-start.5 = (bf16[528,128]{1,0:T(8,128)(2,1)S(1)}, bf16[528,128]{1,0:T(8,128)(2,1)S(1)}, u32[]{:S(2)}, u32[]{:S(2)}) collective-permute-start(bf16[528,128]{1,0:T(8,128)(2,1)S(1)} %constant_dynamic-update-slice_fusion), channel_id=1, source_target_pairs={{0,2},{2,0},{4,6},{6,4},{8,10},{10,8},{12,14},{14,12},{16,18},{18,... | collective-permute-start | bytes 405512 | tf_op jit(solution)/shard_map/ppermute | solution.py:422
  15.2 3.4 %shard_map.88.rows = bf16[32,256,128]{2,1,0:T(8,128)(2,1)S(1)} custom-call(s32[32]{0:T(128)} %lengths_hbm, f32[4]{0:T(128)} %weights_hbm.1, s32[32,128,128]{2,1,0:T(8,128)S(1)} %get-tuple-element.18.residuals, bf16[4096,256]{1,0:T(8,128)(2,1)S(1)} %get-tuple-element.19.hot, s32[4096,128]{1,0:T(8,128)S(1)} %get-tuple-element.20.high, ...), custom_call_target="tpu_custom_call" | custom-call | flops 2147483648 | bytes 4194304 | tf_op jit(solution)/shard_map/pallas_call | solution.py:135
  18.6 0.5 %collective-permute-done.3 = bf16[528,128]{1,0:T(8,128)(2,1)S(1)} collective-permute-done((bf16[528,128]{1,0:T(8,128)(2,1)S(1)}, bf16[528,128]{1,0:T(8,128)(2,1)S(1)}, u32[]{:S(2)}, u32[]{:S(2)}) %collective-permute-start.3) | collective-permute-done | bytes 135200 | tf_op jit(solution)/shard_map/ppermute | solution.py:422
  19.1 0.8 %collective-permute-done.4 = bf16[528,128]{1,0:T(8,128)(2,1)S(1)} collective-permute-done((bf16[528,128]{1,0:T(8,128)(2,1)S(1)}, bf16[528,128]{1,0:T(8,128)(2,1)S(1)}, u32[]{:S(2)}, u32[]{:S(2)}) %collective-permute-start.4) | collective-permute-done | bytes 135200 | tf_op jit(solution)/shard_map/ppermute | solution.py:422
  19.9 0.0 collective-permute-done.5
  19.9 2.9 %shard_map.89 = f32[16,1,128]{2,1,0:T(1,128)S(1)} custom-call(bf16[4,528,128]{2,1,0:T(8,128)(2,1)S(1)} %bitcast.3, bf16[32,256,128]{2,1,0:T(8,128)(2,1)S(1)} %shard_map.88.rows), custom_call_target="tpu_custom_call" | custom-call | flops 805306368 | bytes 2637824 | tf_op jit(solution)/shard_map/pallas_call | solution.py:373
  22.8 11.6 %all_to_all.5.scores = f32[16,1,128]{2,1,0:T(1,128)S(1)} all-to-all(f32[16,1,128]{2,1,0:T(1,128)S(1)} %shard_map.89), channel_id=1, replica_groups=mesh['shard'=16,'rep'=2] {'shard'}, dimensions={0} | all-to-all | bytes 16384 | tf_op jit(solution)/shard_map/all_to_all | solution.py:456
  34.4 0.9 %shard_map.90 = (f32[4,32]{1,0:T(4,128)}, f32[4,32]{1,0:T(4,128)}) custom-call(s32[8,128]{1,0:T(8,128)S(1)} %get-tuple-element.12.plan, f32[16,1,128]{2,1,0:T(1,128)S(1)} %all_to_all.5.scores), custom_call_target="tpu_custom_call" | custom-call | tf_op jit(solution)/shard_map/pallas_call | solution.py:417
  (6 shorter events, 0.1 us)
Async XLA Ops:
  1.7 8.0 %collective-permute-start = (bf16[144,128]{1,0:T(8,128)(2,1)S(1)}, bf16[144,128]{1,0:T(8,128)(2,1)S(1)}, u32[]{:S(2)}, u32[]{:S(2)}) collective-permute-start(bf16[144,128]{1,0:T(8,128)(2,1)S(1)} %get-tuple-element.14), channel_id=1, source_target_pairs={{0,24},{2,26},{4,28},{6,30},{8,16},{10,18},{12,20},{14,22},{16,8},... | collective-permute-start | bytes 110600 | tf_op jit(solution)/shard_map/ppermute | solution.py:422
  6.8 4.9 %collective-permute-start.1 = (bf16[144,128]{1,0:T(8,128)(2,1)S(1)}, bf16[144,128]{1,0:T(8,128)(2,1)S(1)}, u32[]{:S(2)}, u32[]{:S(2)}) collective-permute-start(bf16[144,128]{1,0:T(8,128)(2,1)S(1)} %get-tuple-element.14), channel_id=1, source_target_pairs={{0,16},{2,18},{4,20},{6,22},{8,24},{10,26},{12,28},{14,30},{16,0},... | collective-permute-start | bytes 110600 | tf_op jit(solution)/shard_map/ppermute | solution.py:422
  6.8 4.9 %collective-permute-start.2 = (bf16[144,128]{1,0:T(8,128)(2,1)S(1)}, bf16[144,128]{1,0:T(8,128)(2,1)S(1)}, u32[]{:S(2)}, u32[]{:S(2)}) collective-permute-start(bf16[144,128]{1,0:T(8,128)(2,1)S(1)} %get-tuple-element.14), channel_id=1, source_target_pairs={{0,8},{2,10},{4,12},{6,14},{8,0},{10,2},{12,4},{14,6},{16,24},{18,... | collective-permute-start | bytes 110600 | tf_op jit(solution)/shard_map/ppermute | solution.py:422
  11.7 7.4 %collective-permute-start.3 = (bf16[528,128]{1,0:T(8,128)(2,1)S(1)}, bf16[528,128]{1,0:T(8,128)(2,1)S(1)}, u32[]{:S(2)}, u32[]{:S(2)}) collective-permute-start(bf16[528,128]{1,0:T(8,128)(2,1)S(1)} %constant_dynamic-update-slice_fusion), channel_id=1, source_target_pairs={{0,6},{2,4},{4,2},{6,0},{8,14},{10,12},{12,10},{14,8},{16,22},{18,... | collective-permute-start | bytes 405512 | tf_op jit(solution)/shard_map/ppermute | solution.py:422
  14.2 5.7 %collective-permute-start.4 = (bf16[528,128]{1,0:T(8,128)(2,1)S(1)}, bf16[528,128]{1,0:T(8,128)(2,1)S(1)}, u32[]{:S(2)}, u32[]{:S(2)}) collective-permute-start(bf16[528,128]{1,0:T(8,128)(2,1)S(1)} %constant_dynamic-update-slice_fusion), channel_id=1, source_target_pairs={{0,4},{2,6},{4,0},{6,2},{8,12},{10,14},{12,8},{14,10},{16,20},{18,... | collective-permute-start | bytes 405512 | tf_op jit(solution)/shard_map/ppermute | solution.py:422
  14.7 5.2 %collective-permute-start.5 = (bf16[528,128]{1,0:T(8,128)(2,1)S(1)}, bf16[528,128]{1,0:T(8,128)(2,1)S(1)}, u32[]{:S(2)}, u32[]{:S(2)}) collective-permute-start(bf16[528,128]{1,0:T(8,128)(2,1)S(1)} %constant_dynamic-update-slice_fusion), channel_id=1, source_target_pairs={{0,2},{2,0},{4,6},{6,4},{8,10},{10,8},{12,14},{14,12},{16,18},{18,... | collective-permute-start | bytes 405512 | tf_op jit(solution)/shard_map/ppermute | solution.py:422

commit v8 on v7

--- a/solution.py
+++ b/solution.py
@@ -16,29 +16,23 @@
 CUTS = (0, 24, 40)
 
 
-def fetch_kernel(
-    lengths_hbm, codes_hbm, residuals_hbm, centroids_hbm,
-    residuals, hot, high, table, lengths, codes, centroids, sems,
-):
-    passages, slots = codes.shape
-    count, width = centroids.shape
+def start_copies(sources, targets, sems):
     copies = [
         pltpu.make_async_copy(source, target, sems.at[i])
-        for i, (source, target) in enumerate(
-            (
-                (lengths_hbm, lengths),
-                (codes_hbm, codes),
-                (centroids_hbm, centroids),
-                (residuals_hbm, residuals),
-            )
-        )
+        for i, (source, target) in enumerate(zip(sources, targets))
     ]
     for copy in copies:
         copy.start()
+    return copies
+
+
+def prepare(copies, lengths_row, codes, centroids, hot, high, table):
+    passages, slots = codes.shape
+    count, width = centroids.shape
     copies[0].wait()
     copies[1].wait()
     columns = jnp.swapaxes(codes[...].astype(jnp.float32), 0, 1).astype(jnp.int32)
-    live = lax.broadcasted_iota(jnp.int32, columns.shape, 0) < lengths[...]
+    live = lax.broadcasted_iota(jnp.int32, columns.shape, 0) < lengths_row[...]
     columns = jnp.where(live, columns, columns[0:1, :])
     low = columns % GROUP
     top = columns // GROUP
@@ -50,106 +44,149 @@
     copies[2].wait()
     for g in range(count // GROUP):
         table[:, g * width : (g + 1) * width] = centroids[g * GROUP : (g + 1) * GROUP, :]
-    copies[3].wait()
-
-
-def fetch(lengths, codes, residual_codes, centroids):
-    passages, slots = codes.shape
-    count, width = centroids.shape
-    operands = (lengths.reshape(1, passages), codes, residual_codes, centroids)
+    for copy in copies[3:]:
+        copy.wait()
+
+
+def build_rows(first, residuals, hot, high, table, rows, lengths, weights):
+    _, slots, width = residuals.shape
+    groups = table.shape[1] // width
+    token = lax.broadcasted_iota(jnp.int32, (slots, width), 0)
+    spread = jnp.dot(
+        hot[first * slots : (first + STEP) * slots, :],
+        table[...],
+        preferred_element_type=jnp.float32,
+    )
+    for p in range(first, first + STEP):
+        at = p - first
+        part = spread[at * slots : (at + 1) * slots]
+        choice = [part[:, g * width : (g + 1) * width] for g in range(groups)]
+        group = high[p * slots : (p + 1) * slots, :]
+        bit = 1
+        while len(choice) > 1:
+            odd = (group & bit) != 0
+            choice = [jnp.where(odd, choice[k + 1], choice[k]) for k in range(0, len(choice), 2)]
+            bit *= 2
+        cent = choice[0]
+        code = residuals[p]
+        code = jnp.where(token < lengths[p], code, code[0:1, :])
+        odd = (code & 1) == 1
+        low = jnp.where(odd, weights[1], weights[0])
+        top = jnp.where(odd, weights[3], weights[2])
+        values = cent + jnp.where(code >= 2, top, low)
+        norm = lax.rsqrt(jnp.sum(values * values, axis=-1, keepdims=True) + 1e-06)
+        rows[p, :slots, :] = (values * norm).astype(jnp.bfloat16)
+        rows[p, slots:, :] = cent.astype(jnp.bfloat16)
+
+
+def fetches_late(ways):
+    shards = lax.axis_size("shard")
+    odd_member = lax.axis_index("shard") // (shards // ways) % 2 == 1
+    return jnp.logical_and(odd_member, lax.axis_index("rep") % 2 == 1)
+
+
+def fetch_kernel(ways, *refs):
+    sources = refs[:6]
+    residuals, hot, high, table = refs[6:10]
+    lengths_row, codes, centroids, lengths, weights, sems = refs[10:]
+
+    @pl.when(jnp.logical_not(fetches_late(ways)))
+    def _():
+        targets = (lengths_row, codes, centroids, lengths, weights, residuals)
+        copies = start_copies(sources, targets, sems)
+        prepare(copies, lengths_row, codes, centroids, hot, high, table)
+
+
+def index_scratch(lengths, bucket_weights, codes, centroids, count):
+    return [
+        pltpu.VMEM((1, lengths.shape[0]), lengths.dtype),
+        pltpu.VMEM(codes.shape, codes.dtype),
+        pltpu.VMEM(centroids.shape, centroids.dtype),
+        pltpu.SMEM(lengths.shape, lengths.dtype),
+        pltpu.SMEM(bucket_weights.shape, bucket_weights.dtype),
+        pltpu.SemaphoreType.DMA((count,)),
+    ]
+
+
+def index_arrays(codes, centroids, width):
+    tokens = codes.size
+    return [
+        pltpu.VMEM(codes.shape + (width,), jnp.int32),
+        pltpu.VMEM((tokens, GROUP), jnp.bfloat16),
+        pltpu.VMEM((tokens, width), jnp.int32),
+        pltpu.VMEM((GROUP, centroids.size // GROUP), jnp.bfloat16),
+    ]
+
+
+def fetch(lengths, bucket_weights, codes, residual_codes, centroids, ways):
+    passages = codes.shape[0]
+    width = centroids.shape[1]
+    operands = (
+        lengths.reshape(1, passages), codes, centroids, lengths, bucket_weights, residual_codes
+    )
     return pl.pallas_call(
-        fetch_kernel,
+        functools.partial(fetch_kernel, ways),
         in_specs=[pl.BlockSpec(memory_space=pltpu.HBM)] * len(operands),
         out_specs=[pl.BlockSpec(memory_space=pltpu.VMEM)] * 4,
-        out_shape=(
-            pltpu.VMEM(residual_codes.shape, residual_codes.dtype),
-            pltpu.VMEM((passages * slots, GROUP), jnp.bfloat16),
-            pltpu.VMEM((passages * slots, width), jnp.int32),
-            pltpu.VMEM((GROUP, count // GROUP * width), jnp.bfloat16),
-        ),
-        scratch_shapes=[
-            pltpu.VMEM((1, passages), lengths.dtype),
-            pltpu.VMEM(codes.shape, codes.dtype),
-            pltpu.VMEM(centroids.shape, centroids.dtype),
-            pltpu.SemaphoreType.DMA((len(operands),)),
-        ],
-        compiler_params=pltpu.CompilerParams(vmem_limit_bytes=24 * 2**20),
+        out_shape=index_arrays(codes, centroids, width),
+        scratch_shapes=index_scratch(lengths, bucket_weights, codes, centroids, len(operands)),
+        compiler_params=pltpu.CompilerParams(vmem_limit_bytes=32 * 2**20),
         cost_estimate=pl.CostEstimate(
             flops=0, bytes_accessed=2 * residual_codes.nbytes, transcendentals=0
         ),
     )(*[pltpu.with_memory_space_constraint(x, pltpu.HBM) for x in operands])
 
 
-def decompress_kernel(
-    lengths_hbm, weights_hbm, residuals, hot, high, table, rows_out, lengths, weights, sems
-):
-    passages, slots, width = residuals.shape
-    groups = table.shape[1] // width
-    small = [
-        pltpu.make_async_copy(lengths_hbm, lengths, sems.at[0]),
-        pltpu.make_async_copy(weights_hbm, weights, sems.at[1]),
-    ]
-    for copy in small:
-        copy.start()
-    token = lax.broadcasted_iota(jnp.int32, (slots, width), 0)
-    for first in range(0, passages, STEP):
-        spread = jnp.dot(
-            hot[first * slots : (first + STEP) * slots, :],
-            table[...],
-            preferred_element_type=jnp.float32,
-        )
-        if first == 0:
-            for copy in small:
-                copy.wait()
-        for p in range(first, first + STEP):
-            at = p - first
-            part = spread[at * slots : (at + 1) * slots]
-            choice = [part[:, g * width : (g + 1) * width] for g in range(groups)]
-            group = high[p * slots : (p + 1) * slots, :]
-            bit = 1
-            while len(choice) > 1:
-                odd = (group & bit) != 0
-                choice = [
-                    jnp.where(odd, choice[k + 1], choice[k]) for k in range(0, len(choice), 2)
-                ]
-                bit *= 2
-            cent = choice[0]
-            code = residuals[p]
-            code = jnp.where(token < lengths[p], code, code[0:1, :])
-            odd = (code & 1) == 1
-            low = jnp.where(odd, weights[1], weights[0])
-            top = jnp.where(odd, weights[3], weights[2])
-            values = cent + jnp.where(code >= 2, top, low)
-            norm = lax.rsqrt(jnp.sum(values * values, axis=-1, keepdims=True) + 1e-06)
-            rows_out[p, :slots, :] = (values * norm).astype(jnp.bfloat16)
-            rows_out[p, slots:, :] = cent.astype(jnp.bfloat16)
-
-
-def decompress(lengths, bucket_weights, residual_codes, hot, high, table):
-    passages, slots, width = residual_codes.shape
-    scalars = [pltpu.with_memory_space_constraint(x, pltpu.HBM) for x in (lengths, bucket_weights)]
-    arrays = [
-        pltpu.with_memory_space_constraint(x, pltpu.VMEM)
-        for x in (residual_codes, hot, high, table)
-    ]
+def decompress_kernel(ways, *refs):
+    sources = refs[:6]
+    early = refs[6:10]
+    rows = refs[10]
+    lengths_row, codes, centroids, lengths, weights, sems = refs[11:17]
+    own = refs[17:]
+    passages = codes.shape[0]
+    late = fetches_late(ways)
+
+    @pl.when(jnp.logical_not(late))
+    def _():
+        copies = start_copies(sources[3:5], (lengths, weights), sems)
+        for copy in copies:
+            copy.wait()
+        for first in range(0, passages, STEP):
+            build_rows(first, *early, rows, lengths, weights)
+
+    @pl.when(late)
+    def _():
+        targets = (lengths_row, codes, centroids, lengths, weights, own[0])
+        copies = start_copies(sources, targets, sems)
+        prepare(copies, lengths_row, codes, centroids, *own[1:])
+        for first in range(0, passages, STEP):
+            build_rows(first, *own, rows, lengths, weights)
+
+
+def decompress(lengths, bucket_weights, codes, residual_codes, centroids, ways, early):
+    passages, slots = codes.shape
+    width = centroids.shape[1]
+    operands = (
+        lengths.reshape(1, passages), codes, centroids, lengths, bucket_weights, residual_codes
+    )
     return pl.pallas_call(
-        decompress_kernel,
-        in_specs=[pl.BlockSpec(memory_space=pltpu.HBM)] * 2
-        + [pl.BlockSpec(memory_space=pltpu.VMEM)] * 4,
+        functools.partial(decompress_kernel, ways),
+        in_specs=[pl.BlockSpec(memory_space=pltpu.HBM)] * len(operands)
+        + [pl.BlockSpec(memory_space=pltpu.VMEM)] * len(early),
         out_specs=pl.BlockSpec(memory_space=pltpu.VMEM),
         out_shape=pltpu.VMEM((passages, 2 * slots, width), jnp.bfloat16),
-        scratch_shapes=[
-            pltpu.SMEM(lengths.shape, lengths.dtype),
-            pltpu.SMEM(bucket_weights.shape, bucket_weights.dtype),
-            pltpu.SemaphoreType.DMA((2,)),
-        ],
+        scratch_shapes=index_scratch(lengths, bucket_weights, codes, centroids, len(operands))
+        + index_arrays(codes, centroids, width),
         compiler_params=pltpu.CompilerParams(vmem_limit_bytes=40 * 2**20),
         cost_estimate=pl.CostEstimate(
-            flops=2 * hot.size * table.shape[1],
-            bytes_accessed=4 * passages * slots * width * 2,
+            flops=2 * codes.size * centroids.size,
+            bytes_accessed=4 * codes.size * width,
             transcendentals=0,
         ),
-    )(*scalars, *arrays)
+    )(
+        *[pltpu.with_memory_space_constraint(x, pltpu.HBM) for x in operands],
+        *[pltpu.with_memory_space_constraint(x, pltpu.VMEM) for x in early],
+    )
 
 
 def plan_kernel(shards, cap, passages, ways, queries_hbm, candidates_hbm, block, plan, candidates, query_sem, cand_sem):
@@ -435,7 +472,7 @@
         queries.reshape(tokens, width), candidates, shards, cap, passages, first_ways
     )
     block, codes = lax.optimization_barrier((block, codes))
-    residual_codes, hot, high, table = fetch(lengths, codes, residual_codes, centroids)
+    early = fetch(lengths, bucket_weights, codes, residual_codes, centroids, first_ways)
     offsets = [0]
     stride = shards
     while stride > 1:
@@ -450,7 +487,9 @@
         stride //= ways
         if stride > 1:
             block, lengths = lax.optimization_barrier((block, lengths))
-    rows = decompress(lengths, bucket_weights, residual_codes, hot, high, table)
+    rows = decompress(
+        lengths, bucket_weights, codes, residual_codes, centroids, first_ways, early
+    )
     blocks = block.reshape(shards // first_ways, first_ways * tokens + META, width)
     scores = score(blocks, rows, offsets, query_tokens, cap, first_ways)
     back = lax.all_to_all(scores, "shard", split_axis=0, concat_axis=0, tiled=True)

time: 35.5 us -> 35.2 us (level)
  blocking collectives: 11.6 us -> 11.2 us
    all_to_all x1, blocking collectives: 11.6 us -> 11.2 us  [per_device(): lax.all_to_all(scores, 'shard', split_axis=0, concat_axis=0, tiled=True)]
where the time goes in v8:
time: 35.2 us; the launch traced here: 34.9 us
  blocking collectives  11.2 us (32%)
  Pallas kernels  10.5 us (30%)
  starting transfers between devices  9.31 us (26%)
  waiting for transfers between devices  3.1 us (9%)
  between operations  0.69 us (2%)
    all_to_all x1, blocking collectives, per_device(): lax.all_to_all(scores, 'shard', split_axis=0, concat_axis=0, tiled=True)  11.2 us
    ppermute x6, starting transfers between devices, exchange(): lax.ppermute(block, 'shard', [(i, i ^ step) for i in range(shards)])  9.31 us
    pallas_call x1, Pallas kernels, decompress(): pl.pallas_call(functools.partial(decompress_kernel, ways), in_specs=[pl.B...  3.46 us
    ppermute x6, waiting for transfers between devices, exchange(): lax.ppermute(block, 'shard', [(i, i ^ step) for i in range(shards)])  3.1 us
    pallas_call x1, Pallas kernels, score(): pl.pallas_call(functools.partial(score_kernel, query_tokens, cap, ways, o...  2.86 us
    pallas_call x1, Pallas kernels, fetch(): pl.pallas_call(functools.partial(fetch_kernel, ways), in_specs=[pl.BlockS...  2.26 us
    pallas_call x1, Pallas kernels, make_plan(): pl.pallas_call(functools.partial(plan_kernel, shards, cap, passages, ways...  1.04 us
    pallas_call x1, Pallas kernels, pick(): return pl.pallas_call(pick_kernel, out_shape=(result, result))(*operands)  0.9 us
  transfers between devices with their start and end apart: 6, of which 3 were waited for; matrix products, arithmetic and copies ran while one was open for 0% of the time, Pallas kernels for 16%

profile of v8, /device:TPU:0, one launch (start us, length us, event | category | flops | bytes accessed | tf_op | source)
XLA Modules:
  0.0 34.9 jit_solution(18019557034890034295)
XLA Ops:
  0.6 1.0 %shard_map.86 = (bf16[144,128]{1,0:T(8,128)(2,1)S(1)}, s32[8,128]{1,0:T(8,128)S(1)}) custom-call(bf16[128,128]{1,0:T(8,128)(2,1)} %bitcast.5, s32[4,32]{1,0:T(4,128)} %candidates_hbm.1), custom_call_target="tpu_custom_call" | custom-call | tf_op jit(solution)/shard_map/pallas_call | solution.py:232
  1.7 5.1 %collective-permute-start = (bf16[144,128]{1,0:T(8,128)(2,1)S(1)}, bf16[144,128]{1,0:T(8,128)(2,1)S(1)}, u32[]{:S(2)}, u32[]{:S(2)}) collective-permute-start(bf16[144,128]{1,0:T(8,128)(2,1)S(1)} %get-tuple-element.14), channel_id=1, source_target_pairs={{0,24},{2,26},{4,28},{6,30},{8,16},{10,18},{12,20},{14,22},{16,8},... | collective-permute-start | bytes 110600 | tf_op jit(solution)/shard_map/ppermute | solution.py:459
  6.8 0.0 collective-permute-start.1
  6.8 0.6 %collective-permute-start.2 = (bf16[144,128]{1,0:T(8,128)(2,1)S(1)}, bf16[144,128]{1,0:T(8,128)(2,1)S(1)}, u32[]{:S(2)}, u32[]{:S(2)}) collective-permute-start(bf16[144,128]{1,0:T(8,128)(2,1)S(1)} %get-tuple-element.14), channel_id=1, source_target_pairs={{0,8},{2,10},{4,12},{6,14},{8,0},{10,2},{12,4},{14,6},{16,24},{18,... | collective-permute-start | bytes 110600 | tf_op jit(solution)/shard_map/ppermute | solution.py:459
  7.4 2.3 %shard_map.87 = (s32[32,128,128]{2,1,0:T(8,128)S(1)}, bf16[4096,256]{1,0:T(8,128)(2,1)S(1)}, s32[4096,128]{1,0:T(8,128)S(1)}, bf16[256,1024]{1,0:T(8,128)(2,1)S(1)}) custom-call(s32[1,32]{1,0:T(1,128)} %bitcast.6, s32[32,128]{1,0:T(8,128)} %refs_1_.1, bf16[2048,128]{1,0:T(8,128)(2,1)} %refs_2_.3, s32[32]{0:T(128)} %refs_3_.2, f32[4]{0:T(128)} %refs_4_.3, ...), custom_call_target="tpu_custom_call" | custom-call | bytes 4194304 | tf_op jit(solution)/shard_map/pallas_call | solution.py:127
  9.7 0.0 collective-permute-done
  9.7 1.9 %collective-permute-done.1 = bf16[144,128]{1,0:T(8,128)(2,1)S(1)} collective-permute-done((bf16[144,128]{1,0:T(8,128)(2,1)S(1)}, bf16[144,128]{1,0:T(8,128)(2,1)S(1)}, u32[]{:S(2)}, u32[]{:S(2)}) %collective-permute-start.1) | collective-permute-done | bytes 36896 | tf_op jit(solution)/shard_map/ppermute | solution.py:459
  11.7 0.0 collective-permute-done.2
  11.7 2.5 %collective-permute-start.3 = (bf16[528,128]{1,0:T(8,128)(2,1)S(1)}, bf16[528,128]{1,0:T(8,128)(2,1)S(1)}, u32[]{:S(2)}, u32[]{:S(2)}) collective-permute-start(bf16[528,128]{1,0:T(8,128)(2,1)S(1)} %constant_dynamic-update-slice_fusion), channel_id=1, source_target_pairs={{0,6},{2,4},{4,2},{6,0},{8,14},{10,12},{12,10},{14,8},{16,22},{18,... | collective-permute-start | bytes 405512 | tf_op jit(solution)/shard_map/ppermute | solution.py:459
  14.2 0.5 %collective-permute-start.4 = (bf16[528,128]{1,0:T(8,128)(2,1)S(1)}, bf16[528,128]{1,0:T(8,128)(2,1)S(1)}, u32[]{:S(2)}, u32[]{:S(2)}) collective-permute-start(bf16[528,128]{1,0:T(8,128)(2,1)S(1)} %constant_dynamic-update-slice_fusion), channel_id=1, source_target_pairs={{0,4},{2,6},{4,0},{6,2},{8,12},{10,14},{12,8},{14,10},{16,20},{18,... | collective-permute-start | bytes 405512 | tf_op jit(solution)/shard_map/ppermute | solution.py:459
  14.7 0.5 %collective-permute-start.5 = (bf16[528,128]{1,0:T(8,128)(2,1)S(1)}, bf16[528,128]{1,0:T(8,128)(2,1)S(1)}, u32[]{:S(2)}, u32[]{:S(2)}) collective-permute-start(bf16[528,128]{1,0:T(8,128)(2,1)S(1)} %constant_dynamic-update-slice_fusion), channel_id=1, source_target_pairs={{0,2},{2,0},{4,6},{6,4},{8,10},{10,8},{12,14},{14,12},{16,18},{18,... | collective-permute-start | bytes 405512 | tf_op jit(solution)/shard_map/ppermute | solution.py:459
  15.2 3.5 %shard_map.88.rows = bf16[32,256,128]{2,1,0:T(8,128)(2,1)S(1)} custom-call(s32[1,32]{1,0:T(1,128)} %bitcast.7, s32[32,128]{1,0:T(8,128)} %refs_1_.1, bf16[2048,128]{1,0:T(8,128)(2,1)} %refs_2_.3, s32[32]{0:T(128)} %refs_3_.2, f32[4]{0:T(128)} %refs_4_.3, s32[32,128,128]{2,1,0:T(8,128)} %refs_5_.3, s32[32,128,128]{2,1,0:T(8,128)S(1)} %get-tuple-element.18.refs_6_, ...), custom_call_target="tpu_custom_call" | custom-call | flops 2147483648 | bytes 2097152 | tf_op jit(solution)/shard_map/pallas_call | solution.py:172
  18.7 0.4 %collective-permute-done.3 = bf16[528,128]{1,0:T(8,128)(2,1)S(1)} collective-permute-done((bf16[528,128]{1,0:T(8,128)(2,1)S(1)}, bf16[528,128]{1,0:T(8,128)(2,1)S(1)}, u32[]{:S(2)}, u32[]{:S(2)}) %collective-permute-start.3) | collective-permute-done | bytes 135200 | tf_op jit(solution)/shard_map/ppermute | solution.py:459
  19.1 0.8 %collective-permute-done.4 = bf16[528,128]{1,0:T(8,128)(2,1)S(1)} collective-permute-done((bf16[528,128]{1,0:T(8,128)(2,1)S(1)}, bf16[528,128]{1,0:T(8,128)(2,1)S(1)}, u32[]{:S(2)}, u32[]{:S(2)}) %collective-permute-start.4) | collective-permute-done | bytes 135200 | tf_op jit(solution)/shard_map/ppermute | solution.py:459
  19.9 0.0 collective-permute-done.5
  19.9 2.9 %shard_map.89 = f32[16,1,128]{2,1,0:T(1,128)S(1)} custom-call(bf16[4,528,128]{2,1,0:T(8,128)(2,1)S(1)} %bitcast.4, bf16[32,256,128]{2,1,0:T(8,128)(2,1)S(1)} %shard_map.88.rows), custom_call_target="tpu_custom_call" | custom-call | flops 805306368 | bytes 2637824 | tf_op jit(solution)/shard_map/pallas_call | solution.py:410
  22.8 11.2 %all_to_all.5.scores = f32[16,1,128]{2,1,0:T(1,128)S(1)} all-to-all(f32[16,1,128]{2,1,0:T(1,128)S(1)} %shard_map.89), channel_id=1, replica_groups=mesh['shard'=16,'rep'=2] {'shard'}, dimensions={0} | all-to-all | bytes 16384 | tf_op jit(solution)/shard_map/all_to_all | solution.py:495
  34.0 0.9 %shard_map.90 = (f32[4,32]{1,0:T(4,128)}, f32[4,32]{1,0:T(4,128)}) custom-call(s32[8,128]{1,0:T(8,128)S(1)} %get-tuple-element.12.plan, f32[16,1,128]{2,1,0:T(1,128)S(1)} %all_to_all.5.scores), custom_call_target="tpu_custom_call" | custom-call | tf_op jit(solution)/shard_map/pallas_call | solution.py:454
  (6 shorter events, 0.1 us)
Async XLA Ops:
  1.7 8.0 %collective-permute-start = (bf16[144,128]{1,0:T(8,128)(2,1)S(1)}, bf16[144,128]{1,0:T(8,128)(2,1)S(1)}, u32[]{:S(2)}, u32[]{:S(2)}) collective-permute-start(bf16[144,128]{1,0:T(8,128)(2,1)S(1)} %get-tuple-element.14), channel_id=1, source_target_pairs={{0,24},{2,26},{4,28},{6,30},{8,16},{10,18},{12,20},{14,22},{16,8},... | collective-permute-start | bytes 110600 | tf_op jit(solution)/shard_map/ppermute | solution.py:459
  6.8 4.9 %collective-permute-start.1 = (bf16[144,128]{1,0:T(8,128)(2,1)S(1)}, bf16[144,128]{1,0:T(8,128)(2,1)S(1)}, u32[]{:S(2)}, u32[]{:S(2)}) collective-permute-start(bf16[144,128]{1,0:T(8,128)(2,1)S(1)} %get-tuple-element.14), channel_id=1, source_target_pairs={{0,16},{2,18},{4,20},{6,22},{8,24},{10,26},{12,28},{14,30},{16,0},... | collective-permute-start | bytes 110600 | tf_op jit(solution)/shard_map/ppermute | solution.py:459
  6.8 4.9 %collective-permute-start.2 = (bf16[144,128]{1,0:T(8,128)(2,1)S(1)}, bf16[144,128]{1,0:T(8,128)(2,1)S(1)}, u32[]{:S(2)}, u32[]{:S(2)}) collective-permute-start(bf16[144,128]{1,0:T(8,128)(2,1)S(1)} %get-tuple-element.14), channel_id=1, source_target_pairs={{0,8},{2,10},{4,12},{6,14},{8,0},{10,2},{12,4},{14,6},{16,24},{18,... | collective-permute-start | bytes 110600 | tf_op jit(solution)/shard_map/ppermute | solution.py:459
  11.7 7.4 %collective-permute-start.3 = (bf16[528,128]{1,0:T(8,128)(2,1)S(1)}, bf16[528,128]{1,0:T(8,128)(2,1)S(1)}, u32[]{:S(2)}, u32[]{:S(2)}) collective-permute-start(bf16[528,128]{1,0:T(8,128)(2,1)S(1)} %constant_dynamic-update-slice_fusion), channel_id=1, source_target_pairs={{0,6},{2,4},{4,2},{6,0},{8,14},{10,12},{12,10},{14,8},{16,22},{18,... | collective-permute-start | bytes 405512 | tf_op jit(solution)/shard_map/ppermute | solution.py:459
  14.2 5.7 %collective-permute-start.4 = (bf16[528,128]{1,0:T(8,128)(2,1)S(1)}, bf16[528,128]{1,0:T(8,128)(2,1)S(1)}, u32[]{:S(2)}, u32[]{:S(2)}) collective-permute-start(bf16[528,128]{1,0:T(8,128)(2,1)S(1)} %constant_dynamic-update-slice_fusion), channel_id=1, source_target_pairs={{0,4},{2,6},{4,0},{6,2},{8,12},{10,14},{12,8},{14,10},{16,20},{18,... | collective-permute-start | bytes 405512 | tf_op jit(solution)/shard_map/ppermute | solution.py:459
  14.7 5.2 %collective-permute-start.5 = (bf16[528,128]{1,0:T(8,128)(2,1)S(1)}, bf16[528,128]{1,0:T(8,128)(2,1)S(1)}, u32[]{:S(2)}, u32[]{:S(2)}) collective-permute-start(bf16[528,128]{1,0:T(8,128)(2,1)S(1)} %constant_dynamic-update-slice_fusion), channel_id=1, source_target_pairs={{0,2},{2,0},{4,6},{6,4},{8,10},{10,8},{12,14},{14,12},{16,18},{18,... | collective-permute-start | bytes 405512 | tf_op jit(solution)/shard_map/ppermute | solution.py:459

commit v9 on v8

--- a/solution.py
+++ b/solution.py
@@ -8,6 +8,7 @@
 from jax.sharding import PartitionSpec as P
 
 GROUP = 256
+DEAD = 1 << 16
 STEP = 4
 META = 16
 LANES = 128
@@ -26,7 +27,7 @@
     return copies
 
 
-def prepare(copies, lengths_row, codes, centroids, hot, high, table):
+def prepare(copies, lengths_row, codes, centroids, weights, hot, high, table, levels):
     passages, slots = codes.shape
     count, width = centroids.shape
     copies[0].wait()
@@ -35,7 +36,7 @@
     live = lax.broadcasted_iota(jnp.int32, columns.shape, 0) < lengths_row[...]
     columns = jnp.where(live, columns, columns[0:1, :])
     low = columns % GROUP
-    top = columns // GROUP
+    top = jnp.where(live, columns // GROUP, columns // GROUP + DEAD)
     lane = lax.broadcasted_iota(jnp.int32, (slots, GROUP), 1)
     for p in range(passages):
         at = slice(p * slots, (p + 1) * slots)
@@ -46,12 +47,14 @@
         table[:, g * width : (g + 1) * width] = centroids[g * GROUP : (g + 1) * GROUP, :]
     for copy in copies[3:]:
         copy.wait()
-
-
-def build_rows(first, residuals, hot, high, table, rows, lengths, weights):
+    for k in range(weights.shape[0]):
+        levels[k : k + 1, :] = jnp.full((1, width), weights[k])
+
+
+def build_rows(first, residuals, hot, high, table, levels, rows):
     _, slots, width = residuals.shape
     groups = table.shape[1] // width
-    token = lax.broadcasted_iota(jnp.int32, (slots, width), 0)
+    level = [jnp.broadcast_to(levels[k : k + 1, :], (slots, width)) for k in range(4)]
     spread = jnp.dot(
         hot[first * slots : (first + STEP) * slots, :],
         table[...],
@@ -69,10 +72,10 @@
             bit *= 2
         cent = choice[0]
         code = residuals[p]
-        code = jnp.where(token < lengths[p], code, code[0:1, :])
+        code = jnp.where(group < DEAD, code, code[0:1, :])
         odd = (code & 1) == 1
-        low = jnp.where(odd, weights[1], weights[0])
-        top = jnp.where(odd, weights[3], weights[2])
+        low = jnp.where(odd, level[1], level[0])
+        top = jnp.where(odd, level[3], level[2])
         values = cent + jnp.where(code >= 2, top, low)
         norm = lax.rsqrt(jnp.sum(values * values, axis=-1, keepdims=True) + 1e-06)
         rows[p, :slots, :] = (values * norm).astype(jnp.bfloat16)
@@ -86,15 +89,15 @@
 
 
 def fetch_kernel(ways, *refs):
-    sources = refs[:6]
-    residuals, hot, high, table = refs[6:10]
-    lengths_row, codes, centroids, lengths, weights, sems = refs[10:]
+    sources = refs[:5]
+    residuals, hot, high, table, levels = refs[5:10]
+    lengths_row, codes, centroids, weights, sems = refs[10:]
 
     @pl.when(jnp.logical_not(fetches_late(ways)))
     def _():
-        targets = (lengths_row, codes, centroids, lengths, weights, residuals)
+        targets = (lengths_row, codes, centroids, weights, residuals)
         copies = start_copies(sources, targets, sems)
-        prepare(copies, lengths_row, codes, centroids, hot, high, table)
+        prepare(copies, lengths_row, codes, centroids, weights, hot, high, table, levels)
 
 
 def index_scratch(lengths, bucket_weights, codes, centroids, count):
@@ -102,7 +105,6 @@
         pltpu.VMEM((1, lengths.shape[0]), lengths.dtype),
         pltpu.VMEM(codes.shape, codes.dtype),
         pltpu.VMEM(centroids.shape, centroids.dtype),
-        pltpu.SMEM(lengths.shape, lengths.dtype),
         pltpu.SMEM(bucket_weights.shape, bucket_weights.dtype),
         pltpu.SemaphoreType.DMA((count,)),
     ]
@@ -115,6 +117,7 @@
         pltpu.VMEM((tokens, GROUP), jnp.bfloat16),
         pltpu.VMEM((tokens, width), jnp.int32),
         pltpu.VMEM((GROUP, centroids.size // GROUP), jnp.bfloat16),
+        pltpu.VMEM((8, width), jnp.float32),
     ]
 
 
@@ -122,12 +125,12 @@
     passages = codes.shape[0]
     width = centroids.shape[1]
     operands = (
-        lengths.reshape(1, passages), codes, centroids, lengths, bucket_weights, residual_codes
+        lengths.reshape(1, passages), codes, centroids, bucket_weights, residual_codes
     )
     return pl.pallas_call(
         functools.partial(fetch_kernel, ways),
         in_specs=[pl.BlockSpec(memory_space=pltpu.HBM)] * len(operands),
-        out_specs=[pl.BlockSpec(memory_space=pltpu.VMEM)] * 4,
+        out_specs=[pl.BlockSpec(memory_space=pltpu.VMEM)] * 5,
         out_shape=index_arrays(codes, centroids, width),
         scratch_shapes=index_scratch(lengths, bucket_weights, codes, centroids, len(operands)),
         compiler_params=pltpu.CompilerParams(vmem_limit_bytes=32 * 2**20),
@@ -138,36 +141,33 @@
 
 
 def decompress_kernel(ways, *refs):
-    sources = refs[:6]
-    early = refs[6:10]
+    sources = refs[:5]
+    early = refs[5:10]
     rows = refs[10]
-    lengths_row, codes, centroids, lengths, weights, sems = refs[11:17]
-    own = refs[17:]
+    lengths_row, codes, centroids, weights, sems = refs[11:16]
+    own = refs[16:]
     passages = codes.shape[0]
     late = fetches_late(ways)
 
     @pl.when(jnp.logical_not(late))
     def _():
-        copies = start_copies(sources[3:5], (lengths, weights), sems)
-        for copy in copies:
-            copy.wait()
         for first in range(0, passages, STEP):
-            build_rows(first, *early, rows, lengths, weights)
+            build_rows(first, *early, rows)
 
     @pl.when(late)
     def _():
-        targets = (lengths_row, codes, centroids, lengths, weights, own[0])
+        targets = (lengths_row, codes, centroids, weights, own[0])
         copies = start_copies(sources, targets, sems)
-        prepare(copies, lengths_row, codes, centroids, *own[1:])
+        prepare(copies, lengths_row, codes, centroids, weights, *own[1:])
         for first in range(0, passages, STEP):
-            build_rows(first, *own, rows, lengths, weights)
+            build_rows(first, *own, rows)
 
 
 def decompress(lengths, bucket_weights, codes, residual_codes, centroids, ways, early):
     passages, slots = codes.shape
     width = centroids.shape[1]
     operands = (
-        lengths.reshape(1, passages), codes, centroids, lengths, bucket_weights, residual_codes
+        lengths.reshape(1, passages), codes, centroids, bucket_weights, residual_codes
     )
     return pl.pallas_call(
         functools.partial(decompress_kernel, ways),

time: 35.2 us -> 35.5 us (level)
  waiting for transfers between devices: 3.1 us -> 3.86 us
  Pallas kernels: 10.5 us -> 9.76 us
    ppermute x6, waiting for transfers between devices: 3.1 us -> 3.86 us  [exchange(): lax.ppermute(block, 'shard', [(i, i ^ step) for i in range(shards)])]
    pallas_call x1, Pallas kernels: 3.46 us -> 2.71 us  [decompress(): pl.pallas_call(functools.partial(decompress_kernel, ways), in_specs=[pl.B...]
  transfers between devices with their start and end apart: 6 -> 6, of which waited for: 3 -> 3; matrix products, arithmetic and copies ran while one was open for 0% -> 0% of each run, Pallas kernels for 16% -> 14%
where the time goes in v9:
time: 35.5 us; the launch traced here: 35 us
  blocking collectives  11.2 us (32%)
  Pallas kernels  9.76 us (27%)
  starting transfers between devices  9.31 us (26%)
  waiting for transfers between devices  3.86 us (11%)
  between operations  0.69 us (2%)
    all_to_all x1, blocking collectives, per_device(): lax.all_to_all(scores, 'shard', split_axis=0, concat_axis=0, tiled=True)  11.2 us
    ppermute x6, starting transfers between devices, exchange(): lax.ppermute(block, 'shard', [(i, i ^ step) for i in range(shards)])  9.31 us
    ppermute x6, waiting for transfers between devices, exchange(): lax.ppermute(block, 'shard', [(i, i ^ step) for i in range(shards)])  3.86 us
    pallas_call x1, Pallas kernels, score(): pl.pallas_call(functools.partial(score_kernel, query_tokens, cap, ways, o...  2.87 us
    pallas_call x1, Pallas kernels, decompress(): pl.pallas_call(functools.partial(decompress_kernel, ways), in_specs=[pl.B...  2.71 us
    pallas_call x1, Pallas kernels, fetch(): pl.pallas_call(functools.partial(fetch_kernel, ways), in_specs=[pl.BlockS...  2.25 us
    pallas_call x1, Pallas kernels, make_plan(): pl.pallas_call(functools.partial(plan_kernel, shards, cap, passages, ways...  1.04 us
    pallas_call x1, Pallas kernels, pick(): return pl.pallas_call(pick_kernel, out_shape=(result, result))(*operands)  0.9 us
  transfers between devices with their start and end apart: 6, of which 3 were waited for; matrix products, arithmetic and copies ran while one was open for 0% of the time, Pallas kernels for 14%

profile of v9, /device:TPU:0, one launch (start us, length us, event | category | flops | bytes accessed | tf_op | source)
XLA Modules:
  0.0 35.0 jit_solution(12663462600088686306)
XLA Ops:
  0.6 1.0 %shard_map.86 = (bf16[144,128]{1,0:T(8,128)(2,1)S(1)}, s32[8,128]{1,0:T(8,128)S(1)}) custom-call(bf16[128,128]{1,0:T(8,128)(2,1)} %bitcast.5, s32[4,32]{1,0:T(4,128)} %candidates_hbm.1), custom_call_target="tpu_custom_call" | custom-call | tf_op jit(solution)/shard_map/pallas_call | solution.py:232
  1.7 5.1 %collective-permute-start = (bf16[144,128]{1,0:T(8,128)(2,1)S(1)}, bf16[144,128]{1,0:T(8,128)(2,1)S(1)}, u32[]{:S(2)}, u32[]{:S(2)}) collective-permute-start(bf16[144,128]{1,0:T(8,128)(2,1)S(1)} %get-tuple-element.15), channel_id=1, source_target_pairs={{0,24},{2,26},{4,28},{6,30},{8,16},{10,18},{12,20},{14,22},{16,8},... | collective-permute-start | bytes 110600 | tf_op jit(solution)/shard_map/ppermute | solution.py:459
  6.8 0.0 collective-permute-start.1
  6.8 0.6 %collective-permute-start.2 = (bf16[144,128]{1,0:T(8,128)(2,1)S(1)}, bf16[144,128]{1,0:T(8,128)(2,1)S(1)}, u32[]{:S(2)}, u32[]{:S(2)}) collective-permute-start(bf16[144,128]{1,0:T(8,128)(2,1)S(1)} %get-tuple-element.15), channel_id=1, source_target_pairs={{0,8},{2,10},{4,12},{6,14},{8,0},{10,2},{12,4},{14,6},{16,24},{18,... | collective-permute-start | bytes 110600 | tf_op jit(solution)/shard_map/ppermute | solution.py:459
  7.4 2.2 %shard_map.87 = (s32[32,128,128]{2,1,0:T(8,128)S(1)}, bf16[4096,256]{1,0:T(8,128)(2,1)S(1)}, s32[4096,128]{1,0:T(8,128)S(1)}, bf16[256,1024]{1,0:T(8,128)(2,1)S(1)}, f32[8,128]{1,0:T(8,128)S(1)}) custom-call(s32[1,32]{1,0:T(1,128)} %bitcast.6, s32[32,128]{1,0:T(8,128)} %refs_1_.1, bf16[2048,128]{1,0:T(8,128)(2,1)} %refs_2_.3, f32[4]{0:T(128)} %refs_3_.3, ...), custom_call_target="tpu_custom_call" | custom-call | bytes 4194304 | tf_op jit(solution)/shard_map/pallas_call | solution.py:130
  9.7 0.0 collective-permute-done
  9.7 1.9 %collective-permute-done.1 = bf16[144,128]{1,0:T(8,128)(2,1)S(1)} collective-permute-done((bf16[144,128]{1,0:T(8,128)(2,1)S(1)}, bf16[144,128]{1,0:T(8,128)(2,1)S(1)}, u32[]{:S(2)}, u32[]{:S(2)}) %collective-permute-start.1) | collective-permute-done | bytes 36896 | tf_op jit(solution)/shard_map/ppermute | solution.py:459
  11.7 0.0 collective-permute-done.2
  11.7 2.5 %collective-permute-start.3 = (bf16[528,128]{1,0:T(8,128)(2,1)S(1)}, bf16[528,128]{1,0:T(8,128)(2,1)S(1)}, u32[]{:S(2)}, u32[]{:S(2)}) collective-permute-start(bf16[528,128]{1,0:T(8,128)(2,1)S(1)} %constant_dynamic-update-slice_fusion), channel_id=1, source_target_pairs={{0,6},{2,4},{4,2},{6,0},{8,14},{10,12},{12,10},{14,8},{16,22},{18,... | collective-permute-start | bytes 405512 | tf_op jit(solution)/shard_map/ppermute | solution.py:459
  14.2 0.5 %collective-permute-start.4 = (bf16[528,128]{1,0:T(8,128)(2,1)S(1)}, bf16[528,128]{1,0:T(8,128)(2,1)S(1)}, u32[]{:S(2)}, u32[]{:S(2)}) collective-permute-start(bf16[528,128]{1,0:T(8,128)(2,1)S(1)} %constant_dynamic-update-slice_fusion), channel_id=1, source_target_pairs={{0,4},{2,6},{4,0},{6,2},{8,12},{10,14},{12,8},{14,10},{16,20},{18,... | collective-permute-start | bytes 405512 | tf_op jit(solution)/shard_map/ppermute | solution.py:459
  14.7 0.5 %collective-permute-start.5 = (bf16[528,128]{1,0:T(8,128)(2,1)S(1)}, bf16[528,128]{1,0:T(8,128)(2,1)S(1)}, u32[]{:S(2)}, u32[]{:S(2)}) collective-permute-start(bf16[528,128]{1,0:T(8,128)(2,1)S(1)} %constant_dynamic-update-slice_fusion), channel_id=1, source_target_pairs={{0,2},{2,0},{4,6},{6,4},{8,10},{10,8},{12,14},{14,12},{16,18},{18,... | collective-permute-start | bytes 405512 | tf_op jit(solution)/shard_map/ppermute | solution.py:459
  15.2 2.7 %shard_map.88.rows = bf16[32,256,128]{2,1,0:T(8,128)(2,1)S(1)} custom-call(s32[1,32]{1,0:T(1,128)} %bitcast.7, s32[32,128]{1,0:T(8,128)} %refs_1_.1, bf16[2048,128]{1,0:T(8,128)(2,1)} %refs_2_.3, f32[4]{0:T(128)} %refs_3_.3, s32[32,128,128]{2,1,0:T(8,128)} %refs_4_.3, s32[32,128,128]{2,1,0:T(8,128)S(1)} %get-tuple-element.19.refs_5_, ...), custom_call_target="tpu_custom_call" | custom-call | flops 2147483648 | bytes 2097152 | tf_op jit(solution)/shard_map/pallas_call | solution.py:172
  18.0 1.1 %collective-permute-done.3 = bf16[528,128]{1,0:T(8,128)(2,1)S(1)} collective-permute-done((bf16[528,128]{1,0:T(8,128)(2,1)S(1)}, bf16[528,128]{1,0:T(8,128)(2,1)S(1)}, u32[]{:S(2)}, u32[]{:S(2)}) %collective-permute-start.3) | collective-permute-done | bytes 135200 | tf_op jit(solution)/shard_map/ppermute | solution.py:459
  19.1 0.8 %collective-permute-done.4 = bf16[528,128]{1,0:T(8,128)(2,1)S(1)} collective-permute-done((bf16[528,128]{1,0:T(8,128)(2,1)S(1)}, bf16[528,128]{1,0:T(8,128)(2,1)S(1)}, u32[]{:S(2)}, u32[]{:S(2)}) %collective-permute-start.4) | collective-permute-done | bytes 135200 | tf_op jit(solution)/shard_map/ppermute | solution.py:459
  19.9 0.0 collective-permute-done.5
  19.9 2.9 %shard_map.89 = f32[16,1,128]{2,1,0:T(1,128)S(1)} custom-call(bf16[4,528,128]{2,1,0:T(8,128)(2,1)S(1)} %bitcast.4, bf16[32,256,128]{2,1,0:T(8,128)(2,1)S(1)} %shard_map.88.rows), custom_call_target="tpu_custom_call" | custom-call | flops 805306368 | bytes 2637824 | tf_op jit(solution)/shard_map/pallas_call | solution.py:410
  22.8 11.2 %all_to_all.5.scores = f32[16,1,128]{2,1,0:T(1,128)S(1)} all-to-all(f32[16,1,128]{2,1,0:T(1,128)S(1)} %shard_map.89), channel_id=1, replica_groups=mesh['shard'=16,'rep'=2] {'shard'}, dimensions={0} | all-to-all | bytes 16384 | tf_op jit(solution)/shard_map/all_to_all | solution.py:495
  34.1 0.9 %shard_map.90 = (f32[4,32]{1,0:T(4,128)}, f32[4,32]{1,0:T(4,128)}) custom-call(s32[8,128]{1,0:T(8,128)S(1)} %get-tuple-element.13.plan, f32[16,1,128]{2,1,0:T(1,128)S(1)} %all_to_all.5.scores), custom_call_target="tpu_custom_call" | custom-call | tf_op jit(solution)/shard_map/pallas_call | solution.py:454
  (6 shorter events, 0.1 us)
Async XLA Ops:
  1.7 8.0 %collective-permute-start = (bf16[144,128]{1,0:T(8,128)(2,1)S(1)}, bf16[144,128]{1,0:T(8,128)(2,1)S(1)}, u32[]{:S(2)}, u32[]{:S(2)}) collective-permute-start(bf16[144,128]{1,0:T(8,128)(2,1)S(1)} %get-tuple-element.15), channel_id=1, source_target_pairs={{0,24},{2,26},{4,28},{6,30},{8,16},{10,18},{12,20},{14,22},{16,8},... | collective-permute-start | bytes 110600 | tf_op jit(solution)/shard_map/ppermute | solution.py:459
  6.8 4.9 %collective-permute-start.1 = (bf16[144,128]{1,0:T(8,128)(2,1)S(1)}, bf16[144,128]{1,0:T(8,128)(2,1)S(1)}, u32[]{:S(2)}, u32[]{:S(2)}) collective-permute-start(bf16[144,128]{1,0:T(8,128)(2,1)S(1)} %get-tuple-element.15), channel_id=1, source_target_pairs={{0,16},{2,18},{4,20},{6,22},{8,24},{10,26},{12,28},{14,30},{16,0},... | collective-permute-start | bytes 110600 | tf_op jit(solution)/shard_map/ppermute | solution.py:459
  6.8 4.9 %collective-permute-start.2 = (bf16[144,128]{1,0:T(8,128)(2,1)S(1)}, bf16[144,128]{1,0:T(8,128)(2,1)S(1)}, u32[]{:S(2)}, u32[]{:S(2)}) collective-permute-start(bf16[144,128]{1,0:T(8,128)(2,1)S(1)} %get-tuple-element.15), channel_id=1, source_target_pairs={{0,8},{2,10},{4,12},{6,14},{8,0},{10,2},{12,4},{14,6},{16,24},{18,... | collective-permute-start | bytes 110600 | tf_op jit(solution)/shard_map/ppermute | solution.py:459
  11.7 7.4 %collective-permute-start.3 = (bf16[528,128]{1,0:T(8,128)(2,1)S(1)}, bf16[528,128]{1,0:T(8,128)(2,1)S(1)}, u32[]{:S(2)}, u32[]{:S(2)}) collective-permute-start(bf16[528,128]{1,0:T(8,128)(2,1)S(1)} %constant_dynamic-update-slice_fusion), channel_id=1, source_target_pairs={{0,6},{2,4},{4,2},{6,0},{8,14},{10,12},{12,10},{14,8},{16,22},{18,... | collective-permute-start | bytes 405512 | tf_op jit(solution)/shard_map/ppermute | solution.py:459
  14.2 5.7 %collective-permute-start.4 = (bf16[528,128]{1,0:T(8,128)(2,1)S(1)}, bf16[528,128]{1,0:T(8,128)(2,1)S(1)}, u32[]{:S(2)}, u32[]{:S(2)}) collective-permute-start(bf16[528,128]{1,0:T(8,128)(2,1)S(1)} %constant_dynamic-update-slice_fusion), channel_id=1, source_target_pairs={{0,4},{2,6},{4,0},{6,2},{8,12},{10,14},{12,8},{14,10},{16,20},{18,... | collective-permute-start | bytes 405512 | tf_op jit(solution)/shard_map/ppermute | solution.py:459
  14.7 5.2 %collective-permute-start.5 = (bf16[528,128]{1,0:T(8,128)(2,1)S(1)}, bf16[528,128]{1,0:T(8,128)(2,1)S(1)}, u32[]{:S(2)}, u32[]{:S(2)}) collective-permute-start(bf16[528,128]{1,0:T(8,128)(2,1)S(1)} %constant_dynamic-update-slice_fusion), channel_id=1, source_target_pairs={{0,2},{2,0},{4,6},{6,4},{8,10},{10,8},{12,14},{14,12},{16,18},{18,... | collective-permute-start | bytes 405512 | tf_op jit(solution)/shard_map/ppermute | solution.py:459

commit v10 on v9

--- a/solution.py
+++ b/solution.py
@@ -27,7 +27,7 @@
     return copies
 
 
-def prepare(copies, lengths_row, codes, centroids, weights, hot, high, table, levels):
+def prepare(copies, lengths_row, codes, centroids, weights, hot, high, table, levels, lows):
     passages, slots = codes.shape
     count, width = centroids.shape
     copies[0].wait()
@@ -37,10 +37,12 @@
     columns = jnp.where(live, columns, columns[0:1, :])
     low = columns % GROUP
     top = jnp.where(live, columns // GROUP, columns // GROUP + DEAD)
+    lows[...] = low
     lane = lax.broadcasted_iota(jnp.int32, (slots, GROUP), 1)
     for p in range(passages):
         at = slice(p * slots, (p + 1) * slots)
-        hot[at, :] = (lane == low[:, p : p + 1]).astype(jnp.bfloat16)
+        if p < passages // 2:
+            hot[at, :] = (lane == low[:, p : p + 1]).astype(jnp.bfloat16)
         high[at, :] = jnp.broadcast_to(top[:, p : p + 1], (slots, width))
     copies[2].wait()
     for g in range(count // GROUP):
@@ -51,12 +53,19 @@
         levels[k : k + 1, :] = jnp.full((1, width), weights[k])
 
 
-def build_rows(first, residuals, hot, high, table, levels, rows):
+def build_rows(first, residuals, hot, high, table, levels, lows, rows):
     _, slots, width = residuals.shape
     groups = table.shape[1] // width
     level = [jnp.broadcast_to(levels[k : k + 1, :], (slots, width)) for k in range(4)]
+    if first < residuals.shape[0] // 2:
+        chosen = hot[first * slots : (first + STEP) * slots, :]
+    else:
+        lane = lax.broadcasted_iota(jnp.int32, (slots, GROUP), 1)
+        chosen = jnp.concatenate(
+            [(lane == lows[:, p : p + 1]).astype(jnp.bfloat16) for p in range(first, first + STEP)]
+        )
     spread = jnp.dot(
-        hot[first * slots : (first + STEP) * slots, :],
+        chosen,
         table[...],
         preferred_element_type=jnp.float32,
     )
@@ -90,14 +99,14 @@
 
 def fetch_kernel(ways, *refs):
     sources = refs[:5]
-    residuals, hot, high, table, levels = refs[5:10]
-    lengths_row, codes, centroids, weights, sems = refs[10:]
+    residuals, hot, high, table, levels, lows = refs[5:11]
+    lengths_row, codes, centroids, weights, sems = refs[11:]
 
     @pl.when(jnp.logical_not(fetches_late(ways)))
     def _():
         targets = (lengths_row, codes, centroids, weights, residuals)
         copies = start_copies(sources, targets, sems)
-        prepare(copies, lengths_row, codes, centroids, weights, hot, high, table, levels)
+        prepare(copies, lengths_row, codes, centroids, weights, hot, high, table, levels, lows)
 
 
 def index_scratch(lengths, bucket_weights, codes, centroids, count):
@@ -118,6 +127,7 @@
         pltpu.VMEM((tokens, width), jnp.int32),
         pltpu.VMEM((GROUP, centroids.size // GROUP), jnp.bfloat16),
         pltpu.VMEM((8, width), jnp.float32),
+        pltpu.VMEM(codes.shape[::-1], jnp.int32),
     ]
 
 
@@ -130,7 +140,7 @@
     return pl.pallas_call(
         functools.partial(fetch_kernel, ways),
         in_specs=[pl.BlockSpec(memory_space=pltpu.HBM)] * len(operands),
-        out_specs=[pl.BlockSpec(memory_space=pltpu.VMEM)] * 5,
+        out_specs=[pl.BlockSpec(memory_space=pltpu.VMEM)] * 6,
         out_shape=index_arrays(codes, centroids, width),
         scratch_shapes=index_scratch(lengths, bucket_weights, codes, centroids, len(operands)),
         compiler_params=pltpu.CompilerParams(vmem_limit_bytes=32 * 2**20),
@@ -142,10 +152,10 @@
 
 def decompress_kernel(ways, *refs):
     sources = refs[:5]
-    early = refs[5:10]
-    rows = refs[10]
-    lengths_row, codes, centroids, weights, sems = refs[11:16]
-    own = refs[16:]
+    early = refs[5:11]
+    rows = refs[11]
+    lengths_row, codes, centroids, weights, sems = refs[12:17]
+    own = refs[17:]
     passages = codes.shape[0]
     late = fetches_late(ways)
 

time: 35.5 us -> 35.2 us (level)
  no operation moved by 1% of the time
where the time goes in v10:
time: 35.2 us; the launch traced here: 34.9 us
  blocking collectives  11.2 us (32%)
  Pallas kernels  9.76 us (28%)
  starting transfers between devices  9.31 us (26%)
  waiting for transfers between devices  3.86 us (11%)
  between operations  0.69 us (2%)
    all_to_all x1, blocking collectives, per_device(): lax.all_to_all(scores, 'shard', split_axis=0, concat_axis=0, tiled=True)  11.2 us
    ppermute x6, starting transfers between devices, exchange(): lax.ppermute(block, 'shard', [(i, i ^ step) for i in range(shards)])  9.31 us
    ppermute x6, waiting for transfers between devices, exchange(): lax.ppermute(block, 'shard', [(i, i ^ step) for i in range(shards)])  3.86 us
    pallas_call x1, Pallas kernels, decompress(): pl.pallas_call(functools.partial(decompress_kernel, ways), in_specs=[pl.B...  2.98 us
    pallas_call x1, Pallas kernels, score(): pl.pallas_call(functools.partial(score_kernel, query_tokens, cap, ways, o...  2.87 us
    pallas_call x1, Pallas kernels, fetch(): pl.pallas_call(functools.partial(fetch_kernel, ways), in_specs=[pl.BlockS...  1.98 us
    pallas_call x1, Pallas kernels, make_plan(): pl.pallas_call(functools.partial(plan_kernel, shards, cap, passages, ways...  1.04 us
    pallas_call x1, Pallas kernels, pick(): return pl.pallas_call(pick_kernel, out_shape=(result, result))(*operands)  0.9 us
  transfers between devices with their start and end apart: 6, of which 3 were waited for; matrix products, arithmetic and copies ran while one was open for 0% of the time, Pallas kernels for 14%

profile of v10, /device:TPU:0, one launch (start us, length us, event | category | flops | bytes accessed | tf_op | source)
XLA Modules:
  0.0 34.9 jit_solution(14639840954824076524)
XLA Ops:
  0.6 1.0 %shard_map.86 = (bf16[144,128]{1,0:T(8,128)(2,1)S(1)}, s32[8,128]{1,0:T(8,128)S(1)}) custom-call(bf16[128,128]{1,0:T(8,128)(2,1)} %bitcast.5, s32[4,32]{1,0:T(4,128)} %candidates_hbm.1), custom_call_target="tpu_custom_call" | custom-call | tf_op jit(solution)/shard_map/pallas_call | solution.py:242
  1.7 5.1 %collective-permute-start = (bf16[144,128]{1,0:T(8,128)(2,1)S(1)}, bf16[144,128]{1,0:T(8,128)(2,1)S(1)}, u32[]{:S(2)}, u32[]{:S(2)}) collective-permute-start(bf16[144,128]{1,0:T(8,128)(2,1)S(1)} %get-tuple-element.16), channel_id=1, source_target_pairs={{0,24},{2,26},{4,28},{6,30},{8,16},{10,18},{12,20},{14,22},{16,8},... | collective-permute-start | bytes 110600 | tf_op jit(solution)/shard_map/ppermute | solution.py:469
  6.8 0.0 collective-permute-start.1
  6.8 0.6 %collective-permute-start.2 = (bf16[144,128]{1,0:T(8,128)(2,1)S(1)}, bf16[144,128]{1,0:T(8,128)(2,1)S(1)}, u32[]{:S(2)}, u32[]{:S(2)}) collective-permute-start(bf16[144,128]{1,0:T(8,128)(2,1)S(1)} %get-tuple-element.16), channel_id=1, source_target_pairs={{0,8},{2,10},{4,12},{6,14},{8,0},{10,2},{12,4},{14,6},{16,24},{18,... | collective-permute-start | bytes 110600 | tf_op jit(solution)/shard_map/ppermute | solution.py:469
  7.4 2.0 %shard_map.87 = (s32[32,128,128]{2,1,0:T(8,128)S(1)}, bf16[4096,256]{1,0:T(8,128)(2,1)S(1)}, s32[4096,128]{1,0:T(8,128)S(1)}, bf16[256,1024]{1,0:T(8,128)(2,1)S(...) custom-call(s32[1,32]{1,0:T(1,128)} %bitcast.6, s32[32,128]{1,0:T(8,128)} %refs_1_.1, bf16[2048,128]{1,0:T(8,128)(2,1)} %refs_2_.3, ...), custom_call_target="tpu_custom_call" | custom-call | bytes 4194304 | tf_op jit(solution)/shard_map/pallas_call | solution.py:140
  9.4 0.0 collective-permute-done
  9.4 2.2 %collective-permute-done.1 = bf16[144,128]{1,0:T(8,128)(2,1)S(1)} collective-permute-done((bf16[144,128]{1,0:T(8,128)(2,1)S(1)}, bf16[144,128]{1,0:T(8,128)(2,1)S(1)}, u32[]{:S(2)}, u32[]{:S(2)}) %collective-permute-start.1) | collective-permute-done | bytes 36896 | tf_op jit(solution)/shard_map/ppermute | solution.py:469
  11.7 0.0 collective-permute-done.2
  11.7 2.5 %collective-permute-start.3 = (bf16[528,128]{1,0:T(8,128)(2,1)S(1)}, bf16[528,128]{1,0:T(8,128)(2,1)S(1)}, u32[]{:S(2)}, u32[]{:S(2)}) collective-permute-start(bf16[528,128]{1,0:T(8,128)(2,1)S(1)} %constant_dynamic-update-slice_fusion), channel_id=1, source_target_pairs={{0,6},{2,4},{4,2},{6,0},{8,14},{10,12},{12,10},{14,8},{16,22},{18,... | collective-permute-start | bytes 405512 | tf_op jit(solution)/shard_map/ppermute | solution.py:469
  14.2 0.5 %collective-permute-start.4 = (bf16[528,128]{1,0:T(8,128)(2,1)S(1)}, bf16[528,128]{1,0:T(8,128)(2,1)S(1)}, u32[]{:S(2)}, u32[]{:S(2)}) collective-permute-start(bf16[528,128]{1,0:T(8,128)(2,1)S(1)} %constant_dynamic-update-slice_fusion), channel_id=1, source_target_pairs={{0,4},{2,6},{4,0},{6,2},{8,12},{10,14},{12,8},{14,10},{16,20},{18,... | collective-permute-start | bytes 405512 | tf_op jit(solution)/shard_map/ppermute | solution.py:469
  14.7 0.5 %collective-permute-start.5 = (bf16[528,128]{1,0:T(8,128)(2,1)S(1)}, bf16[528,128]{1,0:T(8,128)(2,1)S(1)}, u32[]{:S(2)}, u32[]{:S(2)}) collective-permute-start(bf16[528,128]{1,0:T(8,128)(2,1)S(1)} %constant_dynamic-update-slice_fusion), channel_id=1, source_target_pairs={{0,2},{2,0},{4,6},{6,4},{8,10},{10,8},{12,14},{14,12},{16,18},{18,... | collective-permute-start | bytes 405512 | tf_op jit(solution)/shard_map/ppermute | solution.py:469
  15.2 3.0 %shard_map.88.rows = bf16[32,256,128]{2,1,0:T(8,128)(2,1)S(1)} custom-call(s32[1,32]{1,0:T(1,128)} %bitcast.7, s32[32,128]{1,0:T(8,128)} %refs_1_.1, bf16[2048,128]{1,0:T(8,128)(2,1)} %refs_2_.3, f32[4]{0:T(128)} %refs_3_.3, s32[32,128,128]{2,1,0:T(8,128)} %refs_4_.3, s32[32,128,128]{2,1,0:T(8,128)S(1)} %get-tuple-element.20.refs_5_, ...), custom_call_target="tpu_custom_call" | custom-call | flops 2147483648 | bytes 2097152 | tf_op jit(solution)/shard_map/pallas_call | solution.py:182
  18.2 0.9 %collective-permute-done.3 = bf16[528,128]{1,0:T(8,128)(2,1)S(1)} collective-permute-done((bf16[528,128]{1,0:T(8,128)(2,1)S(1)}, bf16[528,128]{1,0:T(8,128)(2,1)S(1)}, u32[]{:S(2)}, u32[]{:S(2)}) %collective-permute-start.3) | collective-permute-done | bytes 135200 | tf_op jit(solution)/shard_map/ppermute | solution.py:469
  19.1 0.8 %collective-permute-done.4 = bf16[528,128]{1,0:T(8,128)(2,1)S(1)} collective-permute-done((bf16[528,128]{1,0:T(8,128)(2,1)S(1)}, bf16[528,128]{1,0:T(8,128)(2,1)S(1)}, u32[]{:S(2)}, u32[]{:S(2)}) %collective-permute-start.4) | collective-permute-done | bytes 135200 | tf_op jit(solution)/shard_map/ppermute | solution.py:469
  19.9 0.0 collective-permute-done.5
  19.9 2.9 %shard_map.89 = f32[16,1,128]{2,1,0:T(1,128)S(1)} custom-call(bf16[4,528,128]{2,1,0:T(8,128)(2,1)S(1)} %bitcast.4, bf16[32,256,128]{2,1,0:T(8,128)(2,1)S(1)} %shard_map.88.rows), custom_call_target="tpu_custom_call" | custom-call | flops 805306368 | bytes 2637824 | tf_op jit(solution)/shard_map/pallas_call | solution.py:420
  22.8 11.2 %all_to_all.5.scores = f32[16,1,128]{2,1,0:T(1,128)S(1)} all-to-all(f32[16,1,128]{2,1,0:T(1,128)S(1)} %shard_map.89), channel_id=1, replica_groups=mesh['shard'=16,'rep'=2] {'shard'}, dimensions={0} | all-to-all | bytes 16384 | tf_op jit(solution)/shard_map/all_to_all | solution.py:505
  34.0 0.9 %shard_map.90 = (f32[4,32]{1,0:T(4,128)}, f32[4,32]{1,0:T(4,128)}) custom-call(s32[8,128]{1,0:T(8,128)S(1)} %get-tuple-element.14.plan, f32[16,1,128]{2,1,0:T(1,128)S(1)} %all_to_all.5.scores), custom_call_target="tpu_custom_call" | custom-call | tf_op jit(solution)/shard_map/pallas_call | solution.py:464
  (6 shorter events, 0.1 us)
Async XLA Ops:
  1.7 7.7 %collective-permute-start = (bf16[144,128]{1,0:T(8,128)(2,1)S(1)}, bf16[144,128]{1,0:T(8,128)(2,1)S(1)}, u32[]{:S(2)}, u32[]{:S(2)}) collective-permute-start(bf16[144,128]{1,0:T(8,128)(2,1)S(1)} %get-tuple-element.16), channel_id=1, source_target_pairs={{0,24},{2,26},{4,28},{6,30},{8,16},{10,18},{12,20},{14,22},{16,8},... | collective-permute-start | bytes 110600 | tf_op jit(solution)/shard_map/ppermute | solution.py:469
  6.8 4.9 %collective-permute-start.1 = (bf16[144,128]{1,0:T(8,128)(2,1)S(1)}, bf16[144,128]{1,0:T(8,128)(2,1)S(1)}, u32[]{:S(2)}, u32[]{:S(2)}) collective-permute-start(bf16[144,128]{1,0:T(8,128)(2,1)S(1)} %get-tuple-element.16), channel_id=1, source_target_pairs={{0,16},{2,18},{4,20},{6,22},{8,24},{10,26},{12,28},{14,30},{16,0},... | collective-permute-start | bytes 110600 | tf_op jit(solution)/shard_map/ppermute | solution.py:469
  6.8 4.9 %collective-permute-start.2 = (bf16[144,128]{1,0:T(8,128)(2,1)S(1)}, bf16[144,128]{1,0:T(8,128)(2,1)S(1)}, u32[]{:S(2)}, u32[]{:S(2)}) collective-permute-start(bf16[144,128]{1,0:T(8,128)(2,1)S(1)} %get-tuple-element.16), channel_id=1, source_target_pairs={{0,8},{2,10},{4,12},{6,14},{8,0},{10,2},{12,4},{14,6},{16,24},{18,... | collective-permute-start | bytes 110600 | tf_op jit(solution)/shard_map/ppermute | solution.py:469
  11.7 7.4 %collective-permute-start.3 = (bf16[528,128]{1,0:T(8,128)(2,1)S(1)}, bf16[528,128]{1,0:T(8,128)(2,1)S(1)}, u32[]{:S(2)}, u32[]{:S(2)}) collective-permute-start(bf16[528,128]{1,0:T(8,128)(2,1)S(1)} %constant_dynamic-update-slice_fusion), channel_id=1, source_target_pairs={{0,6},{2,4},{4,2},{6,0},{8,14},{10,12},{12,10},{14,8},{16,22},{18,... | collective-permute-start | bytes 405512 | tf_op jit(solution)/shard_map/ppermute | solution.py:469
  14.2 5.7 %collective-permute-start.4 = (bf16[528,128]{1,0:T(8,128)(2,1)S(1)}, bf16[528,128]{1,0:T(8,128)(2,1)S(1)}, u32[]{:S(2)}, u32[]{:S(2)}) collective-permute-start(bf16[528,128]{1,0:T(8,128)(2,1)S(1)} %constant_dynamic-update-slice_fusion), channel_id=1, source_target_pairs={{0,4},{2,6},{4,0},{6,2},{8,12},{10,14},{12,8},{14,10},{16,20},{18,... | collective-permute-start | bytes 405512 | tf_op jit(solution)/shard_map/ppermute | solution.py:469
  14.7 5.2 %collective-permute-start.5 = (bf16[528,128]{1,0:T(8,128)(2,1)S(1)}, bf16[528,128]{1,0:T(8,128)(2,1)S(1)}, u32[]{:S(2)}, u32[]{:S(2)}) collective-permute-start(bf16[528,128]{1,0:T(8,128)(2,1)S(1)} %constant_dynamic-update-slice_fusion), channel_id=1, source_target_pairs={{0,2},{2,0},{4,6},{6,4},{8,10},{10,8},{12,14},{14,12},{16,18},{18,... | collective-permute-start | bytes 405512 | tf_op jit(solution)/shard_map/ppermute | solution.py:469
